TPU v7x, 256 devices: a whole 4x4x8 slice. The times are simulated.
256 devices in a mesh: sec: 4 (over y), ctx: 16 (over z, core), ch: 4 (over x).
Axes of the slice: x: 4, y: 4, z: 8, core: 2. Of those that a mesh axis runs over, the one named last changes fastest.
Arguments:
- inputs: bfloat16 [2048, 4096], P('ctx', ('ch', 'sec')), may hold values from -2500 to 2500, as said below
- query_fields: bfloat16 [4, 2048, 4096], P('sec', 'ctx', 'ch'), may hold values from -3 to 3
- key_fields: bfloat16 [4, 2048, 4096], P('sec', 'ctx', 'ch'), may hold values from -4 to 4
- norm_gain: float32 [4096], P('ch'), may hold values from 0.1 to 1.9
- short_taps: float32 [2, 7, 4096], P(None, None, 'ch'), may hold values from -2 to 2
- medium_taps: float32 [128, 4096], P(None, 'ch'), may hold values from -0.5 to 0.5
- pole_rates: float32 [8, 4096], P(None, 'ch'), as said below
- pole_residues: float32 [8, 4096], P(None, 'ch'), may hold values from -2 to 2
- direct_term: float32 [4096], P('ch'), may hold values from -3 to 3
Outputs:
- mixed_stream: bfloat16 [2048, 4096], P('ctx', ('ch', 'sec'))
Inputs may be any that keep to these rules, and one draw needn't show every extreme that they name: `inputs`: scaled real values. `pole_rates`: Positive, from 0.2 / 2048 to 1 / 30.
All inputs are finite; a program needn't handle non-finite values.
Results may differ from a plain program's by a relative error of at most 0.013.
Values may be sent and summed in bfloat16 or wider, within the bound.
No kernel may reach another device: no remote copies, remote signals or barrier semaphores. Data moves between devices by JAX's collectives and lax.ppermute only.
A program may use at most 64 MiB of HBM per device.

v0:
```python
from functools import partial

import jax
import jax.numpy as jnp
from jax import lax
from jax.sharding import PartitionSpec as P

D = 4096


norm_eps = 1e-06


def prefix_2(value, axis, join, neutral):
    count, mine = (lax.axis_size(axis), lax.axis_index(axis))
    pieces = jax.tree.map(lambda part: lax.all_gather(part, axis), value)
    total = jax.tree.map(
        lambda part, zero: jnp.full_like(part, 0) + jnp.asarray(zero, part.dtype), value, neutral
    )

    def hop(position, total):
        longer = join(total, jax.tree.map(lambda part: part[position], pieces))
        return jax.tree.map(lambda new, old: jnp.where(position < mine, new, old), longer, total)

    return lax.fori_loop(0, count - 1, hop, total)


def passed_along(value, axis, steps):
    count = lax.axis_size(axis)
    first, last = (max(0, -steps), min(count, count - steps))
    return lax.ppermute(value, axis, [(source, source + steps) for source in range(first, last)])


def batched_depthwise(padded, flipped_taps):
    channels = padded.shape[2]
    return lax.conv_general_dilated(
        padded,
        flipped_taps[:, None, :],
        window_strides=(1,),
        padding="VALID",
        dimension_numbers=("NWC", "WIO", "NWC"),
        feature_group_count=channels,
        precision=lax.Precision.HIGHEST,
    )


def finite_filter(gated, before, filter_taps):
    span = filter_taps.shape[0]
    joined = jnp.concatenate([before[before.shape[0] - (span - 1) :], gated], axis=0)
    return batched_depthwise(joined[None], jnp.flip(filter_taps, 0))[0]


def piece_length(length):
    if length % 128 == 0:
        return 128
    return length


def modal_sum(weights, rates, length):
    offsets = jnp.arange(length, dtype=jnp.float32)
    return jnp.sum(weights[None] * jnp.exp(-rates[None] * offsets[:, None, None]), axis=1)


def piece_ends(gated, rates):
    length = gated.shape[0]
    width = piece_length(length)
    pieces = gated.reshape(length // width, width, gated.shape[1])
    row_ages = jnp.arange(width - 1, -1, -1, dtype=jnp.float32)
    table = jnp.exp(-rates[None] * row_ages[:, None, None])
    ends = jnp.einsum("imc,bic->bmc", table, pieces, precision=lax.Precision.HIGHEST)
    return (pieces, ends)


def long_filter(long_data, rates, residues, direct):
    pieces, ends, incoming = long_data
    count, width, channels = pieces.shape
    weights = residues * jnp.sqrt(-jnp.expm1(-2.0 * rates))
    kernel = modal_sum(weights, rates, width)
    padded = jnp.concatenate([jnp.zeros((count, width - 1, channels), jnp.float32), pieces], axis=1)
    within = batched_depthwise(padded, jnp.flip(kernel, 0))
    span_decay = jnp.exp(-rates * width)
    entering = []
    state = incoming
    for index in range(count):
        entering.append(state)
        state = span_decay * state + ends[index]
    entering = jnp.stack(entering)
    offsets = jnp.arange(1, width + 1, dtype=jnp.float32)
    carry_table = weights[None] * jnp.exp(-rates[None] * offsets[:, None, None])
    carried = jnp.einsum("kmc,bmc->bkc", carry_table, entering, precision=lax.Precision.HIGHEST)
    gated = pieces.reshape(count * width, channels)
    return (within + carried).reshape(count * width, channels) + direct[None] * gated


def combine(earlier, later):
    return (earlier[0] * later[1] + later[0], earlier[1] * later[1])


def carry_in(ends, rates, width, length):
    span_decay = jnp.exp(-rates * width)
    total = jnp.zeros_like(ends[0])
    for index in range(ends.shape[0]):
        total = span_decay * total + ends[index]
    powers = jnp.exp(-rates * length)
    empty = (jnp.zeros_like(total), jnp.ones_like(powers))
    prefix = prefix_2((total, powers), "ctx", combine, empty)
    return prefix[0]


def long_inputs(gated, rates):
    pieces, ends = piece_ends(gated, rates)
    incoming = carry_in(ends, rates, pieces.shape[1], gated.shape[0])
    return (pieces, ends, incoming)


def previous_rows(gated, count):
    return passed_along(gated[gated.shape[0] - count :], "ctx", 1)


def block_params(
    block_index, block_width, short_taps, medium_taps, pole_rates, pole_residues, direct_term
):

    def channel_cut(tables):
        return lax.dynamic_slice_in_dim(
            tables, block_index * block_width, block_width, tables.ndim - 1
        )

    return (
        channel_cut(short_taps),
        channel_cut(medium_taps),
        channel_cut(pole_rates),
        channel_cut(pole_residues),
        channel_cut(direct_term),
    )


def section_filter(kind, gated, before, long_data, params):
    short_pair, medium_block, rate_block, residue_block, direct_block = params
    if kind == 0:
        return finite_filter(gated, before, short_pair[0])
    if kind == 1:
        return finite_filter(gated, before, medium_block)
    if kind == 2:
        return long_filter(long_data, rate_block, residue_block, direct_block)
    return finite_filter(gated, before, short_pair[1])


def gate_update(current, query_block, filtered):
    return (current.astype(jnp.float32) + query_block.astype(jnp.float32) * filtered).astype(
        jnp.bfloat16
    )


def shards(
    inputs,
    query_fields,
    key_fields,
    norm_gain,
    short_taps,
    medium_taps,
    pole_rates,
    pole_residues,
    direct_term,
):
    sections = lax.axis_size("sec")
    segment_index = lax.axis_index("sec")
    block_width = inputs.shape[1]
    squares = jnp.sum(jnp.square(inputs.astype(jnp.float32)), axis=1)
    summed = lax.psum(squares, ("sec", "ch"))
    inverse_rms = lax.rsqrt(summed / D + norm_eps)
    gain_block = lax.dynamic_slice_in_dim(norm_gain, segment_index * block_width, block_width, 0)
    stream = (inputs.astype(jnp.float32) * inverse_rms[:, None] * gain_block[None]).astype(
        jnp.bfloat16
    )
    shard_rows = lax.all_gather(stream, "sec", axis=1, tiled=True)
    own_query = query_fields[0]
    own_key = key_fields[0]
    branches = [partial(section_filter, kind) for kind in range(4)]
    handed = stream
    received = jnp.zeros_like(stream)
    finished = []
    for step_index in range(2 * sections - 1):
        if step_index > 0:
            received = passed_along(handed, "sec", 1)
        chosen = jnp.clip(step_index - segment_index, 0, sections - 1)
        first_input = shard_rows[
            :,
            min(step_index, sections - 1)
            * block_width : (min(step_index, sections - 1) + 1)
            * block_width,
        ]
        current = jnp.where(segment_index == 0, first_input, received)
        query_block = lax.dynamic_slice_in_dim(own_query, chosen * block_width, block_width, 1)
        key_block = lax.dynamic_slice_in_dim(own_key, chosen * block_width, block_width, 1)
        gated = key_block.astype(jnp.float32) * current.astype(jnp.float32)
        params = block_params(
            chosen, block_width, short_taps, medium_taps, pole_rates, pole_residues, direct_term
        )
        before = previous_rows(gated, params[1].shape[0] - 1)
        long_data = long_inputs(gated, params[2])
        filtered = lax.switch(segment_index, branches, gated, before, long_data, params)
        handed = gate_update(current, query_block, filtered)
        if step_index >= sections - 1:
            finished.append(handed)
    returned = lax.all_to_all(jnp.stack(finished), "sec", split_axis=0, concat_axis=0, tiled=True)
    return returned[sections - 1]


def solution(mesh):
    in_specs = (
        P("ctx", ("ch", "sec")),
        P("sec", "ctx", "ch"),
        P("sec", "ctx", "ch"),
        P("ch"),
        P(None, None, "ch"),
        P(None, "ch"),
        P(None, "ch"),
        P(None, "ch"),
        P("ch"),
    )
    out_specs = P("ctx", ("ch", "sec"))
    return jax.shard_map(shards, mesh=mesh, in_specs=in_specs, out_specs=out_specs, check_vma=False)
```

profile of v0, /device:TPU:1, one launch (start us, length us, event | category | flops | bytes accessed | tf_op | source)
XLA Modules:
  0.0 390.7 jit_solution(532116077434133431)
XLA Ops:
  0.0 1.0 fusion.175
  1.0 34.3 %psum.7 = f32[128]{0:T(128)S(1)} all-reduce(f32[128]{0:T(128)S(1)} %fusion.175), channel_id=1, replica_groups=mesh['sec'=4,'ctx'=16,'ch'=4] {'sec','ch'}, use_global_device_ids=true, to_apply=%region_1.0 | all-reduce | flops 128 | bytes 1024 | tf_op jit(solution)/shard_map/psum | solution.py:170
  35.3 0.8 dynamic_slice.381
  36.1 9.4 %all_gather.87 = bf16[128,1024]{1,0:T(8,128)(2,1)S(1)} all-gather(bf16[128,256]{1,0:T(8,128)(2,1)S(1)} %fusion.177), channel_id=1, replica_groups=mesh['sec'=4,'ctx'=16,'ch'=4] {'sec'}, dimensions={1}, use_global_device_ids=true | all-gather | bytes 327680 | tf_op jit(solution)/shard_map/all_gather | solution.py:176
  45.6 14.3 %collective-permute-start = (f32[127,256]{1,0:T(8,128)S(1)}, f32[127,256]{1,0:T(8,128)S(1)}, u32[]{:S(2)}, u32[]{:S(2)}) collective-permute-start(f32[127,256]{1,0:T(8,128)S(1)} %slice.223), channel_id=1, source_target_pairs={{0,4},{4,8},{8,12},{12,16},{16,20},{20,24},{24,28},{28,32},{32,36}... | collective-permute-start | bytes 390152 | tf_op jit(solution)/shard_map/ppermute | solution.py:31
  59.9 0.7 copy-done.5
  60.9 18.6 %all-gather.1 = f32[128,256]{1,0:T(8,128)S(1)} all-gather(f32[8,256]{1,0:T(8,128)S(1)} %get-tuple-element.1968), channel_id=3, replica_groups=mesh['sec'=4,'ctx'=16,'ch'=4] {'ctx'}, dimensions={0}, use_global_device_ids=true | all-gather | bytes 139264 | tf_op jit(solution)/shard_map/all_gather | solution.py:16
  79.6 14.9 %all-gather = f32[128,256]{1,0:T(8,128)S(1)} all-gather(f32[8,256]{1,0:T(8,128)S(1)} %get-tuple-element.1969), channel_id=2, replica_groups=mesh['sec'=4,'ctx'=16,'ch'=4] {'ctx'}, dimensions={0}, use_global_device_ids=true | all-gather | bytes 139264 | tf_op jit(solution)/shard_map/all_gather | solution.py:16
  95.7 1.2 conditional.7
  96.1 0.6 copy-done.15
  97.0 1.3 collective-permute-start.1
  98.4 1.6 collective-permute-done.1
  100.2 16.7 %all-gather.3 = f32[128,256]{1,0:T(8,128)S(1)} all-gather(f32[8,256]{1,0:T(8,128)S(1)} %get-tuple-element.1966), channel_id=5, replica_groups=mesh['sec'=4,'ctx'=16,'ch'=4] {'ctx'}, dimensions={0}, use_global_device_ids=true | all-gather | bytes 139264 | tf_op jit(solution)/shard_map/all_gather | solution.py:16
  116.9 14.8 %all-gather.2 = f32[128,256]{1,0:T(8,128)S(1)} all-gather(f32[8,256]{1,0:T(8,128)S(1)} %get-tuple-element.1967), channel_id=4, replica_groups=mesh['sec'=4,'ctx'=16,'ch'=4] {'ctx'}, dimensions={0}, use_global_device_ids=true | all-gather | bytes 139264 | tf_op jit(solution)/shard_map/all_gather | solution.py:16
  131.7 3.3 collective-permute-start.2
  135.1 0.6 while.99
  135.7 1.3 collective-permute-done.2
  137.0 1.2 conditional.8
  137.4 0.6 copy-done.16
  138.3 5.6 %collective-permute-start.3 = (bf16[128,256]{1,0:T(8,128)(2,1)S(1)}, bf16[128,256]{1,0:T(8,128)(2,1)S(1)}, u32[]{:S(2)}, u32[]{:S(2)}) collective-permute-start(bf16[128,256]{1,0:T(8,128)(2,1)S(1)} %fusion.179), channel_id=1, source_target_pairs={{0,64},{64,128},{128,192},{1,65},{65,129},{129,193},{2,66},{66,130... | collective-permute-start | bytes 196616 | tf_op jit(solution)/shard_map/ppermute | solution.py:31
  143.9 1.3 collective-permute-done.3
  145.5 18.0 %all-gather.5 = f32[128,256]{1,0:T(8,128)S(1)} all-gather(f32[8,256]{1,0:T(8,128)S(1)} %get-tuple-element.1964), channel_id=7, replica_groups=mesh['sec'=4,'ctx'=16,'ch'=4] {'ctx'}, dimensions={0}, use_global_device_ids=true | all-gather | bytes 139264 | tf_op jit(solution)/shard_map/all_gather | solution.py:16
  163.5 15.6 %all-gather.4 = f32[128,256]{1,0:T(8,128)S(1)} all-gather(f32[8,256]{1,0:T(8,128)S(1)} %get-tuple-element.1965), channel_id=6, replica_groups=mesh['sec'=4,'ctx'=16,'ch'=4] {'ctx'}, dimensions={0}, use_global_device_ids=true | all-gather | bytes 139264 | tf_op jit(solution)/shard_map/all_gather | solution.py:16
  179.1 2.6 collective-permute-start.4
  181.6 0.6 while.100
  182.2 1.3 collective-permute-done.4
  183.6 1.4 conditional.9
  184.0 0.6 copy-done.17
  185.0 5.6 %collective-permute-start.5 = (bf16[128,256]{1,0:T(8,128)(2,1)S(1)}, bf16[128,256]{1,0:T(8,128)(2,1)S(1)}, u32[]{:S(2)}, u32[]{:S(2)}) collective-permute-start(bf16[128,256]{1,0:T(8,128)(2,1)S(1)} %fusion.180), channel_id=1, source_target_pairs={{0,64},{64,128},{128,192},{1,65},{65,129},{129,193},{2,66},{66,130... | collective-permute-start | bytes 196616 | tf_op jit(solution)/shard_map/ppermute | solution.py:31
  190.6 1.3 collective-permute-done.5
  192.3 18.0 %all-gather.7 = f32[128,256]{1,0:T(8,128)S(1)} all-gather(f32[8,256]{1,0:T(8,128)S(1)} %get-tuple-element.1962), channel_id=9, replica_groups=mesh['sec'=4,'ctx'=16,'ch'=4] {'ctx'}, dimensions={0}, use_global_device_ids=true | all-gather | bytes 139264 | tf_op jit(solution)/shard_map/all_gather | solution.py:16
  210.3 16.8 %all-gather.6 = f32[128,256]{1,0:T(8,128)S(1)} all-gather(f32[8,256]{1,0:T(8,128)S(1)} %get-tuple-element.1963), channel_id=8, replica_groups=mesh['sec'=4,'ctx'=16,'ch'=4] {'ctx'}, dimensions={0}, use_global_device_ids=true | all-gather | bytes 139264 | tf_op jit(solution)/shard_map/all_gather | solution.py:16
  227.1 1.9 collective-permute-start.6
  229.0 0.6 while.101
  229.6 1.3 collective-permute-done.6
  230.9 1.2 conditional.10
  231.3 0.6 copy-done.18
  232.2 5.3 %collective-permute-start.7 = (bf16[128,256]{1,0:T(8,128)(2,1)S(1)}, bf16[128,256]{1,0:T(8,128)(2,1)S(1)}, u32[]{:S(2)}, u32[]{:S(2)}) collective-permute-start(bf16[128,256]{1,0:T(8,128)(2,1)S(1)} %fusion.181), channel_id=1, source_target_pairs={{0,64},{64,128},{128,192},{1,65},{65,129},{129,193},{2,66},{66,130... | collective-permute-start | bytes 196616 | tf_op jit(solution)/shard_map/ppermute | solution.py:31
  237.5 1.9 collective-permute-done.7
  239.7 17.4 %all-gather.9 = f32[128,256]{1,0:T(8,128)S(1)} all-gather(f32[8,256]{1,0:T(8,128)S(1)} %get-tuple-element.1960), channel_id=11, replica_groups=mesh['sec'=4,'ctx'=16,'ch'=4] {'ctx'}, dimensions={0}, use_global_device_ids=true | all-gather | bytes 139264 | tf_op jit(solution)/shard_map/all_gather | solution.py:16
  257.1 17.4 %all-gather.8 = f32[128,256]{1,0:T(8,128)S(1)} all-gather(f32[8,256]{1,0:T(8,128)S(1)} %get-tuple-element.1961), channel_id=10, replica_groups=mesh['sec'=4,'ctx'=16,'ch'=4] {'ctx'}, dimensions={0}, use_global_device_ids=true | all-gather | bytes 139264 | tf_op jit(solution)/shard_map/all_gather | solution.py:16
  274.6 1.9 collective-permute-start.8
  276.5 0.6 while.102
  277.1 1.3 collective-permute-done.8
  278.4 1.2 conditional.11
  278.8 0.6 copy-done.19
  279.7 5.7 %collective-permute-start.9 = (bf16[128,256]{1,0:T(8,128)(2,1)S(1)}, bf16[128,256]{1,0:T(8,128)(2,1)S(1)}, u32[]{:S(2)}, u32[]{:S(2)}) collective-permute-start(bf16[128,256]{1,0:T(8,128)(2,1)S(1)} %fusion.182), channel_id=1, source_target_pairs={{0,64},{64,128},{128,192},{1,65},{65,129},{129,193},{2,66},{66,130... | collective-permute-start | bytes 196616 | tf_op jit(solution)/shard_map/ppermute | solution.py:31
  285.4 1.7 collective-permute-done.9
  287.4 17.4 %all-gather.11 = f32[128,256]{1,0:T(8,128)S(1)} all-gather(f32[8,256]{1,0:T(8,128)S(1)} %get-tuple-element.1958), channel_id=13, replica_groups=mesh['sec'=4,'ctx'=16,'ch'=4] {'ctx'}, dimensions={0}, use_global_device_ids=true | all-gather | bytes 139264 | tf_op jit(solution)/shard_map/all_gather | solution.py:16
  304.8 17.4 %all-gather.10 = f32[128,256]{1,0:T(8,128)S(1)} all-gather(f32[8,256]{1,0:T(8,128)S(1)} %get-tuple-element.1959), channel_id=12, replica_groups=mesh['sec'=4,'ctx'=16,'ch'=4] {'ctx'}, dimensions={0}, use_global_device_ids=true | all-gather | bytes 139264 | tf_op jit(solution)/shard_map/all_gather | solution.py:16
  322.3 1.9 collective-permute-start.10
  324.8 1.3 collective-permute-done.10
  326.1 1.2 conditional.12
  326.5 0.6 copy-done.20
  327.4 5.5 %collective-permute-start.11 = (bf16[128,256]{1,0:T(8,128)(2,1)S(1)}, bf16[128,256]{1,0:T(8,128)(2,1)S(1)}, u32[]{:S(2)}, u32[]{:S(2)}) collective-permute-start(bf16[128,256]{1,0:T(8,128)(2,1)S(1)} %fusion.183), channel_id=1, source_target_pairs={{0,64},{64,128},{128,192},{1,65},{65,129},{129,193},{2,66},{66,130... | collective-permute-start | bytes 196616 | tf_op jit(solution)/shard_map/ppermute | solution.py:31
  332.9 1.9 collective-permute-done.11
  335.1 17.4 %all-gather.13 = f32[128,256]{1,0:T(8,128)S(1)} all-gather(f32[8,256]{1,0:T(8,128)S(1)} %get-tuple-element.1956), channel_id=15, replica_groups=mesh['sec'=4,'ctx'=16,'ch'=4] {'ctx'}, dimensions={0}, use_global_device_ids=true | all-gather | bytes 139264 | tf_op jit(solution)/shard_map/all_gather | solution.py:16
  352.6 17.4 %all-gather.12 = f32[128,256]{1,0:T(8,128)S(1)} all-gather(f32[8,256]{1,0:T(8,128)S(1)} %get-tuple-element.1957), channel_id=14, replica_groups=mesh['sec'=4,'ctx'=16,'ch'=4] {'ctx'}, dimensions={0}, use_global_device_ids=true | all-gather | bytes 139264 | tf_op jit(solution)/shard_map/all_gather | solution.py:16
  370.0 1.9 collective-permute-start.12
  372.5 1.3 collective-permute-done.12
  373.8 1.2 conditional.13
  374.2 0.6 copy-done.21
  375.2 14.9 %all_to_all.5 = bf16[4,128,256]{2,1,0:T(8,128)(2,1)S(1)} all-to-all(bf16[4,128,256]{2,1,0:T(8,128)(2,1)S(1)} %pad_maximum_fusion.7), channel_id=1, replica_groups=mesh['sec'=4,'ctx'=16,'ch'=4] {'sec'}, dimensions={0} | all-to-all | bytes 524288 | tf_op jit(solution)/shard_map/all_to_all | solution.py:206
  390.1 0.6 slice_bitcast_fusion.14
  (269 shorter events, 9.6 us)
Async XLA Ops:
  0.0 36.1 %copy-start.4 = (bf16[128,256]{1,0:T(8,128)(2,1)S(1)}, bf16[128,256]{1,0:T(8,128)(2,1)}, u32[]{:S(2)}) copy-start(bf16[128,256]{1,0:T(8,128)(2,1)} %param.51) | copy-start | bytes 196612
  0.0 45.5 %copy-start.2 = (bf16[1,128,1024]{2,1,0:T(8,128)(2,1)S(1)}, bf16[1,128,1024]{2,1,0:T(8,128)(2,1)}, u32[]{:S(2)}) copy-start(bf16[1,128,1024]{2,1,0:T(8,128)(2,1)} %param.53) | copy-start | bytes 786436
  45.6 49.5 %collective-permute-start = (f32[127,256]{1,0:T(8,128)S(1)}, f32[127,256]{1,0:T(8,128)S(1)}, u32[]{:S(2)}, u32[]{:S(2)}) collective-permute-start(f32[127,256]{1,0:T(8,128)S(1)} %slice.223), channel_id=1, source_target_pairs={{0,4},{4,8},{8,12},{12,16},{16,20},{20,24},{24,28},{28,32},{32,36}... | collective-permute-start | bytes 390152 | tf_op jit(solution)/shard_map/ppermute | solution.py:31
  59.9 0.8 copy-start.5
  60.6 34.4 %copy-start.1 = (f32[128,1024]{1,0:T(8,128)S(1)}, f32[128,1024]{1,0:T(8,128)}, u32[]{:S(2)}) copy-start(f32[128,1024]{1,0:T(8,128)} %param.56) | copy-start | bytes 1572868
  79.6 15.5 %copy-start.6 = (f32[8,1024]{1,0:T(8,128)S(1)}, f32[8,1024]{1,0:T(8,128)}, u32[]{:S(2)}) copy-start(f32[8,1024]{1,0:T(8,128)} %param.58) | copy-start | bytes 98308
  94.5 0.8 copy-start
  95.0 0.7 copy-start.7
  95.7 1.2 copy-start.3
  96.1 0.7 copy-start.15
  97.0 2.9 collective-permute-start.1
  131.7 5.3 %collective-permute-start.2 = (f32[127,256]{1,0:T(8,128)S(1)}, f32[127,256]{1,0:T(8,128)S(1)}, u32[]{:S(2)}, u32[]{:S(2)}) collective-permute-start(f32[127,256]{1,0:T(8,128)S(1)} %slice.224), channel_id=1, source_target_pairs={{0,4},{4,8},{8,12},{12,16},{16,20},{20,24},{24,28},{28,32},{32,36}... | collective-permute-start | bytes 390152 | tf_op jit(solution)/shard_map/ppermute | solution.py:31
  137.3 0.7 copy-start.16
  138.3 6.9 %collective-permute-start.3 = (bf16[128,256]{1,0:T(8,128)(2,1)S(1)}, bf16[128,256]{1,0:T(8,128)(2,1)S(1)}, u32[]{:S(2)}, u32[]{:S(2)}) collective-permute-start(bf16[128,256]{1,0:T(8,128)(2,1)S(1)} %fusion.179), channel_id=1, source_target_pairs={{0,64},{64,128},{128,192},{1,65},{65,129},{129,193},{2,66},{66,130... | collective-permute-start | bytes 196616 | tf_op jit(solution)/shard_map/ppermute | solution.py:31
  179.1 4.5 %collective-permute-start.4 = (f32[127,256]{1,0:T(8,128)S(1)}, f32[127,256]{1,0:T(8,128)S(1)}, u32[]{:S(2)}, u32[]{:S(2)}) collective-permute-start(f32[127,256]{1,0:T(8,128)S(1)} %slice.225), channel_id=1, source_target_pairs={{0,4},{4,8},{8,12},{12,16},{16,20},{20,24},{24,28},{28,32},{32,36}... | collective-permute-start | bytes 390152 | tf_op jit(solution)/shard_map/ppermute | solution.py:31
  183.9 0.7 copy-start.17
  185.0 6.9 %collective-permute-start.5 = (bf16[128,256]{1,0:T(8,128)(2,1)S(1)}, bf16[128,256]{1,0:T(8,128)(2,1)S(1)}, u32[]{:S(2)}, u32[]{:S(2)}) collective-permute-start(bf16[128,256]{1,0:T(8,128)(2,1)S(1)} %fusion.180), channel_id=1, source_target_pairs={{0,64},{64,128},{128,192},{1,65},{65,129},{129,193},{2,66},{66,130... | collective-permute-start | bytes 196616 | tf_op jit(solution)/shard_map/ppermute | solution.py:31
  227.1 3.8 collective-permute-start.6
  231.2 0.7 copy-start.18
  232.2 7.2 %collective-permute-start.7 = (bf16[128,256]{1,0:T(8,128)(2,1)S(1)}, bf16[128,256]{1,0:T(8,128)(2,1)S(1)}, u32[]{:S(2)}, u32[]{:S(2)}) collective-permute-start(bf16[128,256]{1,0:T(8,128)(2,1)S(1)} %fusion.181), channel_id=1, source_target_pairs={{0,64},{64,128},{128,192},{1,65},{65,129},{129,193},{2,66},{66,130... | collective-permute-start | bytes 196616 | tf_op jit(solution)/shard_map/ppermute | solution.py:31
  274.6 3.8 collective-permute-start.8
  278.8 0.7 copy-start.19
  279.7 7.4 %collective-permute-start.9 = (bf16[128,256]{1,0:T(8,128)(2,1)S(1)}, bf16[128,256]{1,0:T(8,128)(2,1)S(1)}, u32[]{:S(2)}, u32[]{:S(2)}) collective-permute-start(bf16[128,256]{1,0:T(8,128)(2,1)S(1)} %fusion.182), channel_id=1, source_target_pairs={{0,64},{64,128},{128,192},{1,65},{65,129},{129,193},{2,66},{66,130... | collective-permute-start | bytes 196616 | tf_op jit(solution)/shard_map/ppermute | solution.py:31
  322.3 3.8 collective-permute-start.10
  326.5 0.7 copy-start.20
  327.4 7.4 %collective-permute-start.11 = (bf16[128,256]{1,0:T(8,128)(2,1)S(1)}, bf16[128,256]{1,0:T(8,128)(2,1)S(1)}, u32[]{:S(2)}, u32[]{:S(2)}) collective-permute-start(bf16[128,256]{1,0:T(8,128)(2,1)S(1)} %fusion.183), channel_id=1, source_target_pairs={{0,64},{64,128},{128,192},{1,65},{65,129},{129,193},{2,66},{66,130... | collective-permute-start | bytes 196616 | tf_op jit(solution)/shard_map/ppermute | solution.py:31
  370.0 3.8 collective-permute-start.12
  374.2 0.7 copy-start.21
where the time goes:
time: 392 us; the launch traced here: 391 us
  blocking collectives  297 us (76%)
  starting transfers between devices  56.8 us (14%)
  waiting for transfers between devices  17.7 us (5%)
  local copies, waits for them, and re-layouts  10.2 us (3%)
  other arithmetic  4.65 us (1%)
    all_gather x14, blocking collectives, prefix_2(): pieces = jax.tree.map(lambda part: lax.all_gather(part, axis), value)  238 us
    ppermute x13, starting transfers between devices, passed_along(): lax.ppermute(value, axis, [(source, source + steps) for source in range(f...  56.8 us
    psum x1, blocking collectives, shards(): summed = lax.psum(squares, ('sec', 'ch'))  34.3 us
    ppermute x13, waiting for transfers between devices, passed_along(): lax.ppermute(value, axis, [(source, source + steps) for source in range(f...  17.7 us
    all_to_all x1, blocking collectives, shards(): lax.all_to_all(jnp.stack(finished), 'sec', split_axis=0, concat_axis=0, t...  14.9 us
    all_gather x1, blocking collectives, shards(): shard_rows = lax.all_gather(stream, 'sec', axis=1, tiled=True)  9.37 us
  transfers between devices with their start and end apart: 13, of which 12 were waited for; matrix products, arithmetic and copies ran while one was open for 0% of the time, Pallas kernels for 0%

commit v1 on v0

v1 whole, which is shorter than its diff:
```python
import jax
import jax.numpy as jnp
from jax import lax
from jax.experimental import pallas as pl
from jax.experimental.pallas import tpu as pltpu
from jax.sharding import PartitionSpec as P

D = 4096
EPS = 1e-06
ROWS = 128
WIDTH = 256
SEC = 4
CTX = 16
PEERS = 16
f32 = jnp.float32
bf16 = jnp.bfloat16


def shifted(value, axis, steps, wrap):
    count = lax.axis_size(axis)
    pairs = [
        (source, (source + steps) % count)
        for source in range(count)
        if wrap or 0 <= source + steps < count
    ]
    return lax.ppermute(value, axis, pairs)


def lanes_of(position):
    return pl.ds(pl.multiple_of(position * WIDTH, WIDTH), WIDTH)


def pack_kernel(x_ref, q_ref, k_ref, squares_ref, own_ref, *send_refs):
    sec = lax.axis_index("sec")
    x = x_ref[...].astype(f32)
    squared = x * x
    folded = squared[:, :128] + squared[:, 128:]
    squares = jnp.sum(folded.T, axis=0, keepdims=True)
    squares_ref[...] = jnp.broadcast_to(squares, squares_ref.shape)
    for distance, ref in enumerate((own_ref,) + send_refs):
        lanes = lanes_of(lax.rem(sec + distance, SEC))
        ref[0] = q_ref[0, :, lanes]
        ref[1] = k_ref[0, :, lanes]


def field_of(refs, section, which, rows=None):
    distance = lax.rem(lax.axis_index("sec") - section + SEC, SEC)

    def read(ref):
        part = ref[which] if rows is None else ref[which, rows]
        return part.astype(f32)

    chosen = read(refs[0])
    for index in range(1, SEC):
        chosen = jnp.where(distance == index, read(refs[index]), chosen)
    return chosen


def short_sum(padded_ref, taps):
    total = taps[0:1] * padded_ref[8 : 8 + ROWS]
    for tap in range(1, 7):
        total += taps[tap : tap + 1] * padded_ref[8 - tap : 8 - tap + ROWS]
    return total


def first_kernel(
    x_ref, squares_ref, gain_ref, taps_ref, f0, f1, f2, f3,
    head_ref, stream_ref, halo_ref, far_ref, pad_ref,
):
    fields = (f0, f1, f2, f3)
    lanes = lanes_of(lax.axis_index("sec"))
    sums = jnp.sum(squares_ref[...], axis=0, keepdims=True)
    inverse = lax.rsqrt(jnp.broadcast_to(sums, (128, 128)).T / D + EPS)
    inverse = jnp.concatenate([inverse, inverse], axis=1)
    stream = (x_ref[...].astype(f32) * inverse * gain_ref[:, lanes]).astype(bf16).astype(f32)
    gated = field_of(fields, 0, 1) * stream
    pad_ref[0:8] = jnp.zeros((8, WIDTH), f32)
    pad_ref[8:] = gated
    filtered = short_sum(pad_ref, taps_ref[0, :, lanes])
    q0 = field_of(fields, 0, 0)
    k1 = field_of(fields, 1, 1)
    raw = stream + q0 * filtered
    head_ref[...] = raw[0:8]
    rounded = raw.astype(bf16)
    stream_ref[...] = rounded
    rounded = rounded.astype(f32)
    halo_ref[0:8] = k1[0:8] * raw[0:8]
    halo_ref[8:ROWS] = k1[8:] * rounded[8:]
    halo_ref[ROWS : ROWS + 8] = gated[ROWS - 8 :]
    halo_ref[ROWS + 8 : ROWS + 16] = k1[0:8] * q0[0:8]
    far_ref[...] = gated[ROWS - 8 :]


def medium_part(source_ref, taps_ref, partial_ref, groups, first_source):
    low, high = groups

    def step(index, carry):
        shift = lax.rem(index, 8)
        column = index // 8
        here = pl.ds(pl.multiple_of(column * 128, 128), 128)
        taps = [
            jnp.broadcast_to(taps_ref[shift, a : a + 1, here], (8, 128)) for a in range(16)
        ]
        for group in range(low, high):
            total = None
            for a in range(16):
                origin = group - a
                if origin < first_source:
                    continue
                start = 8 * (origin - first_source)
                term = taps[a] * source_ref[start : start + 8, here]
                total = term if total is None else total + term
            start = 8 * (group - low)
            partial_ref[shift, start : start + 8, here] = total
        return carry

    lax.fori_loop(0, 16, step, 0)


def mode_rows(state, decays, weights, rows):
    position = lax.broadcasted_iota(jnp.int32, (8, WIDTH), 0)
    sums = jnp.zeros((8, WIDTH), f32)
    for row in range(8):
        state = decays * state
        if rows is not None:
            state = state + rows[row : row + 1]
        summed = jnp.sum(weights * state, axis=0, keepdims=True)
        sums = jnp.where(position == row, summed, sums)
    return state, sums


def second_kernel(
    own_ref, near_ref, far_ref, head_ref, stream_ref, short_ref, medium_ref,
    rates_ref, residues_ref, direct_ref, f0, f1, f2, f3,
    next_ref, gated_ref, ends_ref, tail_ref,
    source_ref, partial_ref, taps_ref, pad_ref,
):
    fields = (f0, f1, f2, f3)
    sec = lax.axis_index("sec")
    lanes = lanes_of(sec)
    taps = short_ref[0, :, lanes]

    def correction(before):
        pad_ref[0:8] = before
        pad_ref[8:16] = jnp.zeros((8, WIDTH), f32)
        total = jnp.zeros((8, WIDTH), f32)
        for tap in range(1, 7):
            total += taps[tap : tap + 1] * pad_ref[8 - tap : 16 - tap]
        return total

    head_q0 = field_of(fields, 0, 0, pl.ds(0, 16))[0:8]
    head_k1 = field_of(fields, 1, 1, pl.ds(0, 16))[0:8]
    mine = (head_ref[...] + head_q0 * correction(near_ref[ROWS : ROWS + 8])).astype(bf16).astype(f32)
    source_ref[0:8] = near_ref[0:8] + near_ref[ROWS + 8 : ROWS + 16] * correction(far_ref[...])
    source_ref[8:ROWS] = near_ref[8:ROWS]
    source_ref[ROWS : ROWS + 8] = head_k1 * mine
    source_ref[ROWS + 8 :] = own_ref[8:ROWS]
    medium_taps = medium_ref[:, lanes].reshape(16, 8, WIDTH)
    for shift in range(8):
        taps_ref[shift] = medium_taps[:, shift]
    medium_part(source_ref, taps_ref, partial_ref, (-1, 16), -16)
    filtered = partial_ref[0, 8 : 8 + ROWS]
    for shift in range(1, 8):
        filtered += partial_ref[shift, 8 - shift : 8 - shift + ROWS]
    stream = jnp.concatenate([mine, stream_ref[...].astype(f32)[8:]], axis=0)
    stream = (stream + field_of(fields, 1, 0) * filtered).astype(bf16)
    next_ref[...] = stream
    stream = stream.astype(f32)
    gated = field_of(fields, 2, 1) * stream
    gated_ref[...] = gated
    rates = rates_ref[:, lanes]
    decays = jnp.exp(-rates)
    weights = residues_ref[:, lanes] * jnp.sqrt(jnp.tanh(rates) * (1.0 + jnp.exp(-2.0 * rates)))

    def step(index, state):
        rows = gated_ref[pl.ds(pl.multiple_of(index * 8, 8), 8)]
        for row in range(8):
            state = decays * state + rows[row : row + 1]
        return state

    state = lax.fori_loop(0, ROWS // 8 - 1, step, jnp.zeros((8, WIDTH), f32))
    last = gated[ROWS - 8 :]
    state, sums = mode_rows(state, decays, weights, last)
    ends_ref[...] = jnp.broadcast_to(state[None], ends_ref.shape)
    q2 = field_of(fields, 2, 0, pl.ds(ROWS - 16, 16))[8:]
    k3 = field_of(fields, 3, 1, pl.ds(ROWS - 16, 16))[8:]
    tail_ref[0:8] = k3 * (stream[ROWS - 8 :] + q2 * (sums + direct_ref[:, lanes] * last))
    tail_ref[8:16] = k3 * q2


def third_kernel(
    gated_ref, stream_ref, ends_ref, tail_ref, short_ref,
    rates_ref, residues_ref, direct_ref, f0, f1, f2, f3,
    out_ref, sums_ref, pad_ref,
):
    fields = (f0, f1, f2, f3)
    lanes = lanes_of(lax.axis_index("sec"))
    mine = lax.axis_index("ctx")
    rates = rates_ref[:, lanes]
    decays = jnp.exp(-rates)
    weights = residues_ref[:, lanes] * jnp.sqrt(jnp.tanh(rates) * (1.0 + jnp.exp(-2.0 * rates)))
    span = jnp.exp(-rates * ROWS)
    state = jnp.zeros((8, WIDTH), f32)
    previous = state
    for position in range(CTX - 1):
        longer = span * state + ends_ref[position]
        previous = jnp.where(position < mine - 1, longer, previous)
        state = jnp.where(position < mine, longer, state)
    tail_state = jnp.exp(-rates * (ROWS - 8)) * previous
    _, carried = mode_rows(tail_state, decays, weights, None)
    pad_ref[0:8] = tail_ref[0:8] + tail_ref[8:16] * carried

    def step(index, state):
        here = pl.ds(pl.multiple_of(index * 8, 8), 8)
        state, sums = mode_rows(state, decays, weights, gated_ref[here])
        sums_ref[here] = sums
        return state

    lax.fori_loop(0, ROWS // 8, step, state)
    filtered = sums_ref[...] + direct_ref[:, lanes] * gated_ref[...]
    stream = stream_ref[...].astype(f32) + field_of(fields, 2, 0) * filtered
    stream = stream.astype(bf16).astype(f32)
    pad_ref[8:] = field_of(fields, 3, 1) * stream
    filtered = short_sum(pad_ref, short_ref[1, :, lanes])
    out_ref[...] = (stream + field_of(fields, 3, 0) * filtered).astype(bf16)


def shape(dims, dtype):
    return jax.ShapeDtypeStruct(dims, dtype)


def call(kernel, outs, scratch, operands, name, flops=1000000):
    vmem = pl.BlockSpec(memory_space=pltpu.VMEM)
    return pl.pallas_call(
        kernel,
        out_shape=outs,
        in_specs=[vmem] * len(operands),
        out_specs=[vmem] * len(outs),
        scratch_shapes=scratch,
        compiler_params=pltpu.CompilerParams(vmem_limit_bytes=32 * 1024 * 1024),
        cost_estimate=pl.CostEstimate(flops=flops, bytes_accessed=1000000, transcendentals=0),
        name=name,
    )(*operands)


def shards(x, q, k, gain, short, medium, rates, residues, direct):
    gain, direct = gain[None], direct[None]
    pair = shape((2, ROWS, WIDTH), bf16)
    squares, own, *sends = call(
        pack_kernel, [shape((PEERS, 128), f32)] + [pair] * 4, [], (x, q, k), "pack"
    )
    fields = [own] + [
        shifted(part, "sec", distance + 1, True) for distance, part in enumerate(sends)
    ]
    squares = lax.all_to_all(squares, ("sec", "ch"), 0, 0, tiled=True)
    head, stream, halo, far = call(
        first_kernel,
        [
            shape((8, WIDTH), f32),
            shape((ROWS, WIDTH), bf16),
            shape((ROWS + 16, WIDTH), f32),
            shape((8, WIDTH), f32),
        ],
        [pltpu.VMEM((ROWS + 8, WIDTH), f32)],
        (x, squares, gain, short, *fields),
        "first",
    )
    near_in = shifted(halo, "ctx", 1, False)
    far_in = shifted(far, "ctx", 2, False)
    stream, gated, ends, tail = call(
        second_kernel,
        [
            shape((ROWS, WIDTH), bf16),
            shape((ROWS, WIDTH), f32),
            shape((CTX, 8, WIDTH), f32),
            shape((16, WIDTH), f32),
        ],
        [
            pltpu.VMEM((2 * ROWS, WIDTH), f32),
            pltpu.VMEM((8, ROWS + 8, WIDTH), f32),
            pltpu.VMEM((8, 16, WIDTH), f32),
            pltpu.VMEM((16, WIDTH), f32),
        ],
        (halo, near_in, far_in, head, stream, short, medium, rates, residues, direct, *fields),
        "second",
    )
    tail_in = shifted(tail, "ctx", 1, False)
    ends = lax.all_to_all(ends, "ctx", 0, 0, tiled=True)
    (out,) = call(
        third_kernel,
        [shape((ROWS, WIDTH), bf16)],
        [pltpu.VMEM((ROWS, WIDTH), f32), pltpu.VMEM((ROWS + 8, WIDTH), f32)],
        (gated, stream, ends, tail_in, short, rates, residues, direct, *fields),
        "third",
    )
    return out


def solution(mesh):
    in_specs = (
        P("ctx", ("ch", "sec")),
        P("sec", "ctx", "ch"),
        P("sec", "ctx", "ch"),
        P("ch"),
        P(None, None, "ch"),
        P(None, "ch"),
        P(None, "ch"),
        P(None, "ch"),
        P("ch"),
    )
    out_specs = P("ctx", ("ch", "sec"))
    return jax.shard_map(shards, mesh=mesh, in_specs=in_specs, out_specs=out_specs, check_vma=False)
```

time: 392 us -> 54.2 us (0.14)
  blocking collectives: 297 us -> 0 us
  starting transfers between devices: 56.8 us -> 32.9 us
  local copies, waits for them, and re-layouts: 10.2 us -> 2.8 us
  Pallas kernels: 0 us -> 5.18 us
  waiting for transfers between devices: 17.7 us -> 12.8 us
  other arithmetic: 4.65 us -> 0 us
    all_gather x15 -> x0, blocking collectives: 247 us -> none  [the longest x14 238 us: prefix_2(): pieces = jax.tree.map(lambda part: lax.all_gather(part, axis), value)]
    ppermute x13 -> x6, starting transfers between devices: 56.8 us -> 19.3 us  [shifted(): return lax.ppermute(value, axis, pairs)]
    psum x1 -> x0, blocking collectives: 34.3 us -> none  [shards(): summed = lax.psum(squares, ('sec', 'ch'))]
    ppermute x13 -> x6, waiting for transfers between devices: 17.7 us -> 1.63 us  [shifted(): return lax.ppermute(value, axis, pairs)]
    all_to_all x1 -> x0, blocking collectives: 14.9 us -> none  [shards(): lax.all_to_all(jnp.stack(finished), 'sec', split_axis=0, concat_axis=0, t...]
    all_to_all x0 -> x2, starting transfers between devices: none -> 13.6 us  [the longest x1 9.4 us: shards(): ends = lax.all_to_all(ends, 'ctx', 0, 0, tiled=True)]
    all_to_all x0 -> x2, waiting for transfers between devices: none -> 11.1 us  [the longest x1 6.29 us: shards(): squares = lax.all_to_all(squares, ('sec', 'ch'), 0, 0, tiled=True)]
    pallas_call x0 -> x4, Pallas kernels: none -> 5.18 us  [call(): pl.pallas_call(kernel, out_shape=outs, in_specs=[vmem] * len(operands), o...]
  transfers between devices with their start and end apart: 13 -> 8, of which waited for: 12 -> 4; matrix products, arithmetic and copies ran while one was open for 0% -> 0% of each run, Pallas kernels for 0% -> 0%
where the time goes in v1:
time: 54.2 us; the launch traced here: 53.8 us
  starting transfers between devices  32.9 us (61%)
  waiting for transfers between devices  12.8 us (24%)
  Pallas kernels  5.18 us (10%)
  local copies, waits for them, and re-layouts  2.8 us (5%)
    ppermute x6, starting transfers between devices, shifted(): return lax.ppermute(value, axis, pairs)  19.3 us
    all_to_all x1, starting transfers between devices, shards(): ends = lax.all_to_all(ends, 'ctx', 0, 0, tiled=True)  9.4 us
    all_to_all x1, waiting for transfers between devices, shards(): squares = lax.all_to_all(squares, ('sec', 'ch'), 0, 0, tiled=True)  6.29 us
    pallas_call x4, Pallas kernels, call(): pl.pallas_call(kernel, out_shape=outs, in_specs=[vmem] * len(operands), o...  5.18 us
    all_to_all x1, waiting for transfers between devices, shards(): ends = lax.all_to_all(ends, 'ctx', 0, 0, tiled=True)  4.84 us
    all_to_all x1, starting transfers between devices, shards(): squares = lax.all_to_all(squares, ('sec', 'ch'), 0, 0, tiled=True)  4.24 us
    unnamed x21, local copies, waits for them, and re-layouts  2.8 us
    ppermute x6, waiting for transfers between devices, shifted(): return lax.ppermute(value, axis, pairs)  1.63 us
  transfers between devices with their start and end apart: 8, of which 4 were waited for; matrix products, arithmetic and copies ran while one was open for 0% of the time, Pallas kernels for 0%

profile of v1, /device:TPU:1, one launch (start us, length us, event | category | flops | bytes accessed | tf_op | source)
XLA Modules:
  0.0 53.8 jit_solution(12814043593343330593)
XLA Ops:
  0.0 0.0 copy-start.1
  0.0 0.9 %copy-done.1 = bf16[1,128,1024]{2,1,0:T(8,128)(2,1)S(1)} copy-done((bf16[1,128,1024]{2,1,0:T(8,128)(2,1)S(1)}, bf16[1,128,1024]{2,1,0:T(8,128)(2,1)}, u32[]{:S(2)}) %copy-start.1) | copy-done | bytes 262168
  1.0 0.0 copy-start.2
  1.0 0.9 %copy-done.2 = bf16[1,128,1024]{2,1,0:T(8,128)(2,1)S(1)} copy-done((bf16[1,128,1024]{2,1,0:T(8,128)(2,1)S(1)}, bf16[1,128,1024]{2,1,0:T(8,128)(2,1)}, u32[]{:S(2)}) %copy-start.2) | copy-done | bytes 262168
  1.9 0.0 copy-start.3
  1.9 0.8 %copy-done.3 = bf16[128,256]{1,0:T(8,128)(2,1)S(1)} copy-done((bf16[128,256]{1,0:T(8,128)(2,1)S(1)}, bf16[128,256]{1,0:T(8,128)(2,1)}, u32[]{:S(2)}) %copy-start.3) | copy-done | bytes 65560
  2.7 0.0 copy-start.9
  2.7 0.0 copy-start.4
  2.7 0.0 copy-start.8
  2.7 0.7 %pack.1 = (f32[16,128]{1,0:T(8,128)}, bf16[2,128,256]{2,1,0:T(8,128)(2,1)S(1)}, bf16[2,128,256]{2,1,0:T(8,128)(2,1)S(1)}, bf16[2,128,256]{2,1,0:T(8,128)(2,1)S(1)}, bf16[2,128,256]{2,1,0:T(8,128)(2,1)S(1)}) custom-call(bf16[128,256]{1,0:T(8,128)(2,1)S(1)} %copy-done.3, bf16[1,128,1024]{2,1,0:T(8,128)(2,1)S(1)} %copy-done.1, bf16[1,128,1024]{2,1,0:T(8,128)(2,1)S(1)} %copy-done.2), custom_call_target="tpu_custom_call" | custom-call | flops 1000000 | bytes 1000000 | tf_op jit(solution)/shard_map/pack/pallas_call | solution.py:234
  3.5 0.0 copy-start
  3.5 2.1 %collective-permute-start = (bf16[2,128,256]{2,1,0:T(8,128)(2,1)S(1)}, bf16[2,128,256]{2,1,0:T(8,128)(2,1)S(1)}, u32[]{:S(2)}, u32[]{:S(2)}) collective-permute-start(bf16[2,128,256]{2,1,0:T(8,128)(2,1)S(1)} %get-tuple-element.20), channel_id=1, source_target_pairs={{0,64},{64,128},{128,192},{192,0},{1,65},{65,129},{129,193},{193,1... | collective-permute-start | bytes 393224 | tf_op jit(solution)/shard_map/ppermute | solution.py:26
  5.6 2.6 %collective-permute-start.1 = (bf16[2,128,256]{2,1,0:T(8,128)(2,1)S(1)}, bf16[2,128,256]{2,1,0:T(8,128)(2,1)S(1)}, u32[]{:S(2)}, u32[]{:S(2)}) collective-permute-start(bf16[2,128,256]{2,1,0:T(8,128)(2,1)S(1)} %get-tuple-element.21), channel_id=1, source_target_pairs={{0,128},{64,192},{128,0},{192,64},{1,129},{65,193},{129,1},{193,65... | collective-permute-start | bytes 393224 | tf_op jit(solution)/shard_map/ppermute | solution.py:26
  8.2 1.1 %collective-permute-start.2 = (bf16[2,128,256]{2,1,0:T(8,128)(2,1)S(1)}, bf16[2,128,256]{2,1,0:T(8,128)(2,1)S(1)}, u32[]{:S(2)}, u32[]{:S(2)}) collective-permute-start(bf16[2,128,256]{2,1,0:T(8,128)(2,1)S(1)} %get-tuple-element.22), channel_id=1, source_target_pairs={{0,192},{64,0},{128,64},{192,128},{1,193},{65,1},{129,65},{193,129... | collective-permute-start | bytes 393224 | tf_op jit(solution)/shard_map/ppermute | solution.py:26
  9.3 4.2 %all-to-all-start = ((f32[16,1,128]{2,1,0:T(1,128)}), f32[16,1,128]{2,1,0:T(1,128)S(1)}, u32[]{:S(2)}, u32[]{:S(2)}) async-start(f32[16,1,128]{2,1,0:T(1,128)} %bitcast.1), calls=%async_computation | async-start | bytes 16384 | tf_op jit(solution)/shard_map/all_to_all | solution.py:255
  13.5 0.0 copy-done.9
  13.6 6.3 %all-to-all-done = f32[16,1,128]{2,1,0:T(1,128)S(1)} async-done(((f32[16,1,128]{2,1,0:T(1,128)}), f32[16,1,128]{2,1,0:T(1,128)S(1)}, u32[]{:S(2)}, u32[]{:S(2)}) %all-to-all-start) | async-done | bytes 8224 | tf_op jit(solution)/shard_map/all_to_all | solution.py:255
  19.9 0.0 collective-permute-done.f1
  19.9 0.0 collective-permute-done.1.f2
  19.9 0.0 collective-permute-done.2.f3
  19.9 0.0 copy-done.4
  19.9 0.0 copy-done.8
  19.9 0.0 copy-start.5
  19.9 0.0 copy-start.6
  19.9 0.3 first.1
  20.3 0.0 copy-start.7
  20.3 6.4 %collective-permute-start.3 = (f32[144,256]{1,0:T(8,128)S(1)}, f32[144,256]{1,0:T(8,128)S(1)}, u32[]{:S(2)}, u32[]{:S(2)}) collective-permute-start(f32[144,256]{1,0:T(8,128)S(1)} %get-tuple-element.23.own_ref), channel_id=1, source_target_pairs={{0,4},{4,8},{8,12},{12,16},{16,20},{20,24},{24,28},{28,32},{32,36}... | collective-permute-start | bytes 442376 | tf_op jit(solution)/shard_map/ppermute | solution.py:26
  26.7 3.5 %collective-permute-start.4 = (f32[8,256]{1,0:T(8,128)S(1)}, f32[8,256]{1,0:T(8,128)S(1)}, u32[]{:S(2)}, u32[]{:S(2)}) collective-permute-start(f32[8,256]{1,0:T(8,128)S(1)} %get-tuple-element.24), channel_id=1, source_target_pairs={{0,8},{4,12},{8,16},{12,20},{16,24},{20,28},{24,32},{28,36},{32,40... | collective-permute-start | bytes 24584 | tf_op jit(solution)/shard_map/ppermute | solution.py:26
  30.2 0.8 %collective-permute-done.4.far_ref = f32[8,256]{1,0:T(8,128)S(1)} collective-permute-done((f32[8,256]{1,0:T(8,128)S(1)}, f32[8,256]{1,0:T(8,128)S(1)}, u32[]{:S(2)}, u32[]{:S(2)}) %collective-permute-start.4) | collective-permute-done | bytes 8224 | tf_op jit(solution)/shard_map/ppermute | solution.py:26
  31.0 0.0 collective-permute-done.3.near_ref
  31.0 0.0 copy-done
  31.0 0.0 copy-done.5
  31.0 0.0 copy-done.6
  31.0 0.0 copy-done.7
  31.0 2.6 %second.1 = (bf16[128,256]{1,0:T(8,128)(2,1)S(1)}, f32[128,256]{1,0:T(8,128)S(1)}, f32[16,8,256]{2,1,0:T(8,128)}, f32[16,256]{1,0:T(8,128)S(1)}) custom-call(f32[144,256]{1,0:T(8,128)S(1)} %get-tuple-element.23.own_ref, f32[144,256]{1,0:T(8,128)S(1)} %collective-permute-done.3.near_ref, f32[8,256]{1,0:T(8,128)S(1)} %collective-permute-done.4.far_ref, ...), custom_call_target="tpu_custom_call" | custom-call | flops 1000000 | bytes 1000000 | tf_op jit(solution)/shard_map/second/pallas_call | solution.py:234
  33.6 9.4 %all-to-all-start.1 = ((f32[16,8,256]{2,1,0:T(8,128)}), f32[16,8,256]{2,1,0:T(8,128)S(1)}, u32[]{:S(2)}, u32[]{:S(2)}) async-start(f32[16,8,256]{2,1,0:T(8,128)} %get-tuple-element.29), calls=%async_computation.1 | async-start | bytes 262144 | tf_op jit(solution)/shard_map/all_to_all | solution.py:288
  43.0 3.5 %collective-permute-start.5 = (f32[16,256]{1,0:T(8,128)S(1)}, f32[16,256]{1,0:T(8,128)S(1)}, u32[]{:S(2)}, u32[]{:S(2)}) collective-permute-start(f32[16,256]{1,0:T(8,128)S(1)} %get-tuple-element.30), channel_id=1, source_target_pairs={{0,4},{4,8},{8,12},{12,16},{16,20},{20,24},{24,28},{28,32},{32,36}... | collective-permute-start | bytes 49160 | tf_op jit(solution)/shard_map/ppermute | solution.py:26
  46.6 0.8 %collective-permute-done.5.tail_ref = f32[16,256]{1,0:T(8,128)S(1)} collective-permute-done((f32[16,256]{1,0:T(8,128)S(1)}, f32[16,256]{1,0:T(8,128)S(1)}, u32[]{:S(2)}, u32[]{:S(2)}) %collective-permute-start.5) | collective-permute-done | bytes 16416 | tf_op jit(solution)/shard_map/ppermute | solution.py:26
  47.4 4.8 %all-to-all-done.1.ends_ref = f32[16,8,256]{2,1,0:T(8,128)S(1)} async-done(((f32[16,8,256]{2,1,0:T(8,128)}), f32[16,8,256]{2,1,0:T(8,128)S(1)}, u32[]{:S(2)}, u32[]{:S(2)}) %all-to-all-start.1) | async-done | bytes 131104 | tf_op jit(solution)/shard_map/all_to_all | solution.py:288
  52.2 1.5 %third.1 = bf16[128,256]{1,0:T(8,128)(2,1)} custom-call(f32[128,256]{1,0:T(8,128)S(1)} %get-tuple-element.27.gated_ref, bf16[128,256]{1,0:T(8,128)(2,1)S(1)} %get-tuple-element.28.stream_ref, f32[16,8,256]{2,1,0:T(8,128)S(1)} %all-to-all-done.1.ends_ref, f32[16,256]{1,0:T(8,128)S(1)} %collective-permute-done.5.tail_ref, ...), custom_call_target="tpu_custom_call" | custom-call | flops 1000000 | bytes 1000000 | tf_op jit(solution)/shard_map/third/pallas_call | solution.py:234
  (1 shorter events, 0.0 us)
Async XLA Ops:
  0.0 0.9 %copy-start.1 = (bf16[1,128,1024]{2,1,0:T(8,128)(2,1)S(1)}, bf16[1,128,1024]{2,1,0:T(8,128)(2,1)}, u32[]{:S(2)}) copy-start(bf16[1,128,1024]{2,1,0:T(8,128)(2,1)} %q_ref.1) | copy-start | bytes 786436
  1.0 0.9 %copy-start.2 = (bf16[1,128,1024]{2,1,0:T(8,128)(2,1)S(1)}, bf16[1,128,1024]{2,1,0:T(8,128)(2,1)}, u32[]{:S(2)}) copy-start(bf16[1,128,1024]{2,1,0:T(8,128)(2,1)} %k_ref.1) | copy-start | bytes 786436
  1.9 0.8 %copy-start.3 = (bf16[128,256]{1,0:T(8,128)(2,1)S(1)}, bf16[128,256]{1,0:T(8,128)(2,1)}, u32[]{:S(2)}) copy-start(bf16[128,256]{1,0:T(8,128)(2,1)} %x_ref.3) | copy-start | bytes 196612
  2.7 10.8 %copy-start.9 = (f32[2,7,1024]{2,0,1:T(2,128)S(1)}, f32[2,7,1024]{2,0,1:T(2,128)}, u32[]{:S(2)}) copy-start(f32[2,7,1024]{2,0,1:T(2,128)} %param.13) | copy-start | bytes 172036
  2.7 17.1 %copy-start.4 = (bf16[128,256]{1,0:T(8,128)(2,1)S(1)}, bf16[128,256]{1,0:T(8,128)(2,1)}, u32[]{:S(2)}) copy-start(bf16[128,256]{1,0:T(8,128)(2,1)} %x_ref.3) | copy-start | bytes 196612
  2.7 17.1 %copy-start.8 = (f32[1024]{0:T(1024)S(1)}, f32[1024]{0:T(1024)}, u32[]{:S(2)}) copy-start(f32[1024]{0:T(1024)} %param.12) | copy-start | bytes 12292
  3.5 27.5 %copy-start = (f32[128,1024]{1,0:T(8,128)S(1)}, f32[128,1024]{1,0:T(8,128)}, u32[]{:S(2)}) copy-start(f32[128,1024]{1,0:T(8,128)} %medium_ref.1) | copy-start | bytes 1572868
  3.5 16.4 %collective-permute-start = (bf16[2,128,256]{2,1,0:T(8,128)(2,1)S(1)}, bf16[2,128,256]{2,1,0:T(8,128)(2,1)S(1)}, u32[]{:S(2)}, u32[]{:S(2)}) collective-permute-start(bf16[2,128,256]{2,1,0:T(8,128)(2,1)S(1)} %get-tuple-element.20), channel_id=1, source_target_pairs={{0,64},{64,128},{128,192},{192,0},{1,65},{65,129},{129,193},{193,1... | collective-permute-start | bytes 393224 | tf_op jit(solution)/shard_map/ppermute | solution.py:26
  5.6 14.3 %collective-permute-start.1 = (bf16[2,128,256]{2,1,0:T(8,128)(2,1)S(1)}, bf16[2,128,256]{2,1,0:T(8,128)(2,1)S(1)}, u32[]{:S(2)}, u32[]{:S(2)}) collective-permute-start(bf16[2,128,256]{2,1,0:T(8,128)(2,1)S(1)} %get-tuple-element.21), channel_id=1, source_target_pairs={{0,128},{64,192},{128,0},{192,64},{1,129},{65,193},{129,1},{193,65... | collective-permute-start | bytes 393224 | tf_op jit(solution)/shard_map/ppermute | solution.py:26
  8.2 11.7 %collective-permute-start.2 = (bf16[2,128,256]{2,1,0:T(8,128)(2,1)S(1)}, bf16[2,128,256]{2,1,0:T(8,128)(2,1)S(1)}, u32[]{:S(2)}, u32[]{:S(2)}) collective-permute-start(bf16[2,128,256]{2,1,0:T(8,128)(2,1)S(1)} %get-tuple-element.22), channel_id=1, source_target_pairs={{0,192},{64,0},{128,64},{192,128},{1,193},{65,1},{129,65},{193,129... | collective-permute-start | bytes 393224 | tf_op jit(solution)/shard_map/ppermute | solution.py:26
  9.3 10.6 %all-to-all-start = ((f32[16,1,128]{2,1,0:T(1,128)}), f32[16,1,128]{2,1,0:T(1,128)S(1)}, u32[]{:S(2)}, u32[]{:S(2)}) async-start(f32[16,1,128]{2,1,0:T(1,128)} %bitcast.1), calls=%async_computation | async-start | bytes 16384 | tf_op jit(solution)/shard_map/all_to_all | solution.py:255
  19.9 11.1 %copy-start.5 = (f32[8,1024]{1,0:T(8,128)S(1)}, f32[8,1024]{1,0:T(8,128)}, u32[]{:S(2)}) copy-start(f32[8,1024]{1,0:T(8,128)} %rates_ref.3) | copy-start | bytes 98308
  19.9 11.1 %copy-start.6 = (f32[8,1024]{1,0:T(8,128)S(1)}, f32[8,1024]{1,0:T(8,128)}, u32[]{:S(2)}) copy-start(f32[8,1024]{1,0:T(8,128)} %residues_ref.3) | copy-start | bytes 98308
  20.3 10.7 %copy-start.7 = (f32[1024]{0:T(1024)S(1)}, f32[1024]{0:T(1024)}, u32[]{:S(2)}) copy-start(f32[1024]{0:T(1024)} %param.17) | copy-start | bytes 12292
  20.3 10.7 %collective-permute-start.3 = (f32[144,256]{1,0:T(8,128)S(1)}, f32[144,256]{1,0:T(8,128)S(1)}, u32[]{:S(2)}, u32[]{:S(2)}) collective-permute-start(f32[144,256]{1,0:T(8,128)S(1)} %get-tuple-element.23.own_ref), channel_id=1, source_target_pairs={{0,4},{4,8},{8,12},{12,16},{16,20},{20,24},{24,28},{28,32},{32,36}... | collective-permute-start | bytes 442376 | tf_op jit(solution)/shard_map/ppermute | solution.py:26
  26.7 4.3 %collective-permute-start.4 = (f32[8,256]{1,0:T(8,128)S(1)}, f32[8,256]{1,0:T(8,128)S(1)}, u32[]{:S(2)}, u32[]{:S(2)}) collective-permute-start(f32[8,256]{1,0:T(8,128)S(1)} %get-tuple-element.24), channel_id=1, source_target_pairs={{0,8},{4,12},{8,16},{12,20},{16,24},{20,28},{24,32},{28,36},{32,40... | collective-permute-start | bytes 24584 | tf_op jit(solution)/shard_map/ppermute | solution.py:26
  33.6 18.6 %all-to-all-start.1 = ((f32[16,8,256]{2,1,0:T(8,128)}), f32[16,8,256]{2,1,0:T(8,128)S(1)}, u32[]{:S(2)}, u32[]{:S(2)}) async-start(f32[16,8,256]{2,1,0:T(8,128)} %get-tuple-element.29), calls=%async_computation.1 | async-start | bytes 262144 | tf_op jit(solution)/shard_map/all_to_all | solution.py:288
  43.0 4.4 %collective-permute-start.5 = (f32[16,256]{1,0:T(8,128)S(1)}, f32[16,256]{1,0:T(8,128)S(1)}, u32[]{:S(2)}, u32[]{:S(2)}) collective-permute-start(f32[16,256]{1,0:T(8,128)S(1)} %get-tuple-element.30), channel_id=1, source_target_pairs={{0,4},{4,8},{8,12},{12,16},{16,20},{20,24},{24,28},{28,32},{32,36}... | collective-permute-start | bytes 49160 | tf_op jit(solution)/shard_map/ppermute | solution.py:26

commit v2 on v1

--- a/solution.py
+++ b/solution.py
@@ -30,17 +30,32 @@
     return pl.ds(pl.multiple_of(position * WIDTH, WIDTH), WIDTH)
 
 
-def pack_kernel(x_ref, q_ref, k_ref, squares_ref, own_ref, *send_refs):
-    sec = lax.axis_index("sec")
+def squares_kernel(x_hbm, squares_ref, x_ref, sem):
+    load = pltpu.make_async_copy(x_hbm, x_ref, sem)
+    load.start()
+    load.wait()
     x = x_ref[...].astype(f32)
     squared = x * x
     folded = squared[:, :128] + squared[:, 128:]
     squares = jnp.sum(folded.T, axis=0, keepdims=True)
     squares_ref[...] = jnp.broadcast_to(squares, squares_ref.shape)
-    for distance, ref in enumerate((own_ref,) + send_refs):
+
+
+def pack_kernel(after_ref, q_hbm, k_hbm, own_ref, send_1, send_2, send_3, sems):
+    sec = lax.axis_index("sec")
+    loads = []
+    for distance, ref in enumerate((own_ref, send_1, send_2, send_3)):
         lanes = lanes_of(lax.rem(sec + distance, SEC))
-        ref[0] = q_ref[0, :, lanes]
-        ref[1] = k_ref[0, :, lanes]
+        for which, source in enumerate((q_hbm, k_hbm)):
+            loads.append(
+                pltpu.make_async_copy(
+                    source.at[0, :, lanes], ref.at[which], sems.at[2 * distance + which]
+                )
+            )
+    for load in loads:
+        load.start()
+    for load in loads:
+        load.wait()
 
 
 def field_of(refs, section, which, rows=None):
@@ -65,7 +80,7 @@
 
 def first_kernel(
     x_ref, squares_ref, gain_ref, taps_ref, f0, f1, f2, f3,
-    head_ref, stream_ref, halo_ref, far_ref, pad_ref,
+    head_ref, stream_ref, own_ref, halo_ref, far_ref, pad_ref,
 ):
     fields = (f0, f1, f2, f3)
     lanes = lanes_of(lax.axis_index("sec"))
@@ -84,11 +99,17 @@
     rounded = raw.astype(bf16)
     stream_ref[...] = rounded
     rounded = rounded.astype(f32)
-    halo_ref[0:8] = k1[0:8] * raw[0:8]
-    halo_ref[8:ROWS] = k1[8:] * rounded[8:]
-    halo_ref[ROWS : ROWS + 8] = gated[ROWS - 8 :]
-    halo_ref[ROWS + 8 : ROWS + 16] = k1[0:8] * q0[0:8]
-    far_ref[...] = gated[ROWS - 8 :]
+    gated_1 = jnp.concatenate([k1[0:8] * raw[0:8], k1[8:] * rounded[8:]], axis=0)
+    own_ref[...] = gated_1
+    halo_ref[0:ROWS] = gated_1.astype(bf16)
+    last = gated[ROWS - 8 :]
+    gates = k1[0:8] * q0[0:8]
+    halo_ref[ROWS : ROWS + 16] = jnp.concatenate([last, gates], axis=0).astype(bf16)
+    last_rows = pl.ds(ROWS - 16, 16)
+    halo_ref[ROWS + 16 :] = (
+        field_of(fields, 2, 0, last_rows) * field_of(fields, 3, 1, last_rows)
+    ).astype(bf16)
+    far_ref[...] = jnp.concatenate([last, last], axis=0).astype(bf16)
 
 
 def medium_part(source_ref, taps_ref, partial_ref, groups, first_source):
@@ -132,7 +153,7 @@
 def second_kernel(
     own_ref, near_ref, far_ref, head_ref, stream_ref, short_ref, medium_ref,
     rates_ref, residues_ref, direct_ref, f0, f1, f2, f3,
-    next_ref, gated_ref, ends_ref, tail_ref,
+    next_ref, gated_ref, ends_ref,
     source_ref, partial_ref, taps_ref, pad_ref,
 ):
     fields = (f0, f1, f2, f3)
@@ -150,9 +171,12 @@
 
     head_q0 = field_of(fields, 0, 0, pl.ds(0, 16))[0:8]
     head_k1 = field_of(fields, 1, 1, pl.ds(0, 16))[0:8]
-    mine = (head_ref[...] + head_q0 * correction(near_ref[ROWS : ROWS + 8])).astype(bf16).astype(f32)
-    source_ref[0:8] = near_ref[0:8] + near_ref[ROWS + 8 : ROWS + 16] * correction(far_ref[...])
-    source_ref[8:ROWS] = near_ref[8:ROWS]
+    joints = near_ref[ROWS : ROWS + 16].astype(f32)
+    mine = (head_ref[...] + head_q0 * correction(joints[0:8])).astype(bf16).astype(f32)
+    near = near_ref[0:ROWS].astype(f32)
+    far = far_ref[...].astype(f32)
+    source_ref[0:8] = near[0:8] + joints[8:16] * correction(far[0:8])
+    source_ref[8:ROWS] = near[8:]
     source_ref[ROWS : ROWS + 8] = head_k1 * mine
     source_ref[ROWS + 8 :] = own_ref[8:ROWS]
     medium_taps = medium_ref[:, lanes].reshape(16, 8, WIDTH)
@@ -181,15 +205,15 @@
     state = lax.fori_loop(0, ROWS // 8 - 1, step, jnp.zeros((8, WIDTH), f32))
     last = gated[ROWS - 8 :]
     state, sums = mode_rows(state, decays, weights, last)
-    ends_ref[...] = jnp.broadcast_to(state[None], ends_ref.shape)
     q2 = field_of(fields, 2, 0, pl.ds(ROWS - 16, 16))[8:]
     k3 = field_of(fields, 3, 1, pl.ds(ROWS - 16, 16))[8:]
-    tail_ref[0:8] = k3 * (stream[ROWS - 8 :] + q2 * (sums + direct_ref[:, lanes] * last))
-    tail_ref[8:16] = k3 * q2
+    tail = k3 * (stream[ROWS - 8 :] + q2 * (sums + direct_ref[:, lanes] * last))
+    sent = jnp.concatenate([state, tail], axis=0).astype(bf16)
+    ends_ref[...] = jnp.broadcast_to(sent[None], ends_ref.shape)
 
 
 def third_kernel(
-    gated_ref, stream_ref, ends_ref, tail_ref, short_ref,
+    gated_ref, stream_ref, ends_ref, near_ref, short_ref,
     rates_ref, residues_ref, direct_ref, f0, f1, f2, f3,
     out_ref, sums_ref, pad_ref,
 ):
@@ -202,13 +226,17 @@
     span = jnp.exp(-rates * ROWS)
     state = jnp.zeros((8, WIDTH), f32)
     previous = state
+    tail = state
     for position in range(CTX - 1):
-        longer = span * state + ends_ref[position]
+        received = ends_ref[position].astype(f32)
+        longer = span * state + received[0:8]
+        tail = jnp.where(position == mine - 1, received[8:16], tail)
         previous = jnp.where(position < mine - 1, longer, previous)
         state = jnp.where(position < mine, longer, state)
     tail_state = jnp.exp(-rates * (ROWS - 8)) * previous
     _, carried = mode_rows(tail_state, decays, weights, None)
-    pad_ref[0:8] = tail_ref[0:8] + tail_ref[8:16] * carried
+    gates = near_ref[ROWS + 16 :].astype(f32)[8:]
+    pad_ref[0:8] = tail + gates * carried
 
     def step(index, state):
         here = pl.ds(pl.multiple_of(index * 8, 8), 8)
@@ -229,15 +257,18 @@
     return jax.ShapeDtypeStruct(dims, dtype)
 
 
-def call(kernel, outs, scratch, operands, name, flops=1000000):
+def call(kernel, outs, scratch, operands, name, in_hbm=(), flops=1000000, room=32):
     vmem = pl.BlockSpec(memory_space=pltpu.VMEM)
     return pl.pallas_call(
         kernel,
         out_shape=outs,
-        in_specs=[vmem] * len(operands),
+        in_specs=[
+            pl.BlockSpec(memory_space=pltpu.HBM) if index in in_hbm else vmem
+            for index in range(len(operands))
+        ],
         out_specs=[vmem] * len(outs),
         scratch_shapes=scratch,
-        compiler_params=pltpu.CompilerParams(vmem_limit_bytes=32 * 1024 * 1024),
+        compiler_params=pltpu.CompilerParams(vmem_limit_bytes=room * 1024 * 1024),
         cost_estimate=pl.CostEstimate(flops=flops, bytes_accessed=1000000, transcendentals=0),
         name=name,
     )(*operands)
@@ -246,20 +277,37 @@
 def shards(x, q, k, gain, short, medium, rates, residues, direct):
     gain, direct = gain[None], direct[None]
     pair = shape((2, ROWS, WIDTH), bf16)
-    squares, own, *sends = call(
-        pack_kernel, [shape((PEERS, 128), f32)] + [pair] * 4, [], (x, q, k), "pack"
+    (squares,) = call(
+        squares_kernel,
+        [shape((PEERS, 128), f32)],
+        [pltpu.VMEM((ROWS, WIDTH), bf16), pltpu.SemaphoreType.DMA],
+        (x,),
+        "squares",
+        in_hbm=(0,),
+        room=60,
+    )
+    own, *sends = call(
+        pack_kernel,
+        [pair] * 4,
+        [pltpu.SemaphoreType.DMA((8,))],
+        (squares, q, k),
+        "pack",
+        in_hbm=(0, 1, 2),
+        flops=10**11,
+        room=60,
     )
     fields = [own] + [
         shifted(part, "sec", distance + 1, True) for distance, part in enumerate(sends)
     ]
     squares = lax.all_to_all(squares, ("sec", "ch"), 0, 0, tiled=True)
-    head, stream, halo, far = call(
+    head, stream, gated, halo, far = call(
         first_kernel,
         [
             shape((8, WIDTH), f32),
             shape((ROWS, WIDTH), bf16),
-            shape((ROWS + 16, WIDTH), f32),
-            shape((8, WIDTH), f32),
+            shape((ROWS, WIDTH), f32),
+            shape((ROWS + 32, WIDTH), bf16),
+            shape((16, WIDTH), bf16),
         ],
         [pltpu.VMEM((ROWS + 8, WIDTH), f32)],
         (x, squares, gain, short, *fields),
@@ -267,13 +315,12 @@
     )
     near_in = shifted(halo, "ctx", 1, False)
     far_in = shifted(far, "ctx", 2, False)
-    stream, gated, ends, tail = call(
+    stream, gated, ends = call(
         second_kernel,
         [
             shape((ROWS, WIDTH), bf16),
             shape((ROWS, WIDTH), f32),
-            shape((CTX, 8, WIDTH), f32),
-            shape((16, WIDTH), f32),
+            shape((CTX, 16, WIDTH), bf16),
         ],
         [
             pltpu.VMEM((2 * ROWS, WIDTH), f32),
@@ -281,16 +328,15 @@
             pltpu.VMEM((8, 16, WIDTH), f32),
             pltpu.VMEM((16, WIDTH), f32),
         ],
-        (halo, near_in, far_in, head, stream, short, medium, rates, residues, direct, *fields),
+        (gated, near_in, far_in, head, stream, short, medium, rates, residues, direct, *fields),
         "second",
     )
-    tail_in = shifted(tail, "ctx", 1, False)
     ends = lax.all_to_all(ends, "ctx", 0, 0, tiled=True)
     (out,) = call(
         third_kernel,
         [shape((ROWS, WIDTH), bf16)],
         [pltpu.VMEM((ROWS, WIDTH), f32), pltpu.VMEM((ROWS + 8, WIDTH), f32)],
-        (gated, stream, ends, tail_in, short, rates, residues, direct, *fields),
+        (gated, stream, ends, near_in, short, rates, residues, direct, *fields),
         "third",
     )
     return out

time: 54.2 us -> 53.4 us (0.985)
  blocking collectives: 0 us -> 18.4 us
  starting transfers between devices: 32.9 us -> 20 us
  waiting for transfers between devices: 12.8 us -> 7.07 us
  local copies, waits for them, and re-layouts: 2.8 us -> 0.07 us
  Pallas kernels: 5.18 us -> 7.38 us
    all_to_all x0 -> x1, blocking collectives: none -> 18.4 us  [shards(): ends = lax.all_to_all(ends, 'ctx', 0, 0, tiled=True)]
    all_to_all x1 -> x0, starting transfers between devices: 9.4 us -> none  [shards(): ends = lax.all_to_all(ends, 'ctx', 0, 0, tiled=True)]
    all_to_all x1 -> x0, waiting for transfers between devices: 4.84 us -> none  [shards(): ends = lax.all_to_all(ends, 'ctx', 0, 0, tiled=True)]
    ppermute x6 -> x5, starting transfers between devices: 19.3 us -> 15.8 us  [shifted(): return lax.ppermute(value, axis, pairs)]
    unnamed x21 -> x17, local copies, waits for them, and re-layouts: 2.8 us -> 0.07 us
    pallas_call x4 -> x5, Pallas kernels: 5.18 us -> 7.38 us  [call(): pl.pallas_call(kernel, out_shape=outs, in_specs=[pl.BlockSpec(memory_spac...]
    ppermute x6 -> x5, waiting for transfers between devices: 1.63 us -> 0.79 us  [shifted(): return lax.ppermute(value, axis, pairs)]
  transfers between devices with their start and end apart: 8 -> 6, of which waited for: 4 -> 2; matrix products, arithmetic and copies ran while one was open for 0% -> 0% of each run, Pallas kernels for 0% -> 0%
where the time goes in v2:
time: 53.4 us; the launch traced here: 53.1 us
  starting transfers between devices  20 us (37%)
  blocking collectives  18.4 us (34%)
  Pallas kernels  7.38 us (14%)
  waiting for transfers between devices  7.07 us (13%)
    all_to_all x1, blocking collectives, shards(): ends = lax.all_to_all(ends, 'ctx', 0, 0, tiled=True)  18.4 us
    ppermute x5, starting transfers between devices, shifted(): return lax.ppermute(value, axis, pairs)  15.8 us
    pallas_call x5, Pallas kernels, call(): pl.pallas_call(kernel, out_shape=outs, in_specs=[pl.BlockSpec(memory_spac...  7.38 us
    all_to_all x1, waiting for transfers between devices, shards(): squares = lax.all_to_all(squares, ('sec', 'ch'), 0, 0, tiled=True)  6.29 us
    all_to_all x1, starting transfers between devices, shards(): squares = lax.all_to_all(squares, ('sec', 'ch'), 0, 0, tiled=True)  4.24 us
  transfers between devices with their start and end apart: 6, of which 2 were waited for; matrix products, arithmetic and copies ran while one was open for 0% of the time, Pallas kernels for 0%

profile of v2, /device:TPU:1, one launch (start us, length us, event | category | flops | bytes accessed | tf_op | source)
XLA Modules:
  0.0 53.1 jit_solution(11695041707381437313)
XLA Ops:
  0.0 1.6 %squares.1.after_ref = f32[16,128]{1,0:T(8,128)} custom-call(bf16[128,256]{1,0:T(8,128)(2,1)} %x_ref.1), custom_call_target="tpu_custom_call" | custom-call | flops 1000000 | bytes 1000000 | tf_op jit(solution)/shard_map/squares/pallas_call | solution.py:262
  1.6 0.0 copy-start.7
  1.6 0.0 copy-start.2
  1.6 0.0 copy-start.6
  1.6 0.0 copy-start.3
  1.6 0.0 copy-start.4
  1.6 2.0 %pack.1 = (bf16[2,128,256]{2,1,0:T(8,128)(2,1)}, bf16[2,128,256]{2,1,0:T(8,128)(2,1)}, bf16[2,128,256]{2,1,0:T(8,128)(2,1)}, bf16[2,128,256]{2,1,0:T(8,128)(2,1)}) custom-call(f32[16,128]{1,0:T(8,128)} %squares.1.after_ref, bf16[1,128,1024]{2,1,0:T(8,128)(2,1)} %q_hbm.1, bf16[1,128,1024]{2,1,0:T(8,128)(2,1)} %k_hbm.1), custom_call_target="tpu_custom_call" | custom-call | flops 99999997952 | bytes 1000000 | tf_op jit(solution)/shard_map/pack/pallas_call | solution.py:262
  3.6 0.0 copy-start
  3.6 0.0 copy-start.1
  3.6 2.2 %collective-permute-start = (bf16[2,128,256]{2,1,0:T(8,128)(2,1)}, bf16[2,128,256]{2,1,0:T(8,128)(2,1)S(1)}, u32[]{:S(2)}, u32[]{:S(2)}) collective-permute-start(bf16[2,128,256]{2,1,0:T(8,128)(2,1)} %get-tuple-element.18), channel_id=1, source_target_pairs={{0,64},{64,128},{128,192},{192,0},{1,65},{65,129},{129,193},{193,1... | collective-permute-start | bytes 393224 | tf_op jit(solution)/shard_map/ppermute | solution.py:26
  5.8 2.6 %collective-permute-start.1 = (bf16[2,128,256]{2,1,0:T(8,128)(2,1)}, bf16[2,128,256]{2,1,0:T(8,128)(2,1)S(1)}, u32[]{:S(2)}, u32[]{:S(2)}) collective-permute-start(bf16[2,128,256]{2,1,0:T(8,128)(2,1)} %get-tuple-element.19), channel_id=1, source_target_pairs={{0,128},{64,192},{128,0},{192,64},{1,129},{65,193},{129,1},{193,65... | collective-permute-start | bytes 393224 | tf_op jit(solution)/shard_map/ppermute | solution.py:26
  8.5 1.1 %collective-permute-start.2 = (bf16[2,128,256]{2,1,0:T(8,128)(2,1)}, bf16[2,128,256]{2,1,0:T(8,128)(2,1)S(1)}, u32[]{:S(2)}, u32[]{:S(2)}) collective-permute-start(bf16[2,128,256]{2,1,0:T(8,128)(2,1)} %get-tuple-element.20), channel_id=1, source_target_pairs={{0,192},{64,0},{128,64},{192,128},{1,193},{65,1},{129,65},{193,129... | collective-permute-start | bytes 393224 | tf_op jit(solution)/shard_map/ppermute | solution.py:26
  9.5 4.2 %all-to-all-start = ((f32[16,1,128]{2,1,0:T(1,128)}), f32[16,1,128]{2,1,0:T(1,128)S(1)}, u32[]{:S(2)}, u32[]{:S(2)}) async-start(f32[16,1,128]{2,1,0:T(1,128)} %bitcast.1), calls=%async_computation | async-start | bytes 16384 | tf_op jit(solution)/shard_map/all_to_all | solution.py:302
  13.8 0.0 copy-done.7
  13.8 6.3 %all-to-all-done = f32[16,1,128]{2,1,0:T(1,128)S(1)} async-done(((f32[16,1,128]{2,1,0:T(1,128)}), f32[16,1,128]{2,1,0:T(1,128)S(1)}, u32[]{:S(2)}, u32[]{:S(2)}) %all-to-all-start) | async-done | bytes 8224 | tf_op jit(solution)/shard_map/all_to_all | solution.py:302
  20.1 0.0 collective-permute-done.f1
  20.1 0.0 collective-permute-done.1.f2
  20.1 0.0 collective-permute-done.2.f3
  20.1 0.0 copy-done.2
  20.1 0.0 copy-done.6
  20.1 0.0 copy-done
  20.1 0.3 first.1
  20.5 6.4 %collective-permute-start.3 = (bf16[160,256]{1,0:T(8,128)(2,1)S(1)}, bf16[160,256]{1,0:T(8,128)(2,1)S(1)}, u32[]{:S(2)}, u32[]{:S(2)}) collective-permute-start(bf16[160,256]{1,0:T(8,128)(2,1)S(1)} %get-tuple-element.22), channel_id=1, source_target_pairs={{0,4},{4,8},{8,12},{12,16},{16,20},{20,24},{24,28},{28,32},{32,36}... | collective-permute-start | bytes 245768 | tf_op jit(solution)/shard_map/ppermute | solution.py:26
  26.9 0.0 copy-start.5
  26.9 3.5 %collective-permute-start.4 = (bf16[16,256]{1,0:T(8,128)(2,1)S(1)}, bf16[16,256]{1,0:T(8,128)(2,1)S(1)}, u32[]{:S(2)}, u32[]{:S(2)}) collective-permute-start(bf16[16,256]{1,0:T(8,128)(2,1)S(1)} %get-tuple-element.23), channel_id=1, source_target_pairs={{0,8},{4,12},{8,16},{12,20},{16,24},{20,28},{24,32},{28,36},{32,40... | collective-permute-start | bytes 24584 | tf_op jit(solution)/shard_map/ppermute | solution.py:26
  30.4 0.8 %collective-permute-done.4.far_ref = bf16[16,256]{1,0:T(8,128)(2,1)S(1)} collective-permute-done((bf16[16,256]{1,0:T(8,128)(2,1)S(1)}, bf16[16,256]{1,0:T(8,128)(2,1)S(1)}, u32[]{:S(2)}, u32[]{:S(2)}) %collective-permute-start.4) | collective-permute-done | bytes 8224 | tf_op jit(solution)/shard_map/ppermute | solution.py:26
  31.2 0.0 collective-permute-done.3.near_ref
  31.2 0.0 copy-done.3
  31.2 0.0 copy-done.4
  31.2 0.0 copy-done.1
  31.2 0.0 copy-done.5
  31.2 2.0 %second.1 = (bf16[128,256]{1,0:T(8,128)(2,1)S(1)}, f32[128,256]{1,0:T(8,128)S(1)}, bf16[16,16,256]{2,1,0:T(8,128)(2,1)S(1)}) custom-call(f32[128,256]{1,0:T(8,128)S(1)} %get-tuple-element.21.own_ref, bf16[160,256]{1,0:T(8,128)(2,1)S(1)} %collective-permute-done.3.near_ref, bf16[16,256]{1,0:T(8,128)(2,1)S(1)} %collective-permute-done.4.far_ref, ...), custom_call_target="tpu_custom_call" | custom-call | flops 1000000 | bytes 1000000 | tf_op jit(solution)/shard_map/second/pallas_call | solution.py:262
  33.2 18.4 %all_to_all.16.ends_ref = bf16[16,16,256]{2,1,0:T(8,128)(2,1)S(1)} all-to-all(bf16[16,16,256]{2,1,0:T(8,128)(2,1)S(1)} %get-tuple-element.28), channel_id=1, replica_groups=mesh['sec'=4,'ctx'=16,'ch'=4] {'ctx'}, dimensions={0} | all-to-all | bytes 262144 | tf_op jit(solution)/shard_map/all_to_all | solution.py:334
  51.6 1.5 %third.1 = bf16[128,256]{1,0:T(8,128)(2,1)} custom-call(f32[128,256]{1,0:T(8,128)S(1)} %get-tuple-element.26.gated_ref, bf16[128,256]{1,0:T(8,128)(2,1)S(1)} %get-tuple-element.27.stream_ref, bf16[16,16,256]{2,1,0:T(8,128)(2,1)S(1)} %all_to_all.16.ends_ref, bf16[160,256]{1,0:T(8,128)(2,1)S(1)} %collective-permute-done.3.near_ref, ...), custom_call_target="tpu_custom_call" | custom-call | flops 1000000 | bytes 1000000 | tf_op jit(solution)/shard_map/third/pallas_call | solution.py:262
  (1 shorter events, 0.0 us)
Async XLA Ops:
  1.6 12.2 %copy-start.7 = (f32[2,7,1024]{2,0,1:T(2,128)S(1)}, f32[2,7,1024]{2,0,1:T(2,128)}, u32[]{:S(2)}) copy-start(f32[2,7,1024]{2,0,1:T(2,128)} %param.13) | copy-start | bytes 172036
  1.6 18.5 %copy-start.2 = (bf16[128,256]{1,0:T(8,128)(2,1)S(1)}, bf16[128,256]{1,0:T(8,128)(2,1)}, u32[]{:S(2)}) copy-start(bf16[128,256]{1,0:T(8,128)(2,1)} %x_ref.1) | copy-start | bytes 196612
  1.6 18.5 %copy-start.6 = (f32[1024]{0:T(1024)S(1)}, f32[1024]{0:T(1024)}, u32[]{:S(2)}) copy-start(f32[1024]{0:T(1024)} %param.12) | copy-start | bytes 12292
  1.6 29.6 %copy-start.3 = (f32[8,1024]{1,0:T(8,128)S(1)}, f32[8,1024]{1,0:T(8,128)}, u32[]{:S(2)}) copy-start(f32[8,1024]{1,0:T(8,128)} %rates_ref.3) | copy-start | bytes 98308
  1.6 29.6 %copy-start.4 = (f32[8,1024]{1,0:T(8,128)S(1)}, f32[8,1024]{1,0:T(8,128)}, u32[]{:S(2)}) copy-start(f32[8,1024]{1,0:T(8,128)} %residues_ref.3) | copy-start | bytes 98308
  3.6 16.5 %copy-start = (bf16[2,128,256]{2,1,0:T(8,128)(2,1)S(1)}, bf16[2,128,256]{2,1,0:T(8,128)(2,1)}, u32[]{:S(2)}) copy-start(bf16[2,128,256]{2,1,0:T(8,128)(2,1)} %get-tuple-element.17.f0) | copy-start | bytes 393220
  3.6 27.6 %copy-start.1 = (f32[128,1024]{1,0:T(8,128)S(1)}, f32[128,1024]{1,0:T(8,128)}, u32[]{:S(2)}) copy-start(f32[128,1024]{1,0:T(8,128)} %medium_ref.1) | copy-start | bytes 1572868
  3.6 16.5 %collective-permute-start = (bf16[2,128,256]{2,1,0:T(8,128)(2,1)}, bf16[2,128,256]{2,1,0:T(8,128)(2,1)S(1)}, u32[]{:S(2)}, u32[]{:S(2)}) collective-permute-start(bf16[2,128,256]{2,1,0:T(8,128)(2,1)} %get-tuple-element.18), channel_id=1, source_target_pairs={{0,64},{64,128},{128,192},{192,0},{1,65},{65,129},{129,193},{193,1... | collective-permute-start | bytes 393224 | tf_op jit(solution)/shard_map/ppermute | solution.py:26
  5.8 14.3 %collective-permute-start.1 = (bf16[2,128,256]{2,1,0:T(8,128)(2,1)}, bf16[2,128,256]{2,1,0:T(8,128)(2,1)S(1)}, u32[]{:S(2)}, u32[]{:S(2)}) collective-permute-start(bf16[2,128,256]{2,1,0:T(8,128)(2,1)} %get-tuple-element.19), channel_id=1, source_target_pairs={{0,128},{64,192},{128,0},{192,64},{1,129},{65,193},{129,1},{193,65... | collective-permute-start | bytes 393224 | tf_op jit(solution)/shard_map/ppermute | solution.py:26
  8.5 11.7 %collective-permute-start.2 = (bf16[2,128,256]{2,1,0:T(8,128)(2,1)}, bf16[2,128,256]{2,1,0:T(8,128)(2,1)S(1)}, u32[]{:S(2)}, u32[]{:S(2)}) collective-permute-start(bf16[2,128,256]{2,1,0:T(8,128)(2,1)} %get-tuple-element.20), channel_id=1, source_target_pairs={{0,192},{64,0},{128,64},{192,128},{1,193},{65,1},{129,65},{193,129... | collective-permute-start | bytes 393224 | tf_op jit(solution)/shard_map/ppermute | solution.py:26
  9.5 10.6 %all-to-all-start = ((f32[16,1,128]{2,1,0:T(1,128)}), f32[16,1,128]{2,1,0:T(1,128)S(1)}, u32[]{:S(2)}, u32[]{:S(2)}) async-start(f32[16,1,128]{2,1,0:T(1,128)} %bitcast.1), calls=%async_computation | async-start | bytes 16384 | tf_op jit(solution)/shard_map/all_to_all | solution.py:302
  20.5 10.7 %collective-permute-start.3 = (bf16[160,256]{1,0:T(8,128)(2,1)S(1)}, bf16[160,256]{1,0:T(8,128)(2,1)S(1)}, u32[]{:S(2)}, u32[]{:S(2)}) collective-permute-start(bf16[160,256]{1,0:T(8,128)(2,1)S(1)} %get-tuple-element.22), channel_id=1, source_target_pairs={{0,4},{4,8},{8,12},{12,16},{16,20},{20,24},{24,28},{28,32},{32,36}... | collective-permute-start | bytes 245768 | tf_op jit(solution)/shard_map/ppermute | solution.py:26
  26.9 4.4 %copy-start.5 = (f32[1024]{0:T(1024)S(1)}, f32[1024]{0:T(1024)}, u32[]{:S(2)}) copy-start(f32[1024]{0:T(1024)} %param.17) | copy-start | bytes 12292
  26.9 4.3 %collective-permute-start.4 = (bf16[16,256]{1,0:T(8,128)(2,1)S(1)}, bf16[16,256]{1,0:T(8,128)(2,1)S(1)}, u32[]{:S(2)}, u32[]{:S(2)}) collective-permute-start(bf16[16,256]{1,0:T(8,128)(2,1)S(1)} %get-tuple-element.23), channel_id=1, source_target_pairs={{0,8},{4,12},{8,16},{12,20},{16,24},{20,28},{24,32},{28,36},{32,40... | collective-permute-start | bytes 24584 | tf_op jit(solution)/shard_map/ppermute | solution.py:26

commit v3 on v2

v3 whole, which is shorter than its diff:
```python
import jax
import jax.numpy as jnp
from jax import lax
from jax.experimental import pallas as pl
from jax.experimental.pallas import tpu as pltpu
from jax.sharding import PartitionSpec as P

D = 4096
EPS = 1e-06
ROWS = 128
WIDTH = 256
SEC = 4
CTX = 16
PEERS = 16
f32 = jnp.float32
bf16 = jnp.bfloat16


def shifted(value, axis, steps, wrap):
    count = lax.axis_size(axis)
    pairs = [
        (source, (source + steps) % count)
        for source in range(count)
        if wrap or 0 <= source + steps < count
    ]
    return lax.ppermute(value, axis, pairs)


def lanes_of(position):
    return pl.ds(pl.multiple_of(position * WIDTH, WIDTH), WIDTH)


def pack_kernel(x_hbm, q_hbm, k_hbm, squares_ref, own_ref, send_1, send_2, send_3, x_ref, sems):
    sec = lax.axis_index("sec")
    first = pltpu.make_async_copy(x_hbm, x_ref, sems.at[8])
    first.start()
    loads = []
    for distance, ref in enumerate((own_ref, send_1, send_2, send_3)):
        lanes = lanes_of(lax.rem(sec + distance, SEC))
        for which, source in enumerate((q_hbm, k_hbm)):
            loads.append(
                pltpu.make_async_copy(
                    source.at[0, :, lanes], ref.at[which], sems.at[2 * distance + which]
                )
            )
    for load in loads:
        load.start()
    first.wait()
    x = x_ref[...].astype(f32)
    squared = x * x
    folded = squared[:, :128] + squared[:, 128:]
    squares = jnp.sum(folded.T, axis=0, keepdims=True)
    squares_ref[...] = jnp.broadcast_to(squares, squares_ref.shape)
    for load in loads:
        load.wait()


def field_of(refs, section, which, rows=None):
    distance = lax.rem(lax.axis_index("sec") - section + SEC, SEC)

    def read(ref):
        part = ref[which] if rows is None else ref[which, rows]
        return part.astype(f32)

    chosen = read(refs[0])
    for index in range(1, SEC):
        chosen = jnp.where(distance == index, read(refs[index]), chosen)
    return chosen


def short_sum(padded_ref, taps):
    total = taps[0:1] * padded_ref[8 : 8 + ROWS]
    for tap in range(1, 7):
        total += taps[tap : tap + 1] * padded_ref[8 - tap : 8 - tap + ROWS]
    return total


def entry_kernel(x_ref, squares_ref, gain_ref, stream_ref):
    lanes = lanes_of(lax.axis_index("sec"))
    sums = jnp.sum(squares_ref[...], axis=0, keepdims=True)
    inverse = lax.rsqrt(jnp.broadcast_to(sums, (128, 128)).T / D + EPS)
    inverse = jnp.concatenate([inverse, inverse], axis=1)
    stream_ref[...] = (x_ref[...].astype(f32) * inverse * gain_ref[:, lanes]).astype(bf16)


def first_kernel(
    entry_ref, taps_ref, f0, f1, f2, f3,
    head_ref, stream_ref, own_ref, halo_ref, far_ref, pad_ref,
):
    fields = (f0, f1, f2, f3)
    lanes = lanes_of(lax.axis_index("sec"))
    stream = entry_ref[...].astype(f32)
    gated = field_of(fields, 0, 1) * stream
    pad_ref[0:8] = jnp.zeros((8, WIDTH), f32)
    pad_ref[8:] = gated
    filtered = short_sum(pad_ref, taps_ref[0, :, lanes])
    q0 = field_of(fields, 0, 0)
    k1 = field_of(fields, 1, 1)
    raw = stream + q0 * filtered
    head_ref[...] = raw[0:8]
    rounded = raw.astype(bf16)
    stream_ref[...] = rounded
    rounded = rounded.astype(f32)
    gated_1 = jnp.concatenate([k1[0:8] * raw[0:8], k1[8:] * rounded[8:]], axis=0)
    own_ref[...] = gated_1
    halo_ref[0:ROWS] = gated_1.astype(bf16)
    last = gated[ROWS - 8 :]
    gates = k1[0:8] * q0[0:8]
    halo_ref[ROWS : ROWS + 16] = jnp.concatenate([last, gates], axis=0).astype(bf16)
    last_rows = pl.ds(ROWS - 16, 16)
    halo_ref[ROWS + 16 :] = (
        field_of(fields, 2, 0, last_rows) * field_of(fields, 3, 1, last_rows)
    ).astype(bf16)
    far_ref[...] = jnp.concatenate([last, last], axis=0).astype(bf16)


def medium_part(source_ref, taps_ref, partial_ref, low, sources, earlier_ref=None):
    first, last = sources

    def step(index, carry):
        shift = lax.rem(index, 8)
        here = pl.ds(pl.multiple_of((index // 8) * 128, 128), 128)
        taps = [jnp.broadcast_to(taps_ref[shift, a : a + 1, here], (8, 128)) for a in range(16)]
        for group in range(low, 16):
            total = None
            if earlier_ref is not None and group >= 1:
                total = earlier_ref[shift, 8 * group - 8 : 8 * group, here]
            for a in range(16):
                origin = group - a
                if origin < first or origin > last:
                    continue
                start = 8 * (origin - first)
                term = taps[a] * source_ref[start : start + 8, here]
                total = term if total is None else total + term
            start = 8 * (group - low)
            partial_ref[shift, start : start + 8, here] = total
        return carry

    lax.fori_loop(0, 16, step, 0)


def own_kernel(
    gated_ref, medium_ref, rates_ref, residues_ref, partial_ref, taps_ref, powers_ref, carry_ref, kernel_ref
):
    lanes = lanes_of(lax.axis_index("sec"))
    medium_taps = medium_ref[:, lanes].reshape(16, 8, WIDTH)
    for shift in range(8):
        taps_ref[shift] = medium_taps[:, shift]
    medium_part(gated_ref.at[pl.ds(8, ROWS - 8)], taps_ref, partial_ref, 1, (1, 15))
    rates = rates_ref[:, lanes]
    weights = residues_ref[:, lanes] * jnp.sqrt(jnp.tanh(rates) * (1.0 + jnp.exp(-2.0 * rates)))
    position = lax.broadcasted_iota(jnp.int32, (8, WIDTH), 0)
    carries = []
    for age in range(9):
        power = jnp.exp(-rates * age)
        powers_ref[age] = power
        if age < 8:
            row = jnp.sum(weights * power, axis=0, keepdims=True)
            kernel_ref[age] = jnp.where(position >= age, row, 0.0)
        if age > 0:
            carries.append(weights * power)
    carries = jnp.stack(carries, axis=0)
    for mode in range(8):
        carry_ref[mode] = carries[:, mode]


def carried_rows(carry_ref, state):
    total = carry_ref[0] * state[0:1]
    for mode in range(1, 8):
        total += carry_ref[mode] * state[mode : mode + 1]
    return total


def within_rows(kernel_ref, rows, padded_ref):
    count = rows.shape[0]
    grouped = (count // 8, 8, WIDTH)
    total = rows.reshape(grouped) * kernel_ref[0][None]
    for age in range(1, 8):
        total += padded_ref[8 - age : 8 - age + count].reshape(grouped) * kernel_ref[age][None]
    return total.reshape(count, WIDTH)


def second_kernel(
    near_ref, far_ref, head_ref, stream_ref, short_ref,
    partial_ref, taps_ref, powers_ref, carry_ref, kernel_ref, direct_ref, f0, f1, f2, f3,
    next_ref, gated_ref, steps_ref, ends_ref, tail_ref,
    source_ref, sums_ref, pad_ref,
):
    fields = (f0, f1, f2, f3)
    lanes = lanes_of(lax.axis_index("sec"))
    taps = short_ref[0, :, lanes]

    def correction(before):
        pad_ref[0:8] = before
        pad_ref[8:16] = jnp.zeros((8, WIDTH), f32)
        total = jnp.zeros((8, WIDTH), f32)
        for tap in range(1, 7):
            total += taps[tap : tap + 1] * pad_ref[8 - tap : 16 - tap]
        return total

    head_q0 = field_of(fields, 0, 0, pl.ds(0, 16))[0:8]
    head_k1 = field_of(fields, 1, 1, pl.ds(0, 16))[0:8]
    joints = near_ref[ROWS : ROWS + 16].astype(f32)
    mine = (head_ref[...] + head_q0 * correction(joints[0:8])).astype(bf16).astype(f32)
    near = near_ref[0:ROWS].astype(f32)
    far = far_ref[...].astype(f32)
    source_ref[0:8] = near[0:8] + joints[8:16] * correction(far[0:8])
    source_ref[8:ROWS] = near[8:]
    source_ref[ROWS:] = head_k1 * mine
    medium_part(source_ref, taps_ref, sums_ref, -1, (-16, 0), partial_ref)
    filtered = sums_ref[0, 8 : 8 + ROWS]
    for shift in range(1, 8):
        filtered += sums_ref[shift, 8 - shift : 8 - shift + ROWS]
    stream = jnp.concatenate([mine, stream_ref[...].astype(f32)[8:]], axis=0)
    stream = (stream + field_of(fields, 1, 0) * filtered).astype(bf16)
    next_ref[...] = stream
    stream = stream.astype(f32)
    gated = field_of(fields, 2, 1) * stream
    gated_ref[...] = gated
    powers = [powers_ref[age] for age in range(9)]
    state = jnp.zeros((8, WIDTH), f32)
    before_last = state
    for group in range(16):
        step = powers[7] * gated[8 * group : 8 * group + 1]
        for row in range(1, 8):
            step += powers[7 - row] * gated[8 * group + row : 8 * group + row + 1]
        steps_ref[group] = step
        before_last = state
        state = powers[8] * state + step
    sent = jnp.concatenate([state[:, :128], state[:, 128:]], axis=0).astype(bf16)
    ends_ref[...] = jnp.broadcast_to(sent[None], ends_ref.shape)
    last = gated[ROWS - 8 :]
    pad_ref[8:16] = last
    sums = within_rows(kernel_ref, last, pad_ref) + carried_rows(carry_ref, before_last)
    q2 = field_of(fields, 2, 0, pl.ds(ROWS - 16, 16))[8:]
    k3 = field_of(fields, 3, 1, pl.ds(ROWS - 16, 16))[8:]
    tail_ref[...] = k3 * (stream[ROWS - 8 :] + q2 * (sums + direct_ref[:, lanes] * last))


def within_kernel(gated_ref, kernel_ref, direct_ref, local_ref, pad_ref):
    lanes = lanes_of(lax.axis_index("sec"))
    gated = gated_ref[...]
    pad_ref[0:8] = jnp.zeros((8, WIDTH), f32)
    pad_ref[8:] = gated
    local_ref[...] = within_rows(kernel_ref, gated, pad_ref) + direct_ref[:, lanes] * gated


def third_kernel(
    local_ref, steps_ref, stream_ref, ends_ref, tail_ref, near_ref, short_ref,
    rates_ref, powers_ref, carry_ref, f0, f1, f2, f3,
    out_ref, sums_ref, pad_ref,
):
    fields = (f0, f1, f2, f3)
    lanes = lanes_of(lax.axis_index("sec"))
    mine = lax.axis_index("ctx")
    rates = rates_ref[:, lanes]
    span = jnp.exp(-rates * ROWS)
    state = jnp.zeros((8, WIDTH), f32)
    previous = state
    for position in range(CTX - 1):
        received = ends_ref[position].astype(f32)
        longer = span * state + jnp.concatenate([received[0:8], received[8:16]], axis=1)
        previous = jnp.where(position < mine - 1, longer, previous)
        state = jnp.where(position < mine, longer, state)
    carried = carried_rows(carry_ref, jnp.exp(-rates * (ROWS - 8)) * previous)
    gates = near_ref[ROWS + 16 :].astype(f32)[8:]
    pad_ref[0:8] = tail_ref[...] + gates * carried
    for group in range(16):
        rows = slice(8 * group, 8 * group + 8)
        sums_ref[rows] = local_ref[rows] + carried_rows(carry_ref, state)
        state = powers_ref[8] * state + steps_ref[group]
    stream = stream_ref[...].astype(f32) + field_of(fields, 2, 0) * sums_ref[...]
    stream = stream.astype(bf16).astype(f32)
    pad_ref[8:] = field_of(fields, 3, 1) * stream
    filtered = short_sum(pad_ref, short_ref[1, :, lanes])
    out_ref[...] = (stream + field_of(fields, 3, 0) * filtered).astype(bf16)


def shape(dims, dtype):
    return jax.ShapeDtypeStruct(dims, dtype)


def call(kernel, outs, scratch, operands, name, in_hbm=(), flops=1000000, room=32):
    vmem = pl.BlockSpec(memory_space=pltpu.VMEM)
    return pl.pallas_call(
        kernel,
        out_shape=outs,
        in_specs=[
            pl.BlockSpec(memory_space=pltpu.HBM) if index in in_hbm else vmem
            for index in range(len(operands))
        ],
        out_specs=[vmem] * len(outs),
        scratch_shapes=scratch,
        compiler_params=pltpu.CompilerParams(vmem_limit_bytes=room * 1024 * 1024),
        cost_estimate=pl.CostEstimate(flops=flops, bytes_accessed=1000000, transcendentals=0),
        name=name,
    )(*operands)


def shards(x, q, k, gain, short, medium, rates, residues, direct):
    gain, direct = gain[None], direct[None]
    pair = shape((2, ROWS, WIDTH), bf16)
    squares, own, *sends = call(
        pack_kernel,
        [shape((PEERS, 128), f32)] + [pair] * 4,
        [pltpu.VMEM((ROWS, WIDTH), bf16), pltpu.SemaphoreType.DMA((9,))],
        (x, q, k),
        "pack",
        in_hbm=(0, 1, 2),
        room=60,
    )
    fields = [own] + [
        shifted(part, "sec", distance + 1, True) for distance, part in enumerate(sends)
    ]
    squares = lax.all_to_all(squares, ("sec", "ch"), 0, 0, tiled=True)
    (entry,) = call(
        entry_kernel, [shape((ROWS, WIDTH), bf16)], [], (x, squares, gain), "entry", flops=10**11
    )
    head, stream, gated, halo, far = call(
        first_kernel,
        [
            shape((8, WIDTH), f32),
            shape((ROWS, WIDTH), bf16),
            shape((ROWS, WIDTH), f32),
            shape((ROWS + 32, WIDTH), bf16),
            shape((16, WIDTH), bf16),
        ],
        [pltpu.VMEM((ROWS + 8, WIDTH), f32)],
        (entry, short, *fields),
        "first",
    )
    near_in = shifted(halo, "ctx", 1, False)
    far_in = shifted(far, "ctx", 2, False)
    table = shape((8, 8, WIDTH), f32)
    partial, taps, powers, carry, kernel = call(
        own_kernel,
        [
            shape((8, ROWS - 8, WIDTH), f32),
            shape((8, 16, WIDTH), f32),
            shape((9, 8, WIDTH), f32),
            table,
            table,
        ],
        [],
        (gated, medium, rates, residues),
        "own",
        flops=10**9,
    )
    stream, gated, steps, ends, tail = call(
        second_kernel,
        [
            shape((ROWS, WIDTH), bf16),
            shape((ROWS, WIDTH), f32),
            shape((16, 8, WIDTH), f32),
            shape((CTX, 16, 128), bf16),
            shape((8, WIDTH), f32),
        ],
        [
            pltpu.VMEM((ROWS + 8, WIDTH), f32),
            pltpu.VMEM((8, ROWS + 8, WIDTH), f32),
            pltpu.VMEM((16, WIDTH), f32),
        ],
        (near_in, far_in, head, stream, short, partial, taps, powers, carry, kernel, direct, *fields),
        "second",
    )
    tail_in = shifted(tail, "ctx", 1, False)
    ends = lax.all_to_all(ends, "ctx", 0, 0, tiled=True)
    (local,) = call(
        within_kernel,
        [shape((ROWS, WIDTH), f32)],
        [pltpu.VMEM((ROWS + 8, WIDTH), f32)],
        (gated, kernel, direct),
        "within",
        flops=10**9,
    )
    (out,) = call(
        third_kernel,
        [shape((ROWS, WIDTH), bf16)],
        [pltpu.VMEM((ROWS, WIDTH), f32), pltpu.VMEM((ROWS + 8, WIDTH), f32)],
        (local, steps, stream, ends, tail_in, near_in, short, rates, powers, carry, *fields),
        "third",
    )
    return out


def solution(mesh):
    in_specs = (
        P("ctx", ("ch", "sec")),
        P("sec", "ctx", "ch"),
        P("sec", "ctx", "ch"),
        P("ch"),
        P(None, None, "ch"),
        P(None, "ch"),
        P(None, "ch"),
        P(None, "ch"),
        P("ch"),
    )
    out_specs = P("ctx", ("ch", "sec"))
    return jax.shard_map(shards, mesh=mesh, in_specs=in_specs, out_specs=out_specs, check_vma=False)
```

time: 53.4 us -> 51.5 us (0.964)
  blocking collectives: 18.4 us -> 0 us
  starting transfers between devices: 20 us -> 34.9 us
  waiting for transfers between devices: 7.07 us -> 8.99 us
  Pallas kernels: 7.38 us -> 6.32 us
  local copies, waits for them, and re-layouts: 0.07 us -> 0.74 us
    all_to_all x1 -> x0, blocking collectives: 18.4 us -> none  [shards(): ends = lax.all_to_all(ends, 'ctx', 0, 0, tiled=True)]
    all_to_all x0 -> x1, starting transfers between devices: none -> 9.65 us  [shards(): ends = lax.all_to_all(ends, 'ctx', 0, 0, tiled=True)]
    all_to_all x1, waiting for transfers between devices: 6.29 us -> 1.28 us  [shards(): squares = lax.all_to_all(squares, ('sec', 'ch'), 0, 0, tiled=True)]
    all_to_all x0 -> x1, waiting for transfers between devices: none -> 3.5 us  [shards(): ends = lax.all_to_all(ends, 'ctx', 0, 0, tiled=True)]
    ppermute x5 -> x6, waiting for transfers between devices: 0.79 us -> 4.22 us  [shifted(): return lax.ppermute(value, axis, pairs)]
    all_to_all x1, starting transfers between devices: 4.24 us -> 7.6 us  [shards(): squares = lax.all_to_all(squares, ('sec', 'ch'), 0, 0, tiled=True)]
    ppermute x5 -> x6, starting transfers between devices: 15.8 us -> 17.6 us  [shifted(): return lax.ppermute(value, axis, pairs)]
    pallas_call x5 -> x7, Pallas kernels: 7.38 us -> 6.32 us  [call(): pl.pallas_call(kernel, out_shape=outs, in_specs=[pl.BlockSpec(memory_spac...]
  transfers between devices with their start and end apart: 6 -> 8, of which waited for: 2 -> 6; matrix products, arithmetic and copies ran while one was open for 0% -> 0% of each run, Pallas kernels for 0% -> 2%
where the time goes in v3:
time: 51.5 us; the launch traced here: 51.1 us
  starting transfers between devices  34.9 us (68%)
  waiting for transfers between devices  8.99 us (17%)
  Pallas kernels  6.32 us (12%)
  local copies, waits for them, and re-layouts  0.74 us (1%)
    ppermute x6, starting transfers between devices, shifted(): return lax.ppermute(value, axis, pairs)  17.6 us
    all_to_all x1, starting transfers between devices, shards(): ends = lax.all_to_all(ends, 'ctx', 0, 0, tiled=True)  9.65 us
    all_to_all x1, starting transfers between devices, shards(): squares = lax.all_to_all(squares, ('sec', 'ch'), 0, 0, tiled=True)  7.6 us
    pallas_call x7, Pallas kernels, call(): pl.pallas_call(kernel, out_shape=outs, in_specs=[pl.BlockSpec(memory_spac...  6.32 us
    ppermute x6, waiting for transfers between devices, shifted(): return lax.ppermute(value, axis, pairs)  4.22 us
    all_to_all x1, waiting for transfers between devices, shards(): ends = lax.all_to_all(ends, 'ctx', 0, 0, tiled=True)  3.5 us
    all_to_all x1, waiting for transfers between devices, shards(): squares = lax.all_to_all(squares, ('sec', 'ch'), 0, 0, tiled=True)  1.28 us
  transfers between devices with their start and end apart: 8, of which 6 were waited for; matrix products, arithmetic and copies ran while one was open for 0% of the time, Pallas kernels for 2%

profile of v3, /device:TPU:1, one launch (start us, length us, event | category | flops | bytes accessed | tf_op | source)
XLA Modules:
  0.0 51.1 jit_solution(11544883593697291634)
XLA Ops:
  0.0 0.0 copy-start.7
  0.0 2.0 %pack.1 = (f32[16,128]{1,0:T(8,128)}, bf16[2,128,256]{2,1,0:T(8,128)(2,1)}, bf16[2,128,256]{2,1,0:T(8,128)(2,1)}, bf16[2,128,256]{2,1,0:T(8,128)(2,1)}, bf16[2,128,256]{2,1,0:T(8,128)(2,1)}) custom-call(bf16[128,256]{1,0:T(8,128)(2,1)} %x_ref.1, bf16[1,128,1024]{2,1,0:T(8,128)(2,1)} %q_hbm.1, bf16[1,128,1024]{2,1,0:T(8,128)(2,1)} %k_hbm.1), custom_call_target="tpu_custom_call" | custom-call | flops 1000000 | bytes 1000000 | tf_op jit(solution)/shard_map/pack/pallas_call | solution.py:285
  2.0 7.6 %all-to-all-start = ((f32[16,1,128]{2,1,0:T(1,128)}), f32[16,1,128]{2,1,0:T(1,128)S(1)}, u32[]{:S(2)}, u32[]{:S(2)}) async-start(f32[16,1,128]{2,1,0:T(1,128)} %bitcast.10), calls=%async_computation | async-start | bytes 16384 | tf_op jit(solution)/shard_map/all_to_all | solution.py:315
  9.6 0.0 copy-start.1
  9.6 1.4 %collective-permute-start = (bf16[2,128,256]{2,1,0:T(8,128)(2,1)}, bf16[2,128,256]{2,1,0:T(8,128)(2,1)S(1)}, u32[]{:S(2)}, u32[]{:S(2)}) collective-permute-start(bf16[2,128,256]{2,1,0:T(8,128)(2,1)} %get-tuple-element.27), channel_id=1, source_target_pairs={{0,64},{64,128},{128,192},{192,0},{1,65},{65,129},{129,193},{193,1... | collective-permute-start | bytes 393224 | tf_op jit(solution)/shard_map/ppermute | solution.py:26
  11.0 2.4 %collective-permute-start.1 = (bf16[2,128,256]{2,1,0:T(8,128)(2,1)}, bf16[2,128,256]{2,1,0:T(8,128)(2,1)S(1)}, u32[]{:S(2)}, u32[]{:S(2)}) collective-permute-start(bf16[2,128,256]{2,1,0:T(8,128)(2,1)} %get-tuple-element.28), channel_id=1, source_target_pairs={{0,128},{64,192},{128,0},{192,64},{1,129},{65,193},{129,1},{193,65... | collective-permute-start | bytes 393224 | tf_op jit(solution)/shard_map/ppermute | solution.py:26
  13.4 0.0 copy-start.6
  13.4 1.2 %collective-permute-start.2 = (bf16[2,128,256]{2,1,0:T(8,128)(2,1)}, bf16[2,128,256]{2,1,0:T(8,128)(2,1)S(1)}, u32[]{:S(2)}, u32[]{:S(2)}) collective-permute-start(bf16[2,128,256]{2,1,0:T(8,128)(2,1)} %get-tuple-element.29), channel_id=1, source_target_pairs={{0,192},{64,0},{128,64},{192,128},{1,193},{65,1},{129,65},{193,129... | collective-permute-start | bytes 393224 | tf_op jit(solution)/shard_map/ppermute | solution.py:26
  14.6 0.0 copy-done.7
  14.6 1.3 %all-to-all-done = f32[16,1,128]{2,1,0:T(1,128)S(1)} async-done(((f32[16,1,128]{2,1,0:T(1,128)}), f32[16,1,128]{2,1,0:T(1,128)S(1)}, u32[]{:S(2)}, u32[]{:S(2)}) %all-to-all-start) | async-done | bytes 8224 | tf_op jit(solution)/shard_map/all_to_all | solution.py:315
  15.9 0.0 copy-done.1
  15.9 0.0 copy-done.6
  15.9 0.0 copy-start
  15.9 0.1 entry.1.entry_ref
  16.0 0.0 copy-start.4
  16.1 0.0 collective-permute-done.f1
  16.1 2.5 %collective-permute-done.1.f2 = bf16[2,128,256]{2,1,0:T(8,128)(2,1)S(1)} collective-permute-done((bf16[2,128,256]{2,1,0:T(8,128)(2,1)}, bf16[2,128,256]{2,1,0:T(8,128)(2,1)S(1)}, u32[]{:S(2)}, u32[]{:S(2)}) %collective-permute-start.1) | collective-permute-done | bytes 131104 | tf_op jit(solution)/shard_map/ppermute | solution.py:26
  18.5 0.6 %collective-permute-done.2.f3 = bf16[2,128,256]{2,1,0:T(8,128)(2,1)S(1)} collective-permute-done((bf16[2,128,256]{2,1,0:T(8,128)(2,1)}, bf16[2,128,256]{2,1,0:T(8,128)(2,1)S(1)}, u32[]{:S(2)}, u32[]{:S(2)}) %collective-permute-start.2) | collective-permute-done | bytes 131104 | tf_op jit(solution)/shard_map/ppermute | solution.py:26
  19.1 0.0 copy-done
  19.2 0.0 copy-start.2
  19.2 0.0 copy-start.5
  19.2 0.3 first.1
  19.4 3.5 %collective-permute-start.4 = (bf16[16,256]{1,0:T(8,128)(2,1)S(1)}, bf16[16,256]{1,0:T(8,128)(2,1)S(1)}, u32[]{:S(2)}, u32[]{:S(2)}) collective-permute-start(bf16[16,256]{1,0:T(8,128)(2,1)S(1)} %get-tuple-element.31), channel_id=1, source_target_pairs={{0,8},{4,12},{8,16},{12,20},{16,24},{20,28},{24,32},{28,36},{32,40... | collective-permute-start | bytes 24584 | tf_op jit(solution)/shard_map/ppermute | solution.py:26
  23.0 5.5 %collective-permute-start.3 = (bf16[160,256]{1,0:T(8,128)(2,1)S(1)}, bf16[160,256]{1,0:T(8,128)(2,1)S(1)}, u32[]{:S(2)}, u32[]{:S(2)}) collective-permute-start(bf16[160,256]{1,0:T(8,128)(2,1)S(1)} %get-tuple-element.30), channel_id=1, source_target_pairs={{0,4},{4,8},{8,12},{12,16},{16,20},{20,24},{24,28},{28,32},{32,36}... | collective-permute-start | bytes 245768 | tf_op jit(solution)/shard_map/ppermute | solution.py:26
  28.5 0.0 copy-done.4
  28.6 0.0 copy-done.2
  28.6 0.0 copy-done.5
  28.6 0.9 %own.1 = (f32[8,120,256]{2,1,0:T(8,128)S(1)}, f32[8,16,256]{2,1,0:T(8,128)S(1)}, f32[9,8,256]{2,1,0:T(8,128)S(1)}, f32[8,8,256]{2,1,0:T(8,128)S(1)}, f32[8,8,256]{2,1,0:T(8,128)S(1)}) custom-call(f32[128,256]{1,0:T(8,128)S(1)} %get-tuple-element.34.gated_ref, f32[128,1024]{1,0:T(8,128)S(1)} %copy-done.4, f32[8,1024]{1,0:T(8,128)S(1)} %copy-done.2, ...), custom_call_target="tpu_custom_call" | custom-call | flops 1000000000 | bytes 1000000 | tf_op jit(solution)/shard_map/own/pallas_call | solution.py:285
  29.5 0.0 collective-permute-done.4.far_ref
  29.5 0.5 %collective-permute-done.3.near_ref = bf16[160,256]{1,0:T(8,128)(2,1)S(1)} collective-permute-done((bf16[160,256]{1,0:T(8,128)(2,1)S(1)}, bf16[160,256]{1,0:T(8,128)(2,1)S(1)}, u32[]{:S(2)}, u32[]{:S(2)}) %collective-permute-start.3) | collective-permute-done | bytes 81952 | tf_op jit(solution)/shard_map/ppermute | solution.py:26
  30.0 0.0 copy-start.3
  30.0 0.7 %copy-done.3 = f32[1024]{0:T(1024)S(1)} copy-done((f32[1024]{0:T(1024)S(1)}, f32[1024]{0:T(1024)}, u32[]{:S(2)}) %copy-start.3) | copy-done | bytes 4120
  30.7 1.8 %second.1 = (bf16[128,256]{1,0:T(8,128)(2,1)S(1)}, f32[128,256]{1,0:T(8,128)S(1)}, f32[16,8,256]{2,1,0:T(8,128)S(1)}, bf16[16,16,128]{2,1,0:T(8,128)(2,1)}, f32[8,256]{1,0:T(8,128)S(1)}) custom-call(bf16[160,256]{1,0:T(8,128)(2,1)S(1)} %collective-permute-done.3.near_ref, bf16[16,256]{1,0:T(8,128)(2,1)S(1)} %collective-permute-done.4.far_ref, ...), custom_call_target="tpu_custom_call" | custom-call | flops 1000000 | bytes 1000000 | tf_op jit(solution)/shard_map/second/pallas_call | solution.py:285
  32.5 9.6 %all-to-all-start.1 = ((bf16[16,16,128]{2,1,0:T(8,128)(2,1)}), bf16[16,16,128]{2,1,0:T(8,128)(2,1)S(1)}, u32[]{:S(2)}, u32[]{:S(2)}) async-start(bf16[16,16,128]{2,1,0:T(8,128)(2,1)} %get-tuple-element.43), calls=%async_computation.1 | async-start | bytes 131072 | tf_op jit(solution)/shard_map/all_to_all | solution.py:367
  42.2 3.5 %collective-permute-start.5 = (f32[8,256]{1,0:T(8,128)S(1)}, f32[8,256]{1,0:T(8,128)S(1)}, u32[]{:S(2)}, u32[]{:S(2)}) collective-permute-start(f32[8,256]{1,0:T(8,128)S(1)} %get-tuple-element.44), channel_id=1, source_target_pairs={{0,4},{4,8},{8,12},{12,16},{16,20},{20,24},{24,28},{28,32},{32,36}... | collective-permute-start | bytes 24584 | tf_op jit(solution)/shard_map/ppermute | solution.py:26
  45.7 0.2 within.1.local_ref
  45.9 0.6 %collective-permute-done.5.tail_ref = f32[8,256]{1,0:T(8,128)S(1)} collective-permute-done((f32[8,256]{1,0:T(8,128)S(1)}, f32[8,256]{1,0:T(8,128)S(1)}, u32[]{:S(2)}, u32[]{:S(2)}) %collective-permute-start.5) | collective-permute-done | bytes 8224 | tf_op jit(solution)/shard_map/ppermute | solution.py:26
  46.5 3.5 %all-to-all-done.1.ends_ref = bf16[16,16,128]{2,1,0:T(8,128)(2,1)S(1)} async-done(((bf16[16,16,128]{2,1,0:T(8,128)(2,1)}), bf16[16,16,128]{2,1,0:T(8,128)(2,1)S(1)}, u32[]{:S(2)}, u32[]{:S(2)}) %all-to-all-start.1) | async-done | bytes 65568 | tf_op jit(solution)/shard_map/all_to_all | solution.py:367
  50.0 1.1 %third.1 = bf16[128,256]{1,0:T(8,128)(2,1)} custom-call(f32[128,256]{1,0:T(8,128)S(1)} %within.1.local_ref, f32[16,8,256]{2,1,0:T(8,128)S(1)} %get-tuple-element.41.steps_ref, bf16[128,256]{1,0:T(8,128)(2,1)S(1)} %get-tuple-element.42.stream_ref, bf16[16,16,128]{2,1,0:T(8,128)(2,1)S(1)} %all-to-all-done.1.ends_ref, ...), custom_call_target="tpu_custom_call" | custom-call | flops 1000000 | bytes 1000000 | tf_op jit(solution)/shard_map/third/pallas_call | solution.py:285
  (1 shorter events, 0.0 us)
Async XLA Ops:
  0.0 14.6 %copy-start.7 = (f32[2,7,1024]{2,0,1:T(2,128)S(1)}, f32[2,7,1024]{2,0,1:T(2,128)}, u32[]{:S(2)}) copy-start(f32[2,7,1024]{2,0,1:T(2,128)} %param.13) | copy-start | bytes 172036
  2.0 13.9 %all-to-all-start = ((f32[16,1,128]{2,1,0:T(1,128)}), f32[16,1,128]{2,1,0:T(1,128)S(1)}, u32[]{:S(2)}, u32[]{:S(2)}) async-start(f32[16,1,128]{2,1,0:T(1,128)} %bitcast.10), calls=%async_computation | async-start | bytes 16384 | tf_op jit(solution)/shard_map/all_to_all | solution.py:315
  9.6 6.3 %copy-start.1 = (bf16[128,256]{1,0:T(8,128)(2,1)S(1)}, bf16[128,256]{1,0:T(8,128)(2,1)}, u32[]{:S(2)}) copy-start(bf16[128,256]{1,0:T(8,128)(2,1)} %x_ref.1) | copy-start | bytes 196612
  9.6 6.5 %collective-permute-start = (bf16[2,128,256]{2,1,0:T(8,128)(2,1)}, bf16[2,128,256]{2,1,0:T(8,128)(2,1)S(1)}, u32[]{:S(2)}, u32[]{:S(2)}) collective-permute-start(bf16[2,128,256]{2,1,0:T(8,128)(2,1)} %get-tuple-element.27), channel_id=1, source_target_pairs={{0,64},{64,128},{128,192},{192,0},{1,65},{65,129},{129,193},{193,1... | collective-permute-start | bytes 393224 | tf_op jit(solution)/shard_map/ppermute | solution.py:26
  11.0 7.5 %collective-permute-start.1 = (bf16[2,128,256]{2,1,0:T(8,128)(2,1)}, bf16[2,128,256]{2,1,0:T(8,128)(2,1)S(1)}, u32[]{:S(2)}, u32[]{:S(2)}) collective-permute-start(bf16[2,128,256]{2,1,0:T(8,128)(2,1)} %get-tuple-element.28), channel_id=1, source_target_pairs={{0,128},{64,192},{128,0},{192,64},{1,129},{65,193},{129,1},{193,65... | collective-permute-start | bytes 393224 | tf_op jit(solution)/shard_map/ppermute | solution.py:26
  13.4 2.5 %copy-start.6 = (f32[1024]{0:T(1024)S(1)}, f32[1024]{0:T(1024)}, u32[]{:S(2)}) copy-start(f32[1024]{0:T(1024)} %param.12) | copy-start | bytes 12292
  13.4 5.7 %collective-permute-start.2 = (bf16[2,128,256]{2,1,0:T(8,128)(2,1)}, bf16[2,128,256]{2,1,0:T(8,128)(2,1)S(1)}, u32[]{:S(2)}, u32[]{:S(2)}) collective-permute-start(bf16[2,128,256]{2,1,0:T(8,128)(2,1)} %get-tuple-element.29), channel_id=1, source_target_pairs={{0,192},{64,0},{128,64},{192,128},{1,193},{65,1},{129,65},{193,129... | collective-permute-start | bytes 393224 | tf_op jit(solution)/shard_map/ppermute | solution.py:26
  15.9 3.2 %copy-start = (bf16[2,128,256]{2,1,0:T(8,128)(2,1)S(1)}, bf16[2,128,256]{2,1,0:T(8,128)(2,1)}, u32[]{:S(2)}) copy-start(bf16[2,128,256]{2,1,0:T(8,128)(2,1)} %get-tuple-element.26.f0) | copy-start | bytes 393220
  16.0 12.5 %copy-start.4 = (f32[128,1024]{1,0:T(8,128)S(1)}, f32[128,1024]{1,0:T(8,128)}, u32[]{:S(2)}) copy-start(f32[128,1024]{1,0:T(8,128)} %medium_ref.1) | copy-start | bytes 1572868
  19.2 9.4 %copy-start.2 = (f32[8,1024]{1,0:T(8,128)S(1)}, f32[8,1024]{1,0:T(8,128)}, u32[]{:S(2)}) copy-start(f32[8,1024]{1,0:T(8,128)} %rates_ref.3) | copy-start | bytes 98308
  19.2 9.4 %copy-start.5 = (f32[8,1024]{1,0:T(8,128)S(1)}, f32[8,1024]{1,0:T(8,128)}, u32[]{:S(2)}) copy-start(f32[8,1024]{1,0:T(8,128)} %residues_ref.1) | copy-start | bytes 98308
  19.4 10.0 %collective-permute-start.4 = (bf16[16,256]{1,0:T(8,128)(2,1)S(1)}, bf16[16,256]{1,0:T(8,128)(2,1)S(1)}, u32[]{:S(2)}, u32[]{:S(2)}) collective-permute-start(bf16[16,256]{1,0:T(8,128)(2,1)S(1)} %get-tuple-element.31), channel_id=1, source_target_pairs={{0,8},{4,12},{8,16},{12,20},{16,24},{20,28},{24,32},{28,36},{32,40... | collective-permute-start | bytes 24584 | tf_op jit(solution)/shard_map/ppermute | solution.py:26
  23.0 7.0 %collective-permute-start.3 = (bf16[160,256]{1,0:T(8,128)(2,1)S(1)}, bf16[160,256]{1,0:T(8,128)(2,1)S(1)}, u32[]{:S(2)}, u32[]{:S(2)}) collective-permute-start(bf16[160,256]{1,0:T(8,128)(2,1)S(1)} %get-tuple-element.30), channel_id=1, source_target_pairs={{0,4},{4,8},{8,12},{12,16},{16,20},{20,24},{24,28},{28,32},{32,36}... | collective-permute-start | bytes 245768 | tf_op jit(solution)/shard_map/ppermute | solution.py:26
  30.0 0.7 %copy-start.3 = (f32[1024]{0:T(1024)S(1)}, f32[1024]{0:T(1024)}, u32[]{:S(2)}) copy-start(f32[1024]{0:T(1024)} %param.17) | copy-start | bytes 12292
  32.5 17.5 %all-to-all-start.1 = ((bf16[16,16,128]{2,1,0:T(8,128)(2,1)}), bf16[16,16,128]{2,1,0:T(8,128)(2,1)S(1)}, u32[]{:S(2)}, u32[]{:S(2)}) async-start(bf16[16,16,128]{2,1,0:T(8,128)(2,1)} %get-tuple-element.43), calls=%async_computation.1 | async-start | bytes 131072 | tf_op jit(solution)/shard_map/all_to_all | solution.py:367
  42.2 4.3 %collective-permute-start.5 = (f32[8,256]{1,0:T(8,128)S(1)}, f32[8,256]{1,0:T(8,128)S(1)}, u32[]{:S(2)}, u32[]{:S(2)}) collective-permute-start(f32[8,256]{1,0:T(8,128)S(1)} %get-tuple-element.44), channel_id=1, source_target_pairs={{0,4},{4,8},{8,12},{12,16},{16,20},{20,24},{24,28},{28,32},{32,36}... | collective-permute-start | bytes 24584 | tf_op jit(solution)/shard_map/ppermute | solution.py:26

commit v4 on v3

--- a/solution.py
+++ b/solution.py
@@ -12,6 +12,7 @@
 SEC = 4
 CTX = 16
 PEERS = 16
+DISTANCES = (0, 2, 1, 3)
 f32 = jnp.float32
 bf16 = jnp.bfloat16
 
@@ -35,12 +36,12 @@
     first = pltpu.make_async_copy(x_hbm, x_ref, sems.at[8])
     first.start()
     loads = []
-    for distance, ref in enumerate((own_ref, send_1, send_2, send_3)):
+    for slot, (distance, ref) in enumerate(zip(DISTANCES, (own_ref, send_1, send_2, send_3))):
         lanes = lanes_of(lax.rem(sec + distance, SEC))
         for which, source in enumerate((q_hbm, k_hbm)):
             loads.append(
                 pltpu.make_async_copy(
-                    source.at[0, :, lanes], ref.at[which], sems.at[2 * distance + which]
+                    source.at[0, :, lanes], ref.at[which], sems.at[2 * slot + which]
                 )
             )
     for load in loads:
@@ -64,7 +65,7 @@
 
     chosen = read(refs[0])
     for index in range(1, SEC):
-        chosen = jnp.where(distance == index, read(refs[index]), chosen)
+        chosen = jnp.where(distance == DISTANCES[index], read(refs[index]), chosen)
     return chosen
 
 
@@ -140,7 +141,8 @@
 
 
 def own_kernel(
-    gated_ref, medium_ref, rates_ref, residues_ref, partial_ref, taps_ref, powers_ref, carry_ref, kernel_ref
+    gated_ref, medium_ref, rates_ref, residues_ref, direct_ref,
+    partial_ref, taps_ref, powers_ref, carry_ref, kernel_ref,
 ):
     lanes = lanes_of(lax.axis_index("sec"))
     medium_taps = medium_ref[:, lanes].reshape(16, 8, WIDTH)
@@ -156,6 +158,8 @@
         powers_ref[age] = power
         if age < 8:
             row = jnp.sum(weights * power, axis=0, keepdims=True)
+            if age == 0:
+                row += direct_ref[:, lanes]
             kernel_ref[age] = jnp.where(position >= age, row, 0.0)
         if age > 0:
             carries.append(weights * power)
@@ -182,7 +186,7 @@
 
 def second_kernel(
     near_ref, far_ref, head_ref, stream_ref, short_ref,
-    partial_ref, taps_ref, powers_ref, carry_ref, kernel_ref, direct_ref, f0, f1, f2, f3,
+    partial_ref, taps_ref, powers_ref, carry_ref, kernel_ref, f0, f1, f2, f3,
     next_ref, gated_ref, steps_ref, ends_ref, tail_ref,
     source_ref, sums_ref, pad_ref,
 ):
@@ -234,15 +238,14 @@
     sums = within_rows(kernel_ref, last, pad_ref) + carried_rows(carry_ref, before_last)
     q2 = field_of(fields, 2, 0, pl.ds(ROWS - 16, 16))[8:]
     k3 = field_of(fields, 3, 1, pl.ds(ROWS - 16, 16))[8:]
-    tail_ref[...] = k3 * (stream[ROWS - 8 :] + q2 * (sums + direct_ref[:, lanes] * last))
-
-
-def within_kernel(gated_ref, kernel_ref, direct_ref, local_ref, pad_ref):
-    lanes = lanes_of(lax.axis_index("sec"))
+    tail_ref[...] = k3 * (stream[ROWS - 8 :] + q2 * sums)
+
+
+def within_kernel(gated_ref, kernel_ref, local_ref, pad_ref):
     gated = gated_ref[...]
     pad_ref[0:8] = jnp.zeros((8, WIDTH), f32)
     pad_ref[8:] = gated
-    local_ref[...] = within_rows(kernel_ref, gated, pad_ref) + direct_ref[:, lanes] * gated
+    local_ref[...] = within_rows(kernel_ref, gated, pad_ref)
 
 
 def third_kernel(
@@ -310,7 +313,7 @@
         room=60,
     )
     fields = [own] + [
-        shifted(part, "sec", distance + 1, True) for distance, part in enumerate(sends)
+        shifted(part, "sec", distance, True) for distance, part in zip(DISTANCES[1:], sends)
     ]
     squares = lax.all_to_all(squares, ("sec", "ch"), 0, 0, tiled=True)
     (entry,) = call(
@@ -342,9 +345,8 @@
             table,
         ],
         [],
-        (gated, medium, rates, residues),
+        (gated, medium, rates, residues, direct),
         "own",
-        flops=10**9,
     )
     stream, gated, steps, ends, tail = call(
         second_kernel,
@@ -360,7 +362,7 @@
             pltpu.VMEM((8, ROWS + 8, WIDTH), f32),
             pltpu.VMEM((16, WIDTH), f32),
         ],
-        (near_in, far_in, head, stream, short, partial, taps, powers, carry, kernel, direct, *fields),
+        (near_in, far_in, head, stream, short, partial, taps, powers, carry, kernel, *fields),
         "second",
     )
     tail_in = shifted(tail, "ctx", 1, False)
@@ -369,7 +371,7 @@
         within_kernel,
         [shape((ROWS, WIDTH), f32)],
         [pltpu.VMEM((ROWS + 8, WIDTH), f32)],
-        (gated, kernel, direct),
+        (gated, kernel),
         "within",
         flops=10**9,
     )

time: 51.5 us -> 49.1 us (0.953)
  waiting for transfers between devices: 8.99 us -> 7.14 us
  local copies, waits for them, and re-layouts: 0.74 us -> 0.06 us
    ppermute x6, waiting for transfers between devices: 4.22 us -> 2.99 us  [shifted(): return lax.ppermute(value, axis, pairs)]
    unnamed x17, local copies, waits for them, and re-layouts: 0.74 us -> 0.06 us
    all_to_all x1, waiting for transfers between devices: 1.28 us -> 0.66 us  [shards(): squares = lax.all_to_all(squares, ('sec', 'ch'), 0, 0, tiled=True)]
    ppermute x6, starting transfers between devices: 17.6 us -> 18.2 us  [shifted(): return lax.ppermute(value, axis, pairs)]
  transfers between devices with their start and end apart: 8 -> 8, of which waited for: 6 -> 4; matrix products, arithmetic and copies ran while one was open for 0% -> 0% of each run, Pallas kernels for 2% -> 2%
where the time goes in v4:
time: 49.1 us; the launch traced here: 48.7 us
  starting transfers between devices  35 us (71%)
  waiting for transfers between devices  7.14 us (15%)
  Pallas kernels  6.31 us (13%)
    ppermute x6, starting transfers between devices, shifted(): return lax.ppermute(value, axis, pairs)  18.2 us
    all_to_all x1, starting transfers between devices, shards(): ends = lax.all_to_all(ends, 'ctx', 0, 0, tiled=True)  9.2 us
    all_to_all x1, starting transfers between devices, shards(): squares = lax.all_to_all(squares, ('sec', 'ch'), 0, 0, tiled=True)  7.6 us
    pallas_call x7, Pallas kernels, call(): pl.pallas_call(kernel, out_shape=outs, in_specs=[pl.BlockSpec(memory_spac...  6.31 us
    all_to_all x1, waiting for transfers between devices, shards(): ends = lax.all_to_all(ends, 'ctx', 0, 0, tiled=True)  3.5 us
    ppermute x6, waiting for transfers between devices, shifted(): return lax.ppermute(value, axis, pairs)  2.99 us
  transfers between devices with their start and end apart: 8, of which 4 were waited for; matrix products, arithmetic and copies ran while one was open for 0% of the time, Pallas kernels for 2%

profile of v4, /device:TPU:1, one launch (start us, length us, event | category | flops | bytes accessed | tf_op | source)
XLA Modules:
  0.0 48.7 jit_solution(5675730613345258119)
XLA Ops:
  0.0 0.0 copy-start.7
  0.0 2.0 %pack.1 = (f32[16,128]{1,0:T(8,128)}, bf16[2,128,256]{2,1,0:T(8,128)(2,1)}, bf16[2,128,256]{2,1,0:T(8,128)(2,1)}, bf16[2,128,256]{2,1,0:T(8,128)(2,1)}, bf16[2,128,256]{2,1,0:T(8,128)(2,1)}) custom-call(bf16[128,256]{1,0:T(8,128)(2,1)} %x_ref.1, bf16[1,128,1024]{2,1,0:T(8,128)(2,1)} %q_hbm.1, bf16[1,128,1024]{2,1,0:T(8,128)(2,1)} %k_hbm.1), custom_call_target="tpu_custom_call" | custom-call | flops 1000000 | bytes 1000000 | tf_op jit(solution)/shard_map/pack/pallas_call | solution.py:288
  2.0 7.6 %all-to-all-start = ((f32[16,1,128]{2,1,0:T(1,128)}), f32[16,1,128]{2,1,0:T(1,128)S(1)}, u32[]{:S(2)}, u32[]{:S(2)}) async-start(f32[16,1,128]{2,1,0:T(1,128)} %bitcast.9), calls=%async_computation | async-start | bytes 16384 | tf_op jit(solution)/shard_map/all_to_all | solution.py:318
  9.6 0.0 copy-start.3
  9.6 3.0 %collective-permute-start = (bf16[2,128,256]{2,1,0:T(8,128)(2,1)}, bf16[2,128,256]{2,1,0:T(8,128)(2,1)S(1)}, u32[]{:S(2)}, u32[]{:S(2)}) collective-permute-start(bf16[2,128,256]{2,1,0:T(8,128)(2,1)} %get-tuple-element.27), channel_id=1, source_target_pairs={{0,128},{64,192},{128,0},{192,64},{1,129},{65,193},{129,1},{193,65... | collective-permute-start | bytes 393224 | tf_op jit(solution)/shard_map/ppermute | solution.py:27
  12.5 0.3 collective-permute-start.1
  12.8 0.0 copy-start.6
  12.8 2.4 %collective-permute-start.2 = (bf16[2,128,256]{2,1,0:T(8,128)(2,1)}, bf16[2,128,256]{2,1,0:T(8,128)(2,1)S(1)}, u32[]{:S(2)}, u32[]{:S(2)}) collective-permute-start(bf16[2,128,256]{2,1,0:T(8,128)(2,1)} %get-tuple-element.29), channel_id=1, source_target_pairs={{0,192},{64,0},{128,64},{192,128},{1,193},{65,1},{129,65},{193,129... | collective-permute-start | bytes 393224 | tf_op jit(solution)/shard_map/ppermute | solution.py:27
  15.2 0.0 copy-done.7
  15.2 0.7 %all-to-all-done = f32[16,1,128]{2,1,0:T(1,128)S(1)} async-done(((f32[16,1,128]{2,1,0:T(1,128)}), f32[16,1,128]{2,1,0:T(1,128)S(1)}, u32[]{:S(2)}, u32[]{:S(2)}) %all-to-all-start) | async-done | bytes 8224 | tf_op jit(solution)/shard_map/all_to_all | solution.py:318
  15.9 0.0 copy-done.3
  15.9 0.0 copy-done.6
  15.9 0.0 copy-start
  15.9 0.1 entry.1.entry_ref
  16.0 0.0 copy-start.1
  16.0 0.0 collective-permute-done.f1
  16.1 2.4 %collective-permute-done.1.f2 = bf16[2,128,256]{2,1,0:T(8,128)(2,1)S(1)} collective-permute-done((bf16[2,128,256]{2,1,0:T(8,128)(2,1)}, bf16[2,128,256]{2,1,0:T(8,128)(2,1)S(1)}, u32[]{:S(2)}, u32[]{:S(2)}) %collective-permute-start.1) | collective-permute-done | bytes 131104 | tf_op jit(solution)/shard_map/ppermute | solution.py:27
  18.4 0.0 collective-permute-done.2.f3
  18.4 0.0 copy-done
  18.4 0.0 copy-start.2
  18.4 0.0 copy-start.4
  18.4 0.3 first.1
  18.7 0.0 copy-start.5
  18.7 5.5 %collective-permute-start.3 = (bf16[160,256]{1,0:T(8,128)(2,1)S(1)}, bf16[160,256]{1,0:T(8,128)(2,1)S(1)}, u32[]{:S(2)}, u32[]{:S(2)}) collective-permute-start(bf16[160,256]{1,0:T(8,128)(2,1)S(1)} %get-tuple-element.30), channel_id=1, source_target_pairs={{0,4},{4,8},{8,12},{12,16},{16,20},{20,24},{24,28},{28,32},{32,36}... | collective-permute-start | bytes 245768 | tf_op jit(solution)/shard_map/ppermute | solution.py:27
  24.3 3.5 %collective-permute-start.4 = (bf16[16,256]{1,0:T(8,128)(2,1)S(1)}, bf16[16,256]{1,0:T(8,128)(2,1)S(1)}, u32[]{:S(2)}, u32[]{:S(2)}) collective-permute-start(bf16[16,256]{1,0:T(8,128)(2,1)S(1)} %get-tuple-element.31), channel_id=1, source_target_pairs={{0,8},{4,12},{8,16},{12,20},{16,24},{20,28},{24,32},{28,36},{32,40... | collective-permute-start | bytes 24584 | tf_op jit(solution)/shard_map/ppermute | solution.py:27
  27.8 0.0 copy-done.1
  27.8 0.0 copy-done.2
  27.9 0.0 copy-done.4
  27.9 0.0 copy-done.5
  27.9 0.9 %own.1 = (f32[8,120,256]{2,1,0:T(8,128)S(1)}, f32[8,16,256]{2,1,0:T(8,128)S(1)}, f32[9,8,256]{2,1,0:T(8,128)S(1)}, f32[8,8,256]{2,1,0:T(8,128)S(1)}, f32[8,8,256]{2,1,0:T(8,128)S(1)}) custom-call(f32[128,256]{1,0:T(8,128)S(1)} %get-tuple-element.34.gated_ref, f32[128,1024]{1,0:T(8,128)S(1)} %copy-done.1, f32[8,1024]{1,0:T(8,128)S(1)} %copy-done.2, ...), custom_call_target="tpu_custom_call" | custom-call | flops 1000000 | bytes 1000000 | tf_op jit(solution)/shard_map/own/pallas_call | solution.py:288
  28.8 0.0 collective-permute-done.4.far_ref
  28.8 0.0 collective-permute-done.3.near_ref
  28.8 1.8 %second.1 = (bf16[128,256]{1,0:T(8,128)(2,1)S(1)}, f32[128,256]{1,0:T(8,128)S(1)}, f32[16,8,256]{2,1,0:T(8,128)S(1)}, bf16[16,16,128]{2,1,0:T(8,128)(2,1)}, f32[8,256]{1,0:T(8,128)S(1)}) custom-call(bf16[160,256]{1,0:T(8,128)(2,1)S(1)} %collective-permute-done.3.near_ref, bf16[16,256]{1,0:T(8,128)(2,1)S(1)} %collective-permute-done.4.far_ref, ...), custom_call_target="tpu_custom_call" | custom-call | flops 1000000 | bytes 1000000 | tf_op jit(solution)/shard_map/second/pallas_call | solution.py:288
  30.6 9.2 %all-to-all-start.1 = ((bf16[16,16,128]{2,1,0:T(8,128)(2,1)}), bf16[16,16,128]{2,1,0:T(8,128)(2,1)S(1)}, u32[]{:S(2)}, u32[]{:S(2)}) async-start(bf16[16,16,128]{2,1,0:T(8,128)(2,1)} %get-tuple-element.43), calls=%async_computation.1 | async-start | bytes 131072 | tf_op jit(solution)/shard_map/all_to_all | solution.py:369
  39.8 3.5 %collective-permute-start.5 = (f32[8,256]{1,0:T(8,128)S(1)}, f32[8,256]{1,0:T(8,128)S(1)}, u32[]{:S(2)}, u32[]{:S(2)}) collective-permute-start(f32[8,256]{1,0:T(8,128)S(1)} %get-tuple-element.44), channel_id=1, source_target_pairs={{0,4},{4,8},{8,12},{12,16},{16,20},{20,24},{24,28},{28,32},{32,36}... | collective-permute-start | bytes 24584 | tf_op jit(solution)/shard_map/ppermute | solution.py:27
  43.4 0.1 within.1.local_ref
  43.5 0.6 %collective-permute-done.5.tail_ref = f32[8,256]{1,0:T(8,128)S(1)} collective-permute-done((f32[8,256]{1,0:T(8,128)S(1)}, f32[8,256]{1,0:T(8,128)S(1)}, u32[]{:S(2)}, u32[]{:S(2)}) %collective-permute-start.5) | collective-permute-done | bytes 8224 | tf_op jit(solution)/shard_map/ppermute | solution.py:27
  44.1 3.5 %all-to-all-done.1.ends_ref = bf16[16,16,128]{2,1,0:T(8,128)(2,1)S(1)} async-done(((bf16[16,16,128]{2,1,0:T(8,128)(2,1)}), bf16[16,16,128]{2,1,0:T(8,128)(2,1)S(1)}, u32[]{:S(2)}, u32[]{:S(2)}) %all-to-all-start.1) | async-done | bytes 65568 | tf_op jit(solution)/shard_map/all_to_all | solution.py:369
  47.6 1.1 %third.1 = bf16[128,256]{1,0:T(8,128)(2,1)} custom-call(f32[128,256]{1,0:T(8,128)S(1)} %within.1.local_ref, f32[16,8,256]{2,1,0:T(8,128)S(1)} %get-tuple-element.41.steps_ref, bf16[128,256]{1,0:T(8,128)(2,1)S(1)} %get-tuple-element.42.stream_ref, bf16[16,16,128]{2,1,0:T(8,128)(2,1)S(1)} %all-to-all-done.1.ends_ref, ...), custom_call_target="tpu_custom_call" | custom-call | flops 1000000 | bytes 1000000 | tf_op jit(solution)/shard_map/third/pallas_call | solution.py:288
  (1 shorter events, 0.0 us)
Async XLA Ops:
  0.0 15.2 %copy-start.7 = (f32[2,7,1024]{2,0,1:T(2,128)S(1)}, f32[2,7,1024]{2,0,1:T(2,128)}, u32[]{:S(2)}) copy-start(f32[2,7,1024]{2,0,1:T(2,128)} %param.13) | copy-start | bytes 172036
  2.0 13.9 %all-to-all-start = ((f32[16,1,128]{2,1,0:T(1,128)}), f32[16,1,128]{2,1,0:T(1,128)S(1)}, u32[]{:S(2)}, u32[]{:S(2)}) async-start(f32[16,1,128]{2,1,0:T(1,128)} %bitcast.9), calls=%async_computation | async-start | bytes 16384 | tf_op jit(solution)/shard_map/all_to_all | solution.py:318
  9.6 6.3 %copy-start.3 = (bf16[128,256]{1,0:T(8,128)(2,1)S(1)}, bf16[128,256]{1,0:T(8,128)(2,1)}, u32[]{:S(2)}) copy-start(bf16[128,256]{1,0:T(8,128)(2,1)} %x_ref.1) | copy-start | bytes 196612
  9.6 6.5 %collective-permute-start = (bf16[2,128,256]{2,1,0:T(8,128)(2,1)}, bf16[2,128,256]{2,1,0:T(8,128)(2,1)S(1)}, u32[]{:S(2)}, u32[]{:S(2)}) collective-permute-start(bf16[2,128,256]{2,1,0:T(8,128)(2,1)} %get-tuple-element.27), channel_id=1, source_target_pairs={{0,128},{64,192},{128,0},{192,64},{1,129},{65,193},{129,1},{193,65... | collective-permute-start | bytes 393224 | tf_op jit(solution)/shard_map/ppermute | solution.py:27
  12.5 5.9 %collective-permute-start.1 = (bf16[2,128,256]{2,1,0:T(8,128)(2,1)}, bf16[2,128,256]{2,1,0:T(8,128)(2,1)S(1)}, u32[]{:S(2)}, u32[]{:S(2)}) collective-permute-start(bf16[2,128,256]{2,1,0:T(8,128)(2,1)} %get-tuple-element.28), channel_id=1, source_target_pairs={{0,64},{64,128},{128,192},{192,0},{1,65},{65,129},{129,193},{193,1... | collective-permute-start | bytes 393224 | tf_op jit(solution)/shard_map/ppermute | solution.py:27
  12.8 3.1 %copy-start.6 = (f32[1024]{0:T(1024)S(1)}, f32[1024]{0:T(1024)}, u32[]{:S(2)}) copy-start(f32[1024]{0:T(1024)} %param.12) | copy-start | bytes 12292
  12.8 5.6 %collective-permute-start.2 = (bf16[2,128,256]{2,1,0:T(8,128)(2,1)}, bf16[2,128,256]{2,1,0:T(8,128)(2,1)S(1)}, u32[]{:S(2)}, u32[]{:S(2)}) collective-permute-start(bf16[2,128,256]{2,1,0:T(8,128)(2,1)} %get-tuple-element.29), channel_id=1, source_target_pairs={{0,192},{64,0},{128,64},{192,128},{1,193},{65,1},{129,65},{193,129... | collective-permute-start | bytes 393224 | tf_op jit(solution)/shard_map/ppermute | solution.py:27
  15.9 2.5 %copy-start = (bf16[2,128,256]{2,1,0:T(8,128)(2,1)S(1)}, bf16[2,128,256]{2,1,0:T(8,128)(2,1)}, u32[]{:S(2)}) copy-start(bf16[2,128,256]{2,1,0:T(8,128)(2,1)} %get-tuple-element.26.f0) | copy-start | bytes 393220
  16.0 11.8 %copy-start.1 = (f32[128,1024]{1,0:T(8,128)S(1)}, f32[128,1024]{1,0:T(8,128)}, u32[]{:S(2)}) copy-start(f32[128,1024]{1,0:T(8,128)} %medium_ref.1) | copy-start | bytes 1572868
  18.4 9.4 %copy-start.2 = (f32[8,1024]{1,0:T(8,128)S(1)}, f32[8,1024]{1,0:T(8,128)}, u32[]{:S(2)}) copy-start(f32[8,1024]{1,0:T(8,128)} %rates_ref.3) | copy-start | bytes 98308
  18.4 9.4 %copy-start.4 = (f32[8,1024]{1,0:T(8,128)S(1)}, f32[8,1024]{1,0:T(8,128)}, u32[]{:S(2)}) copy-start(f32[8,1024]{1,0:T(8,128)} %residues_ref.1) | copy-start | bytes 98308
  18.7 9.1 %copy-start.5 = (f32[1024]{0:T(1024)S(1)}, f32[1024]{0:T(1024)}, u32[]{:S(2)}) copy-start(f32[1024]{0:T(1024)} %param.17) | copy-start | bytes 12292
  18.7 10.0 %collective-permute-start.3 = (bf16[160,256]{1,0:T(8,128)(2,1)S(1)}, bf16[160,256]{1,0:T(8,128)(2,1)S(1)}, u32[]{:S(2)}, u32[]{:S(2)}) collective-permute-start(bf16[160,256]{1,0:T(8,128)(2,1)S(1)} %get-tuple-element.30), channel_id=1, source_target_pairs={{0,4},{4,8},{8,12},{12,16},{16,20},{20,24},{24,28},{28,32},{32,36}... | collective-permute-start | bytes 245768 | tf_op jit(solution)/shard_map/ppermute | solution.py:27
  24.3 4.5 %collective-permute-start.4 = (bf16[16,256]{1,0:T(8,128)(2,1)S(1)}, bf16[16,256]{1,0:T(8,128)(2,1)S(1)}, u32[]{:S(2)}, u32[]{:S(2)}) collective-permute-start(bf16[16,256]{1,0:T(8,128)(2,1)S(1)} %get-tuple-element.31), channel_id=1, source_target_pairs={{0,8},{4,12},{8,16},{12,20},{16,24},{20,28},{24,32},{28,36},{32,40... | collective-permute-start | bytes 24584 | tf_op jit(solution)/shard_map/ppermute | solution.py:27
  30.6 17.0 %all-to-all-start.1 = ((bf16[16,16,128]{2,1,0:T(8,128)(2,1)}), bf16[16,16,128]{2,1,0:T(8,128)(2,1)S(1)}, u32[]{:S(2)}, u32[]{:S(2)}) async-start(bf16[16,16,128]{2,1,0:T(8,128)(2,1)} %get-tuple-element.43), calls=%async_computation.1 | async-start | bytes 131072 | tf_op jit(solution)/shard_map/all_to_all | solution.py:369
  39.8 4.3 %collective-permute-start.5 = (f32[8,256]{1,0:T(8,128)S(1)}, f32[8,256]{1,0:T(8,128)S(1)}, u32[]{:S(2)}, u32[]{:S(2)}) collective-permute-start(f32[8,256]{1,0:T(8,128)S(1)} %get-tuple-element.44), channel_id=1, source_target_pairs={{0,4},{4,8},{8,12},{12,16},{16,20},{20,24},{24,28},{28,32},{32,36}... | collective-permute-start | bytes 24584 | tf_op jit(solution)/shard_map/ppermute | solution.py:27

commit v5 on v4

--- a/solution.py
+++ b/solution.py
@@ -76,7 +76,7 @@
     return total
 
 
-def entry_kernel(x_ref, squares_ref, gain_ref, stream_ref):
+def entry_kernel(x_ref, squares_ref, gain_ref, across_ref, kept_ref, stream_ref):
     lanes = lanes_of(lax.axis_index("sec"))
     sums = jnp.sum(squares_ref[...], axis=0, keepdims=True)
     inverse = lax.rsqrt(jnp.broadcast_to(sums, (128, 128)).T / D + EPS)
@@ -289,7 +289,7 @@
         kernel,
         out_shape=outs,
         in_specs=[
-            pl.BlockSpec(memory_space=pltpu.HBM) if index in in_hbm else vmem
+            pl.BlockSpec(memory_space=pl.ANY) if index in in_hbm else vmem
             for index in range(len(operands))
         ],
         out_specs=[vmem] * len(outs),
@@ -317,7 +317,7 @@
     ]
     squares = lax.all_to_all(squares, ("sec", "ch"), 0, 0, tiled=True)
     (entry,) = call(
-        entry_kernel, [shape((ROWS, WIDTH), bf16)], [], (x, squares, gain), "entry", flops=10**11
+        entry_kernel, [shape((ROWS, WIDTH), bf16)], [], (x, squares, gain, fields[1], own), "entry", in_hbm=(3,), flops=10**10
     )
     head, stream, gated, halo, far = call(
         first_kernel,

time: 49.1 us -> 47.9 us (0.976)
  starting transfers between devices: 35 us -> 33.3 us
  waiting for transfers between devices: 7.14 us -> 7.67 us
    all_to_all x1, starting transfers between devices: 7.6 us -> 4.62 us  [shards(): squares = lax.all_to_all(squares, ('sec', 'ch'), 0, 0, tiled=True)]
    all_to_all x1, waiting for transfers between devices: 0.66 us -> 3.54 us  [shards(): squares = lax.all_to_all(squares, ('sec', 'ch'), 0, 0, tiled=True)]
    ppermute x6, waiting for transfers between devices: 2.99 us -> 0.63 us  [shifted(): return lax.ppermute(value, axis, pairs)]
    ppermute x6, starting transfers between devices: 18.2 us -> 19.5 us  [shifted(): return lax.ppermute(value, axis, pairs)]
  transfers between devices with their start and end apart: 8 -> 8, of which waited for: 4 -> 3; matrix products, arithmetic and copies ran while one was open for 0% -> 0% of each run, Pallas kernels for 2% -> 2%
where the time goes in v5:
time: 47.9 us; the launch traced here: 47.6 us
  starting transfers between devices  33.3 us (70%)
  waiting for transfers between devices  7.67 us (16%)
  Pallas kernels  6.36 us (13%)
    ppermute x6, starting transfers between devices, shifted(): return lax.ppermute(value, axis, pairs)  19.5 us
    all_to_all x1, starting transfers between devices, shards(): ends = lax.all_to_all(ends, 'ctx', 0, 0, tiled=True)  9.2 us
    pallas_call x7, Pallas kernels, call(): pl.pallas_call(kernel, out_shape=outs, in_specs=[pl.BlockSpec(memory_spac...  6.36 us
    all_to_all x1, starting transfers between devices, shards(): squares = lax.all_to_all(squares, ('sec', 'ch'), 0, 0, tiled=True)  4.62 us
    all_to_all x1, waiting for transfers between devices, shards(): squares = lax.all_to_all(squares, ('sec', 'ch'), 0, 0, tiled=True)  3.54 us
    all_to_all x1, waiting for transfers between devices, shards(): ends = lax.all_to_all(ends, 'ctx', 0, 0, tiled=True)  3.5 us
  transfers between devices with their start and end apart: 8, of which 3 were waited for; matrix products, arithmetic and copies ran while one was open for 0% of the time, Pallas kernels for 2%

profile of v5, /device:TPU:1, one launch (start us, length us, event | category | flops | bytes accessed | tf_op | source)
XLA Modules:
  0.0 47.6 jit_solution(7027149814166303396)
XLA Ops:
  0.0 0.0 copy-start.7
  0.0 0.0 copy-start.3
  0.0 2.0 %pack.1 = (f32[16,128]{1,0:T(8,128)}, bf16[2,128,256]{2,1,0:T(8,128)(2,1)}, bf16[2,128,256]{2,1,0:T(8,128)(2,1)}, bf16[2,128,256]{2,1,0:T(8,128)(2,1)}, bf16[2,128,256]{2,1,0:T(8,128)(2,1)}) custom-call(bf16[128,256]{1,0:T(8,128)(2,1)} %x_ref.1, bf16[1,128,1024]{2,1,0:T(8,128)(2,1)} %q_hbm.1, bf16[1,128,1024]{2,1,0:T(8,128)(2,1)} %k_hbm.1), custom_call_target="tpu_custom_call" | custom-call | flops 1000000 | bytes 1000000 | tf_op jit(solution)/shard_map/pack/pallas_call | solution.py:288
  2.0 0.0 copy-start
  2.0 3.8 %collective-permute-start = (bf16[2,128,256]{2,1,0:T(8,128)(2,1)}, bf16[2,128,256]{2,1,0:T(8,128)(2,1)S(1)}, u32[]{:S(2)}, u32[]{:S(2)}) collective-permute-start(bf16[2,128,256]{2,1,0:T(8,128)(2,1)} %get-tuple-element.26), channel_id=1, source_target_pairs={{0,128},{64,192},{128,0},{192,64},{1,129},{65,193},{129,1},{193,65... | collective-permute-start | bytes 393224 | tf_op jit(solution)/shard_map/ppermute | solution.py:27
  5.9 4.6 %all-to-all-start = ((f32[16,1,128]{2,1,0:T(1,128)}), f32[16,1,128]{2,1,0:T(1,128)S(1)}, u32[]{:S(2)}, u32[]{:S(2)}) async-start(f32[16,1,128]{2,1,0:T(1,128)} %bitcast.9), calls=%async_computation | async-start | bytes 16384 | tf_op jit(solution)/shard_map/all_to_all | solution.py:318
  10.5 1.4 %collective-permute-start.1 = (bf16[2,128,256]{2,1,0:T(8,128)(2,1)}, bf16[2,128,256]{2,1,0:T(8,128)(2,1)S(1)}, u32[]{:S(2)}, u32[]{:S(2)}) collective-permute-start(bf16[2,128,256]{2,1,0:T(8,128)(2,1)} %get-tuple-element.28), channel_id=1, source_target_pairs={{0,64},{64,128},{128,192},{192,0},{1,65},{65,129},{129,193},{193,1... | collective-permute-start | bytes 393224 | tf_op jit(solution)/shard_map/ppermute | solution.py:27
  11.8 1.4 %collective-permute-start.2 = (bf16[2,128,256]{2,1,0:T(8,128)(2,1)}, bf16[2,128,256]{2,1,0:T(8,128)(2,1)S(1)}, u32[]{:S(2)}, u32[]{:S(2)}) collective-permute-start(bf16[2,128,256]{2,1,0:T(8,128)(2,1)} %get-tuple-element.29), channel_id=1, source_target_pairs={{0,192},{64,0},{128,64},{192,128},{1,193},{65,1},{129,65},{193,129... | collective-permute-start | bytes 393224 | tf_op jit(solution)/shard_map/ppermute | solution.py:27
  13.2 0.0 copy-done.7
  13.3 0.0 copy-start.6
  13.3 3.5 %all-to-all-done = f32[16,1,128]{2,1,0:T(1,128)S(1)} async-done(((f32[16,1,128]{2,1,0:T(1,128)}), f32[16,1,128]{2,1,0:T(1,128)S(1)}, u32[]{:S(2)}, u32[]{:S(2)}) %all-to-all-start) | async-done | bytes 8224 | tf_op jit(solution)/shard_map/all_to_all | solution.py:318
  16.8 0.0 collective-permute-done.across_ref.f1
  16.8 0.0 copy-done.3
  16.8 0.0 copy-done
  16.8 0.0 copy-done.6
  16.8 0.1 entry.1.entry_ref
  17.0 0.0 copy-start.1
  17.0 0.0 copy-start.2
  17.0 0.0 copy-start.4
  17.0 0.0 collective-permute-done.1.f2
  17.0 0.0 collective-permute-done.2.f3
  17.0 0.3 first.1
  17.3 0.0 copy-start.5
  17.3 5.8 %collective-permute-start.3 = (bf16[160,256]{1,0:T(8,128)(2,1)S(1)}, bf16[160,256]{1,0:T(8,128)(2,1)S(1)}, u32[]{:S(2)}, u32[]{:S(2)}) collective-permute-start(bf16[160,256]{1,0:T(8,128)(2,1)S(1)} %get-tuple-element.30), channel_id=1, source_target_pairs={{0,4},{4,8},{8,12},{12,16},{16,20},{20,24},{24,28},{28,32},{32,36}... | collective-permute-start | bytes 245768 | tf_op jit(solution)/shard_map/ppermute | solution.py:27
  23.1 3.5 %collective-permute-start.4 = (bf16[16,256]{1,0:T(8,128)(2,1)S(1)}, bf16[16,256]{1,0:T(8,128)(2,1)S(1)}, u32[]{:S(2)}, u32[]{:S(2)}) collective-permute-start(bf16[16,256]{1,0:T(8,128)(2,1)S(1)} %get-tuple-element.31), channel_id=1, source_target_pairs={{0,8},{4,12},{8,16},{12,20},{16,24},{20,28},{24,32},{28,36},{32,40... | collective-permute-start | bytes 24584 | tf_op jit(solution)/shard_map/ppermute | solution.py:27
  26.7 0.0 copy-done.1
  26.7 0.0 copy-done.2
  26.7 0.0 copy-done.4
  26.7 0.0 copy-done.5
  26.7 0.9 %own.1 = (f32[8,120,256]{2,1,0:T(8,128)S(1)}, f32[8,16,256]{2,1,0:T(8,128)S(1)}, f32[9,8,256]{2,1,0:T(8,128)S(1)}, f32[8,8,256]{2,1,0:T(8,128)S(1)}, f32[8,8,256]{2,1,0:T(8,128)S(1)}) custom-call(f32[128,256]{1,0:T(8,128)S(1)} %get-tuple-element.34.gated_ref, f32[128,1024]{1,0:T(8,128)S(1)} %copy-done.1, f32[8,1024]{1,0:T(8,128)S(1)} %copy-done.2, ...), custom_call_target="tpu_custom_call" | custom-call | flops 1000000 | bytes 1000000 | tf_op jit(solution)/shard_map/own/pallas_call | solution.py:288
  27.6 0.0 collective-permute-done.4.far_ref
  27.6 0.0 collective-permute-done.3.near_ref
  27.7 1.8 %second.1 = (bf16[128,256]{1,0:T(8,128)(2,1)S(1)}, f32[128,256]{1,0:T(8,128)S(1)}, f32[16,8,256]{2,1,0:T(8,128)S(1)}, bf16[16,16,128]{2,1,0:T(8,128)(2,1)}, f32[8,256]{1,0:T(8,128)S(1)}) custom-call(bf16[160,256]{1,0:T(8,128)(2,1)S(1)} %collective-permute-done.3.near_ref, bf16[16,256]{1,0:T(8,128)(2,1)S(1)} %collective-permute-done.4.far_ref, ...), custom_call_target="tpu_custom_call" | custom-call | flops 1000000 | bytes 1000000 | tf_op jit(solution)/shard_map/second/pallas_call | solution.py:288
  29.5 9.2 %all-to-all-start.1 = ((bf16[16,16,128]{2,1,0:T(8,128)(2,1)}), bf16[16,16,128]{2,1,0:T(8,128)(2,1)S(1)}, u32[]{:S(2)}, u32[]{:S(2)}) async-start(bf16[16,16,128]{2,1,0:T(8,128)(2,1)} %get-tuple-element.43), calls=%async_computation.1 | async-start | bytes 131072 | tf_op jit(solution)/shard_map/all_to_all | solution.py:369
  38.7 3.5 %collective-permute-start.5 = (f32[8,256]{1,0:T(8,128)S(1)}, f32[8,256]{1,0:T(8,128)S(1)}, u32[]{:S(2)}, u32[]{:S(2)}) collective-permute-start(f32[8,256]{1,0:T(8,128)S(1)} %get-tuple-element.44), channel_id=1, source_target_pairs={{0,4},{4,8},{8,12},{12,16},{16,20},{20,24},{24,28},{28,32},{32,36}... | collective-permute-start | bytes 24584 | tf_op jit(solution)/shard_map/ppermute | solution.py:27
  42.2 0.1 within.1.local_ref
  42.4 0.6 %collective-permute-done.5.tail_ref = f32[8,256]{1,0:T(8,128)S(1)} collective-permute-done((f32[8,256]{1,0:T(8,128)S(1)}, f32[8,256]{1,0:T(8,128)S(1)}, u32[]{:S(2)}, u32[]{:S(2)}) %collective-permute-start.5) | collective-permute-done | bytes 8224 | tf_op jit(solution)/shard_map/ppermute | solution.py:27
  43.0 3.5 %all-to-all-done.1.ends_ref = bf16[16,16,128]{2,1,0:T(8,128)(2,1)S(1)} async-done(((bf16[16,16,128]{2,1,0:T(8,128)(2,1)}), bf16[16,16,128]{2,1,0:T(8,128)(2,1)S(1)}, u32[]{:S(2)}, u32[]{:S(2)}) %all-to-all-start.1) | async-done | bytes 65568 | tf_op jit(solution)/shard_map/all_to_all | solution.py:369
  46.5 1.1 %third.1 = bf16[128,256]{1,0:T(8,128)(2,1)} custom-call(f32[128,256]{1,0:T(8,128)S(1)} %within.1.local_ref, f32[16,8,256]{2,1,0:T(8,128)S(1)} %get-tuple-element.41.steps_ref, bf16[128,256]{1,0:T(8,128)(2,1)S(1)} %get-tuple-element.42.stream_ref, bf16[16,16,128]{2,1,0:T(8,128)(2,1)S(1)} %all-to-all-done.1.ends_ref, ...), custom_call_target="tpu_custom_call" | custom-call | flops 1000000 | bytes 1000000 | tf_op jit(solution)/shard_map/third/pallas_call | solution.py:288
  (1 shorter events, 0.0 us)
Async XLA Ops:
  0.0 13.2 %copy-start.7 = (f32[2,7,1024]{2,0,1:T(2,128)S(1)}, f32[2,7,1024]{2,0,1:T(2,128)}, u32[]{:S(2)}) copy-start(f32[2,7,1024]{2,0,1:T(2,128)} %param.13) | copy-start | bytes 172036
  0.0 16.8 %copy-start.3 = (bf16[128,256]{1,0:T(8,128)(2,1)S(1)}, bf16[128,256]{1,0:T(8,128)(2,1)}, u32[]{:S(2)}) copy-start(bf16[128,256]{1,0:T(8,128)(2,1)} %x_ref.1) | copy-start | bytes 196612
  2.0 14.8 %copy-start = (bf16[2,128,256]{2,1,0:T(8,128)(2,1)S(1)}, bf16[2,128,256]{2,1,0:T(8,128)(2,1)}, u32[]{:S(2)}) copy-start(bf16[2,128,256]{2,1,0:T(8,128)(2,1)} %get-tuple-element.27.kept_ref.f0) | copy-start | bytes 393220
  2.0 14.8 %collective-permute-start = (bf16[2,128,256]{2,1,0:T(8,128)(2,1)}, bf16[2,128,256]{2,1,0:T(8,128)(2,1)S(1)}, u32[]{:S(2)}, u32[]{:S(2)}) collective-permute-start(bf16[2,128,256]{2,1,0:T(8,128)(2,1)} %get-tuple-element.26), channel_id=1, source_target_pairs={{0,128},{64,192},{128,0},{192,64},{1,129},{65,193},{129,1},{193,65... | collective-permute-start | bytes 393224 | tf_op jit(solution)/shard_map/ppermute | solution.py:27
  5.9 11.0 %all-to-all-start = ((f32[16,1,128]{2,1,0:T(1,128)}), f32[16,1,128]{2,1,0:T(1,128)S(1)}, u32[]{:S(2)}, u32[]{:S(2)}) async-start(f32[16,1,128]{2,1,0:T(1,128)} %bitcast.9), calls=%async_computation | async-start | bytes 16384 | tf_op jit(solution)/shard_map/all_to_all | solution.py:318
  10.5 6.5 %collective-permute-start.1 = (bf16[2,128,256]{2,1,0:T(8,128)(2,1)}, bf16[2,128,256]{2,1,0:T(8,128)(2,1)S(1)}, u32[]{:S(2)}, u32[]{:S(2)}) collective-permute-start(bf16[2,128,256]{2,1,0:T(8,128)(2,1)} %get-tuple-element.28), channel_id=1, source_target_pairs={{0,64},{64,128},{128,192},{192,0},{1,65},{65,129},{129,193},{193,1... | collective-permute-start | bytes 393224 | tf_op jit(solution)/shard_map/ppermute | solution.py:27
  11.8 5.2 %collective-permute-start.2 = (bf16[2,128,256]{2,1,0:T(8,128)(2,1)}, bf16[2,128,256]{2,1,0:T(8,128)(2,1)S(1)}, u32[]{:S(2)}, u32[]{:S(2)}) collective-permute-start(bf16[2,128,256]{2,1,0:T(8,128)(2,1)} %get-tuple-element.29), channel_id=1, source_target_pairs={{0,192},{64,0},{128,64},{192,128},{1,193},{65,1},{129,65},{193,129... | collective-permute-start | bytes 393224 | tf_op jit(solution)/shard_map/ppermute | solution.py:27
  13.3 3.6 %copy-start.6 = (f32[1024]{0:T(1024)S(1)}, f32[1024]{0:T(1024)}, u32[]{:S(2)}) copy-start(f32[1024]{0:T(1024)} %param.12) | copy-start | bytes 12292
  17.0 9.7 %copy-start.1 = (f32[128,1024]{1,0:T(8,128)S(1)}, f32[128,1024]{1,0:T(8,128)}, u32[]{:S(2)}) copy-start(f32[128,1024]{1,0:T(8,128)} %medium_ref.1) | copy-start | bytes 1572868
  17.0 9.7 %copy-start.2 = (f32[8,1024]{1,0:T(8,128)S(1)}, f32[8,1024]{1,0:T(8,128)}, u32[]{:S(2)}) copy-start(f32[8,1024]{1,0:T(8,128)} %rates_ref.3) | copy-start | bytes 98308
  17.0 9.7 %copy-start.4 = (f32[8,1024]{1,0:T(8,128)S(1)}, f32[8,1024]{1,0:T(8,128)}, u32[]{:S(2)}) copy-start(f32[8,1024]{1,0:T(8,128)} %residues_ref.1) | copy-start | bytes 98308
  17.3 9.4 %copy-start.5 = (f32[1024]{0:T(1024)S(1)}, f32[1024]{0:T(1024)}, u32[]{:S(2)}) copy-start(f32[1024]{0:T(1024)} %param.17) | copy-start | bytes 12292
  17.3 10.3 %collective-permute-start.3 = (bf16[160,256]{1,0:T(8,128)(2,1)S(1)}, bf16[160,256]{1,0:T(8,128)(2,1)S(1)}, u32[]{:S(2)}, u32[]{:S(2)}) collective-permute-start(bf16[160,256]{1,0:T(8,128)(2,1)S(1)} %get-tuple-element.30), channel_id=1, source_target_pairs={{0,4},{4,8},{8,12},{12,16},{16,20},{20,24},{24,28},{28,32},{32,36}... | collective-permute-start | bytes 245768 | tf_op jit(solution)/shard_map/ppermute | solution.py:27
  23.1 4.5 %collective-permute-start.4 = (bf16[16,256]{1,0:T(8,128)(2,1)S(1)}, bf16[16,256]{1,0:T(8,128)(2,1)S(1)}, u32[]{:S(2)}, u32[]{:S(2)}) collective-permute-start(bf16[16,256]{1,0:T(8,128)(2,1)S(1)} %get-tuple-element.31), channel_id=1, source_target_pairs={{0,8},{4,12},{8,16},{12,20},{16,24},{20,28},{24,32},{28,36},{32,40... | collective-permute-start | bytes 24584 | tf_op jit(solution)/shard_map/ppermute | solution.py:27
  29.5 17.0 %all-to-all-start.1 = ((bf16[16,16,128]{2,1,0:T(8,128)(2,1)}), bf16[16,16,128]{2,1,0:T(8,128)(2,1)S(1)}, u32[]{:S(2)}, u32[]{:S(2)}) async-start(bf16[16,16,128]{2,1,0:T(8,128)(2,1)} %get-tuple-element.43), calls=%async_computation.1 | async-start | bytes 131072 | tf_op jit(solution)/shard_map/all_to_all | solution.py:369
  38.7 4.3 %collective-permute-start.5 = (f32[8,256]{1,0:T(8,128)S(1)}, f32[8,256]{1,0:T(8,128)S(1)}, u32[]{:S(2)}, u32[]{:S(2)}) collective-permute-start(f32[8,256]{1,0:T(8,128)S(1)} %get-tuple-element.44), channel_id=1, source_target_pairs={{0,4},{4,8},{8,12},{12,16},{16,20},{20,24},{24,28},{28,32},{32,36}... | collective-permute-start | bytes 24584 | tf_op jit(solution)/shard_map/ppermute | solution.py:27

commit v6 on v5

--- a/solution.py
+++ b/solution.py
@@ -31,7 +31,7 @@
     return pl.ds(pl.multiple_of(position * WIDTH, WIDTH), WIDTH)
 
 
-def pack_kernel(x_hbm, q_hbm, k_hbm, squares_ref, own_ref, send_1, send_2, send_3, x_ref, sems):
+def pack_kernel(x_hbm, q_hbm, k_hbm, squares_hbm, own_ref, send_1, send_2, send_3, x_ref, squares_ref, sems):
     sec = lax.axis_index("sec")
     first = pltpu.make_async_copy(x_hbm, x_ref, sems.at[8])
     first.start()
@@ -52,6 +52,8 @@
     folded = squared[:, :128] + squared[:, 128:]
     squares = jnp.sum(folded.T, axis=0, keepdims=True)
     squares_ref[...] = jnp.broadcast_to(squares, squares_ref.shape)
+    loads.append(pltpu.make_async_copy(squares_ref, squares_hbm, sems.at[9]))
+    loads[-1].start()
     for load in loads:
         load.wait()
 
@@ -137,7 +139,7 @@
             partial_ref[shift, start : start + 8, here] = total
         return carry
 
-    lax.fori_loop(0, 16, step, 0)
+    lax.fori_loop(0, 16, step, 0, unroll=2)
 
 
 def own_kernel(
@@ -283,7 +285,7 @@
     return jax.ShapeDtypeStruct(dims, dtype)
 
 
-def call(kernel, outs, scratch, operands, name, in_hbm=(), flops=1000000, room=32):
+def call(kernel, outs, scratch, operands, name, in_hbm=(), out_hbm=(), flops=1000000, room=32):
     vmem = pl.BlockSpec(memory_space=pltpu.VMEM)
     return pl.pallas_call(
         kernel,
@@ -292,7 +294,10 @@
             pl.BlockSpec(memory_space=pl.ANY) if index in in_hbm else vmem
             for index in range(len(operands))
         ],
-        out_specs=[vmem] * len(outs),
+        out_specs=[
+            pl.BlockSpec(memory_space=pl.ANY) if index in out_hbm else vmem
+            for index in range(len(outs))
+        ],
         scratch_shapes=scratch,
         compiler_params=pltpu.CompilerParams(vmem_limit_bytes=room * 1024 * 1024),
         cost_estimate=pl.CostEstimate(flops=flops, bytes_accessed=1000000, transcendentals=0),
@@ -306,11 +311,15 @@
     squares, own, *sends = call(
         pack_kernel,
         [shape((PEERS, 128), f32)] + [pair] * 4,
-        [pltpu.VMEM((ROWS, WIDTH), bf16), pltpu.SemaphoreType.DMA((9,))],
-        (x, q, k),
+        [
+            pltpu.VMEM((ROWS, WIDTH), bf16),
+            pltpu.VMEM((PEERS, 128), f32),
+            pltpu.SemaphoreType.DMA((10,)),
+        ],
+        tuple(pltpu.with_memory_space_constraint(value, pltpu.HBM) for value in (x, q, k)),
         "pack",
         in_hbm=(0, 1, 2),
-        room=60,
+        out_hbm=(0,),
     )
     fields = [own] + [
         shifted(part, "sec", distance, True) for distance, part in zip(DISTANCES[1:], sends)

time: 47.9 us -> 47.4 us (0.990)
  Pallas kernels: 6.36 us -> 5.75 us
    pallas_call x7, Pallas kernels: 6.36 us -> 5.75 us  [call(): pl.pallas_call(kernel, out_shape=outs, in_specs=[pl.BlockSpec(memory_spac...]
where the time goes in v6:
time: 47.4 us; the launch traced here: 47.1 us
  starting transfers between devices  33.4 us (70%)
  waiting for transfers between devices  7.66 us (16%)
  Pallas kernels  5.75 us (12%)
    ppermute x6, starting transfers between devices, shifted(): return lax.ppermute(value, axis, pairs)  19.5 us
    all_to_all x1, starting transfers between devices, shards(): ends = lax.all_to_all(ends, 'ctx', 0, 0, tiled=True)  9.36 us
    pallas_call x7, Pallas kernels, call(): pl.pallas_call(kernel, out_shape=outs, in_specs=[pl.BlockSpec(memory_spac...  5.75 us
    all_to_all x1, starting transfers between devices, shards(): squares = lax.all_to_all(squares, ('sec', 'ch'), 0, 0, tiled=True)  4.62 us
    all_to_all x1, waiting for transfers between devices, shards(): squares = lax.all_to_all(squares, ('sec', 'ch'), 0, 0, tiled=True)  3.53 us
    all_to_all x1, waiting for transfers between devices, shards(): ends = lax.all_to_all(ends, 'ctx', 0, 0, tiled=True)  3.5 us
  transfers between devices with their start and end apart: 8, of which 3 were waited for; matrix products, arithmetic and copies ran while one was open for 0% of the time, Pallas kernels for 2%

profile of v6, /device:TPU:1, one launch (start us, length us, event | category | flops | bytes accessed | tf_op | source)
XLA Modules:
  0.0 47.1 jit_solution(889645228777287184)
XLA Ops:
  0.0 0.0 copy-start.6
  0.0 1.6 %pack.1 = (f32[16,128]{1,0:T(8,128)}, bf16[2,128,256]{2,1,0:T(8,128)(2,1)S(1)}, bf16[2,128,256]{2,1,0:T(8,128)(2,1)S(1)}, bf16[2,128,256]{2,1,0:T(8,128)(2,1)S(1)}, bf16[2,128,256]{2,1,0:T(8,128)(2,1)S(1)}) custom-call(bf16[128,256]{1,0:T(8,128)(2,1)} %x_ref.1, bf16[1,128,1024]{2,1,0:T(8,128)(2,1)} %q_hbm.1, bf16[1,128,1024]{2,1,0:T(8,128)(2,1)} %k_hbm.1), custom_call_target="tpu_custom_call" | custom-call | flops 1000000 | bytes 1000000 | tf_op jit(solution)/shard_map/pack/pallas_call | solution.py:290
  1.6 3.8 %collective-permute-start = (bf16[2,128,256]{2,1,0:T(8,128)(2,1)S(1)}, bf16[2,128,256]{2,1,0:T(8,128)(2,1)S(1)}, u32[]{:S(2)}, u32[]{:S(2)}) collective-permute-start(bf16[2,128,256]{2,1,0:T(8,128)(2,1)S(1)} %get-tuple-element.26), channel_id=1, source_target_pairs={{0,128},{64,192},{128,0},{192,64},{1,129},{65,193},{129,1},{193,65... | collective-permute-start | bytes 393224 | tf_op jit(solution)/shard_map/ppermute | solution.py:27
  5.5 4.6 %all-to-all-start = ((f32[16,1,128]{2,1,0:T(1,128)}), f32[16,1,128]{2,1,0:T(1,128)S(1)}, u32[]{:S(2)}, u32[]{:S(2)}) async-start(f32[16,1,128]{2,1,0:T(1,128)} %bitcast.1), calls=%async_computation | async-start | bytes 16384 | tf_op jit(solution)/shard_map/all_to_all | solution.py:327
  10.1 0.0 copy-start.2
  10.1 1.4 %collective-permute-start.1 = (bf16[2,128,256]{2,1,0:T(8,128)(2,1)S(1)}, bf16[2,128,256]{2,1,0:T(8,128)(2,1)S(1)}, u32[]{:S(2)}, u32[]{:S(2)}) collective-permute-start(bf16[2,128,256]{2,1,0:T(8,128)(2,1)S(1)} %get-tuple-element.28), channel_id=1, source_target_pairs={{0,64},{64,128},{128,192},{192,0},{1,65},{65,129},{129,193},{193,1... | collective-permute-start | bytes 393224 | tf_op jit(solution)/shard_map/ppermute | solution.py:27
  11.6 1.3 %collective-permute-start.2 = (bf16[2,128,256]{2,1,0:T(8,128)(2,1)S(1)}, bf16[2,128,256]{2,1,0:T(8,128)(2,1)S(1)}, u32[]{:S(2)}, u32[]{:S(2)}) collective-permute-start(bf16[2,128,256]{2,1,0:T(8,128)(2,1)S(1)} %get-tuple-element.29), channel_id=1, source_target_pairs={{0,192},{64,0},{128,64},{192,128},{1,193},{65,1},{129,65},{193,129... | collective-permute-start | bytes 393224 | tf_op jit(solution)/shard_map/ppermute | solution.py:27
  12.9 0.0 copy-done.6
  12.9 0.0 copy-start.5
  12.9 3.5 %all-to-all-done = f32[16,1,128]{2,1,0:T(1,128)S(1)} async-done(((f32[16,1,128]{2,1,0:T(1,128)}), f32[16,1,128]{2,1,0:T(1,128)S(1)}, u32[]{:S(2)}, u32[]{:S(2)}) %all-to-all-start) | async-done | bytes 8224 | tf_op jit(solution)/shard_map/all_to_all | solution.py:327
  16.4 0.0 collective-permute-done.across_ref.f1
  16.4 0.0 copy-done.2
  16.4 0.0 copy-done.5
  16.4 0.1 entry.1.entry_ref
  16.6 0.0 copy-start
  16.6 0.0 copy-start.1
  16.6 0.0 copy-start.3
  16.6 0.0 collective-permute-done.1.f2
  16.6 0.0 collective-permute-done.2.f3
  16.6 0.3 first.1
  16.9 0.0 copy-start.4
  16.9 5.8 %collective-permute-start.3 = (bf16[160,256]{1,0:T(8,128)(2,1)S(1)}, bf16[160,256]{1,0:T(8,128)(2,1)S(1)}, u32[]{:S(2)}, u32[]{:S(2)}) collective-permute-start(bf16[160,256]{1,0:T(8,128)(2,1)S(1)} %get-tuple-element.30), channel_id=1, source_target_pairs={{0,4},{4,8},{8,12},{12,16},{16,20},{20,24},{24,28},{28,32},{32,36}... | collective-permute-start | bytes 245768 | tf_op jit(solution)/shard_map/ppermute | solution.py:27
  22.8 3.5 %collective-permute-start.4 = (bf16[16,256]{1,0:T(8,128)(2,1)S(1)}, bf16[16,256]{1,0:T(8,128)(2,1)S(1)}, u32[]{:S(2)}, u32[]{:S(2)}) collective-permute-start(bf16[16,256]{1,0:T(8,128)(2,1)S(1)} %get-tuple-element.31), channel_id=1, source_target_pairs={{0,8},{4,12},{8,16},{12,20},{16,24},{20,28},{24,32},{28,36},{32,40... | collective-permute-start | bytes 24584 | tf_op jit(solution)/shard_map/ppermute | solution.py:27
  26.3 0.0 copy-done
  26.3 0.0 copy-done.1
  26.3 0.0 copy-done.3
  26.3 0.0 copy-done.4
  26.3 0.7 %own.1 = (f32[8,120,256]{2,1,0:T(8,128)S(1)}, f32[8,16,256]{2,1,0:T(8,128)S(1)}, f32[9,8,256]{2,1,0:T(8,128)S(1)}, f32[8,8,256]{2,1,0:T(8,128)S(1)}, f32[8,8,256]{2,1,0:T(8,128)S(1)}) custom-call(f32[128,256]{1,0:T(8,128)S(1)} %get-tuple-element.34.gated_ref, f32[128,1024]{1,0:T(8,128)S(1)} %copy-done, f32[8,1024]{1,0:T(8,128)S(1)} %copy-done.1, ...), custom_call_target="tpu_custom_call" | custom-call | flops 1000000 | bytes 1000000 | tf_op jit(solution)/shard_map/own/pallas_call | solution.py:290
  27.1 0.0 collective-permute-done.4.far_ref
  27.1 0.0 collective-permute-done.3.near_ref
  27.1 1.8 %second.1 = (bf16[128,256]{1,0:T(8,128)(2,1)S(1)}, f32[128,256]{1,0:T(8,128)S(1)}, f32[16,8,256]{2,1,0:T(8,128)S(1)}, bf16[16,16,128]{2,1,0:T(8,128)(2,1)}, f32[8,256]{1,0:T(8,128)S(1)}) custom-call(bf16[160,256]{1,0:T(8,128)(2,1)S(1)} %collective-permute-done.3.near_ref, bf16[16,256]{1,0:T(8,128)(2,1)S(1)} %collective-permute-done.4.far_ref, ...), custom_call_target="tpu_custom_call" | custom-call | flops 1000000 | bytes 1000000 | tf_op jit(solution)/shard_map/second/pallas_call | solution.py:290
  28.9 9.4 %all-to-all-start.1 = ((bf16[16,16,128]{2,1,0:T(8,128)(2,1)}), bf16[16,16,128]{2,1,0:T(8,128)(2,1)S(1)}, u32[]{:S(2)}, u32[]{:S(2)}) async-start(bf16[16,16,128]{2,1,0:T(8,128)(2,1)} %get-tuple-element.43), calls=%async_computation.1 | async-start | bytes 131072 | tf_op jit(solution)/shard_map/all_to_all | solution.py:378
  38.2 3.5 %collective-permute-start.5 = (f32[8,256]{1,0:T(8,128)S(1)}, f32[8,256]{1,0:T(8,128)S(1)}, u32[]{:S(2)}, u32[]{:S(2)}) collective-permute-start(f32[8,256]{1,0:T(8,128)S(1)} %get-tuple-element.44), channel_id=1, source_target_pairs={{0,4},{4,8},{8,12},{12,16},{16,20},{20,24},{24,28},{28,32},{32,36}... | collective-permute-start | bytes 24584 | tf_op jit(solution)/shard_map/ppermute | solution.py:27
  41.8 0.1 within.1.local_ref
  41.9 0.6 %collective-permute-done.5.tail_ref = f32[8,256]{1,0:T(8,128)S(1)} collective-permute-done((f32[8,256]{1,0:T(8,128)S(1)}, f32[8,256]{1,0:T(8,128)S(1)}, u32[]{:S(2)}, u32[]{:S(2)}) %collective-permute-start.5) | collective-permute-done | bytes 8224 | tf_op jit(solution)/shard_map/ppermute | solution.py:27
  42.5 3.5 %all-to-all-done.1.ends_ref = bf16[16,16,128]{2,1,0:T(8,128)(2,1)S(1)} async-done(((bf16[16,16,128]{2,1,0:T(8,128)(2,1)}), bf16[16,16,128]{2,1,0:T(8,128)(2,1)S(1)}, u32[]{:S(2)}, u32[]{:S(2)}) %all-to-all-start.1) | async-done | bytes 65568 | tf_op jit(solution)/shard_map/all_to_all | solution.py:378
  46.0 1.1 %third.1 = bf16[128,256]{1,0:T(8,128)(2,1)} custom-call(f32[128,256]{1,0:T(8,128)S(1)} %within.1.local_ref, f32[16,8,256]{2,1,0:T(8,128)S(1)} %get-tuple-element.41.steps_ref, bf16[128,256]{1,0:T(8,128)(2,1)S(1)} %get-tuple-element.42.stream_ref, bf16[16,16,128]{2,1,0:T(8,128)(2,1)S(1)} %all-to-all-done.1.ends_ref, ...), custom_call_target="tpu_custom_call" | custom-call | flops 1000000 | bytes 1000000 | tf_op jit(solution)/shard_map/third/pallas_call | solution.py:290
  (1 shorter events, 0.0 us)
Async XLA Ops:
  0.0 12.9 %copy-start.6 = (f32[2,7,1024]{2,0,1:T(2,128)S(1)}, f32[2,7,1024]{2,0,1:T(2,128)}, u32[]{:S(2)}) copy-start(f32[2,7,1024]{2,0,1:T(2,128)} %param.13) | copy-start | bytes 172036
  1.6 14.8 %collective-permute-start = (bf16[2,128,256]{2,1,0:T(8,128)(2,1)S(1)}, bf16[2,128,256]{2,1,0:T(8,128)(2,1)S(1)}, u32[]{:S(2)}, u32[]{:S(2)}) collective-permute-start(bf16[2,128,256]{2,1,0:T(8,128)(2,1)S(1)} %get-tuple-element.26), channel_id=1, source_target_pairs={{0,128},{64,192},{128,0},{192,64},{1,129},{65,193},{129,1},{193,65... | collective-permute-start | bytes 393224 | tf_op jit(solution)/shard_map/ppermute | solution.py:27
  5.5 11.0 %all-to-all-start = ((f32[16,1,128]{2,1,0:T(1,128)}), f32[16,1,128]{2,1,0:T(1,128)S(1)}, u32[]{:S(2)}, u32[]{:S(2)}) async-start(f32[16,1,128]{2,1,0:T(1,128)} %bitcast.1), calls=%async_computation | async-start | bytes 16384 | tf_op jit(solution)/shard_map/all_to_all | solution.py:327
  10.1 6.3 %copy-start.2 = (bf16[128,256]{1,0:T(8,128)(2,1)S(1)}, bf16[128,256]{1,0:T(8,128)(2,1)}, u32[]{:S(2)}) copy-start(bf16[128,256]{1,0:T(8,128)(2,1)} %x_ref.1) | copy-start | bytes 196612
  10.1 6.5 %collective-permute-start.1 = (bf16[2,128,256]{2,1,0:T(8,128)(2,1)S(1)}, bf16[2,128,256]{2,1,0:T(8,128)(2,1)S(1)}, u32[]{:S(2)}, u32[]{:S(2)}) collective-permute-start(bf16[2,128,256]{2,1,0:T(8,128)(2,1)S(1)} %get-tuple-element.28), channel_id=1, source_target_pairs={{0,64},{64,128},{128,192},{192,0},{1,65},{65,129},{129,193},{193,1... | collective-permute-start | bytes 393224 | tf_op jit(solution)/shard_map/ppermute | solution.py:27
  11.6 5.1 %collective-permute-start.2 = (bf16[2,128,256]{2,1,0:T(8,128)(2,1)S(1)}, bf16[2,128,256]{2,1,0:T(8,128)(2,1)S(1)}, u32[]{:S(2)}, u32[]{:S(2)}) collective-permute-start(bf16[2,128,256]{2,1,0:T(8,128)(2,1)S(1)} %get-tuple-element.29), channel_id=1, source_target_pairs={{0,192},{64,0},{128,64},{192,128},{1,193},{65,1},{129,65},{193,129... | collective-permute-start | bytes 393224 | tf_op jit(solution)/shard_map/ppermute | solution.py:27
  12.9 3.5 %copy-start.5 = (f32[1024]{0:T(1024)S(1)}, f32[1024]{0:T(1024)}, u32[]{:S(2)}) copy-start(f32[1024]{0:T(1024)} %param.12) | copy-start | bytes 12292
  16.6 9.7 %copy-start = (f32[128,1024]{1,0:T(8,128)S(1)}, f32[128,1024]{1,0:T(8,128)}, u32[]{:S(2)}) copy-start(f32[128,1024]{1,0:T(8,128)} %medium_ref.1) | copy-start | bytes 1572868
  16.6 9.7 %copy-start.1 = (f32[8,1024]{1,0:T(8,128)S(1)}, f32[8,1024]{1,0:T(8,128)}, u32[]{:S(2)}) copy-start(f32[8,1024]{1,0:T(8,128)} %rates_ref.3) | copy-start | bytes 98308
  16.6 9.7 %copy-start.3 = (f32[8,1024]{1,0:T(8,128)S(1)}, f32[8,1024]{1,0:T(8,128)}, u32[]{:S(2)}) copy-start(f32[8,1024]{1,0:T(8,128)} %residues_ref.1) | copy-start | bytes 98308
  16.9 9.4 %copy-start.4 = (f32[1024]{0:T(1024)S(1)}, f32[1024]{0:T(1024)}, u32[]{:S(2)}) copy-start(f32[1024]{0:T(1024)} %param.17) | copy-start | bytes 12292
  16.9 10.2 %collective-permute-start.3 = (bf16[160,256]{1,0:T(8,128)(2,1)S(1)}, bf16[160,256]{1,0:T(8,128)(2,1)S(1)}, u32[]{:S(2)}, u32[]{:S(2)}) collective-permute-start(bf16[160,256]{1,0:T(8,128)(2,1)S(1)} %get-tuple-element.30), channel_id=1, source_target_pairs={{0,4},{4,8},{8,12},{12,16},{16,20},{20,24},{24,28},{28,32},{32,36}... | collective-permute-start | bytes 245768 | tf_op jit(solution)/shard_map/ppermute | solution.py:27
  22.8 4.3 %collective-permute-start.4 = (bf16[16,256]{1,0:T(8,128)(2,1)S(1)}, bf16[16,256]{1,0:T(8,128)(2,1)S(1)}, u32[]{:S(2)}, u32[]{:S(2)}) collective-permute-start(bf16[16,256]{1,0:T(8,128)(2,1)S(1)} %get-tuple-element.31), channel_id=1, source_target_pairs={{0,8},{4,12},{8,16},{12,20},{16,24},{20,28},{24,32},{28,36},{32,40... | collective-permute-start | bytes 24584 | tf_op jit(solution)/shard_map/ppermute | solution.py:27
  28.9 17.2 %all-to-all-start.1 = ((bf16[16,16,128]{2,1,0:T(8,128)(2,1)}), bf16[16,16,128]{2,1,0:T(8,128)(2,1)S(1)}, u32[]{:S(2)}, u32[]{:S(2)}) async-start(bf16[16,16,128]{2,1,0:T(8,128)(2,1)} %get-tuple-element.43), calls=%async_computation.1 | async-start | bytes 131072 | tf_op jit(solution)/shard_map/all_to_all | solution.py:378
  38.2 4.3 %collective-permute-start.5 = (f32[8,256]{1,0:T(8,128)S(1)}, f32[8,256]{1,0:T(8,128)S(1)}, u32[]{:S(2)}, u32[]{:S(2)}) collective-permute-start(f32[8,256]{1,0:T(8,128)S(1)} %get-tuple-element.44), channel_id=1, source_target_pairs={{0,4},{4,8},{8,12},{12,16},{16,20},{20,24},{24,28},{28,32},{32,36}... | collective-permute-start | bytes 24584 | tf_op jit(solution)/shard_map/ppermute | solution.py:27

commit v7 on v6

--- a/solution.py
+++ b/solution.py
@@ -260,13 +260,15 @@
     mine = lax.axis_index("ctx")
     rates = rates_ref[:, lanes]
     span = jnp.exp(-rates * ROWS)
-    state = jnp.zeros((8, WIDTH), f32)
+    state = 0.0 * span
     previous = state
-    for position in range(CTX - 1):
+
+    def join(position, states):
+        state, previous = states
         received = ends_ref[position].astype(f32)
-        longer = span * state + jnp.concatenate([received[0:8], received[8:16]], axis=1)
-        previous = jnp.where(position < mine - 1, longer, previous)
-        state = jnp.where(position < mine, longer, state)
+        return span * state + jnp.concatenate([received[0:8], received[8:16]], axis=1), state
+
+    state, previous = lax.fori_loop(0, mine, join, (state, previous))
     carried = carried_rows(carry_ref, jnp.exp(-rates * (ROWS - 8)) * previous)
     gates = near_ref[ROWS + 16 :].astype(f32)[8:]
     pad_ref[0:8] = tail_ref[...] + gates * carried

time: 47.4 us -> 47.4 us (level)
  no operation moved by 1% of the time
where the time goes in v7:
time: 47.4 us; the launch traced here: 47.1 us
  starting transfers between devices  33.4 us (70%)
  waiting for transfers between devices  7.66 us (16%)
  Pallas kernels  5.72 us (12%)
    ppermute x6, starting transfers between devices, shifted(): return lax.ppermute(value, axis, pairs)  19.5 us
    all_to_all x1, starting transfers between devices, shards(): ends = lax.all_to_all(ends, 'ctx', 0, 0, tiled=True)  9.36 us
    pallas_call x7, Pallas kernels, call(): pl.pallas_call(kernel, out_shape=outs, in_specs=[pl.BlockSpec(memory_spac...  5.72 us
    all_to_all x1, starting transfers between devices, shards(): squares = lax.all_to_all(squares, ('sec', 'ch'), 0, 0, tiled=True)  4.62 us
    all_to_all x1, waiting for transfers between devices, shards(): squares = lax.all_to_all(squares, ('sec', 'ch'), 0, 0, tiled=True)  3.53 us
    all_to_all x1, waiting for transfers between devices, shards(): ends = lax.all_to_all(ends, 'ctx', 0, 0, tiled=True)  3.5 us
  transfers between devices with their start and end apart: 8, of which 3 were waited for; matrix products, arithmetic and copies ran while one was open for 0% of the time, Pallas kernels for 2%

profile of v7, /device:TPU:1, one launch (start us, length us, event | category | flops | bytes accessed | tf_op | source)
XLA Modules:
  0.0 47.1 jit_solution(7190605085668901714)
XLA Ops:
  0.0 0.0 copy-start.6
  0.0 1.6 %pack.1 = (f32[16,128]{1,0:T(8,128)}, bf16[2,128,256]{2,1,0:T(8,128)(2,1)S(1)}, bf16[2,128,256]{2,1,0:T(8,128)(2,1)S(1)}, bf16[2,128,256]{2,1,0:T(8,128)(2,1)S(1)}, bf16[2,128,256]{2,1,0:T(8,128)(2,1)S(1)}) custom-call(bf16[128,256]{1,0:T(8,128)(2,1)} %x_ref.1, bf16[1,128,1024]{2,1,0:T(8,128)(2,1)} %q_hbm.1, bf16[1,128,1024]{2,1,0:T(8,128)(2,1)} %k_hbm.1), custom_call_target="tpu_custom_call" | custom-call | flops 1000000 | bytes 1000000 | tf_op jit(solution)/shard_map/pack/pallas_call | solution.py:292
  1.6 3.8 %collective-permute-start = (bf16[2,128,256]{2,1,0:T(8,128)(2,1)S(1)}, bf16[2,128,256]{2,1,0:T(8,128)(2,1)S(1)}, u32[]{:S(2)}, u32[]{:S(2)}) collective-permute-start(bf16[2,128,256]{2,1,0:T(8,128)(2,1)S(1)} %get-tuple-element.26), channel_id=1, source_target_pairs={{0,128},{64,192},{128,0},{192,64},{1,129},{65,193},{129,1},{193,65... | collective-permute-start | bytes 393224 | tf_op jit(solution)/shard_map/ppermute | solution.py:27
  5.5 4.6 %all-to-all-start = ((f32[16,1,128]{2,1,0:T(1,128)}), f32[16,1,128]{2,1,0:T(1,128)S(1)}, u32[]{:S(2)}, u32[]{:S(2)}) async-start(f32[16,1,128]{2,1,0:T(1,128)} %bitcast.1), calls=%async_computation | async-start | bytes 16384 | tf_op jit(solution)/shard_map/all_to_all | solution.py:329
  10.1 0.0 copy-start.2
  10.1 1.4 %collective-permute-start.1 = (bf16[2,128,256]{2,1,0:T(8,128)(2,1)S(1)}, bf16[2,128,256]{2,1,0:T(8,128)(2,1)S(1)}, u32[]{:S(2)}, u32[]{:S(2)}) collective-permute-start(bf16[2,128,256]{2,1,0:T(8,128)(2,1)S(1)} %get-tuple-element.28), channel_id=1, source_target_pairs={{0,64},{64,128},{128,192},{192,0},{1,65},{65,129},{129,193},{193,1... | collective-permute-start | bytes 393224 | tf_op jit(solution)/shard_map/ppermute | solution.py:27
  11.6 1.3 %collective-permute-start.2 = (bf16[2,128,256]{2,1,0:T(8,128)(2,1)S(1)}, bf16[2,128,256]{2,1,0:T(8,128)(2,1)S(1)}, u32[]{:S(2)}, u32[]{:S(2)}) collective-permute-start(bf16[2,128,256]{2,1,0:T(8,128)(2,1)S(1)} %get-tuple-element.29), channel_id=1, source_target_pairs={{0,192},{64,0},{128,64},{192,128},{1,193},{65,1},{129,65},{193,129... | collective-permute-start | bytes 393224 | tf_op jit(solution)/shard_map/ppermute | solution.py:27
  12.9 0.0 copy-done.6
  12.9 0.0 copy-start.5
  12.9 3.5 %all-to-all-done = f32[16,1,128]{2,1,0:T(1,128)S(1)} async-done(((f32[16,1,128]{2,1,0:T(1,128)}), f32[16,1,128]{2,1,0:T(1,128)S(1)}, u32[]{:S(2)}, u32[]{:S(2)}) %all-to-all-start) | async-done | bytes 8224 | tf_op jit(solution)/shard_map/all_to_all | solution.py:329
  16.4 0.0 collective-permute-done.across_ref.f1
  16.4 0.0 copy-done.2
  16.4 0.0 copy-done.5
  16.4 0.1 entry.1.entry_ref
  16.6 0.0 copy-start
  16.6 0.0 copy-start.1
  16.6 0.0 copy-start.3
  16.6 0.0 collective-permute-done.1.f2
  16.6 0.0 collective-permute-done.2.f3
  16.6 0.3 first.1
  16.9 0.0 copy-start.4
  16.9 5.8 %collective-permute-start.3 = (bf16[160,256]{1,0:T(8,128)(2,1)S(1)}, bf16[160,256]{1,0:T(8,128)(2,1)S(1)}, u32[]{:S(2)}, u32[]{:S(2)}) collective-permute-start(bf16[160,256]{1,0:T(8,128)(2,1)S(1)} %get-tuple-element.30), channel_id=1, source_target_pairs={{0,4},{4,8},{8,12},{12,16},{16,20},{20,24},{24,28},{28,32},{32,36}... | collective-permute-start | bytes 245768 | tf_op jit(solution)/shard_map/ppermute | solution.py:27
  22.8 3.5 %collective-permute-start.4 = (bf16[16,256]{1,0:T(8,128)(2,1)S(1)}, bf16[16,256]{1,0:T(8,128)(2,1)S(1)}, u32[]{:S(2)}, u32[]{:S(2)}) collective-permute-start(bf16[16,256]{1,0:T(8,128)(2,1)S(1)} %get-tuple-element.31), channel_id=1, source_target_pairs={{0,8},{4,12},{8,16},{12,20},{16,24},{20,28},{24,32},{28,36},{32,40... | collective-permute-start | bytes 24584 | tf_op jit(solution)/shard_map/ppermute | solution.py:27
  26.3 0.0 copy-done
  26.3 0.0 copy-done.1
  26.3 0.0 copy-done.3
  26.3 0.0 copy-done.4
  26.3 0.7 %own.1 = (f32[8,120,256]{2,1,0:T(8,128)S(1)}, f32[8,16,256]{2,1,0:T(8,128)S(1)}, f32[9,8,256]{2,1,0:T(8,128)S(1)}, f32[8,8,256]{2,1,0:T(8,128)S(1)}, f32[8,8,256]{2,1,0:T(8,128)S(1)}) custom-call(f32[128,256]{1,0:T(8,128)S(1)} %get-tuple-element.34.gated_ref, f32[128,1024]{1,0:T(8,128)S(1)} %copy-done, f32[8,1024]{1,0:T(8,128)S(1)} %copy-done.1, ...), custom_call_target="tpu_custom_call" | custom-call | flops 1000000 | bytes 1000000 | tf_op jit(solution)/shard_map/own/pallas_call | solution.py:292
  27.1 0.0 collective-permute-done.4.far_ref
  27.1 0.0 collective-permute-done.3.near_ref
  27.1 1.8 %second.1 = (bf16[128,256]{1,0:T(8,128)(2,1)S(1)}, f32[128,256]{1,0:T(8,128)S(1)}, f32[16,8,256]{2,1,0:T(8,128)S(1)}, bf16[16,16,128]{2,1,0:T(8,128)(2,1)}, f32[8,256]{1,0:T(8,128)S(1)}) custom-call(bf16[160,256]{1,0:T(8,128)(2,1)S(1)} %collective-permute-done.3.near_ref, bf16[16,256]{1,0:T(8,128)(2,1)S(1)} %collective-permute-done.4.far_ref, ...), custom_call_target="tpu_custom_call" | custom-call | flops 1000000 | bytes 1000000 | tf_op jit(solution)/shard_map/second/pallas_call | solution.py:292
  28.9 9.4 %all-to-all-start.1 = ((bf16[16,16,128]{2,1,0:T(8,128)(2,1)}), bf16[16,16,128]{2,1,0:T(8,128)(2,1)S(1)}, u32[]{:S(2)}, u32[]{:S(2)}) async-start(bf16[16,16,128]{2,1,0:T(8,128)(2,1)} %get-tuple-element.43), calls=%async_computation.1 | async-start | bytes 131072 | tf_op jit(solution)/shard_map/all_to_all | solution.py:380
  38.2 3.5 %collective-permute-start.5 = (f32[8,256]{1,0:T(8,128)S(1)}, f32[8,256]{1,0:T(8,128)S(1)}, u32[]{:S(2)}, u32[]{:S(2)}) collective-permute-start(f32[8,256]{1,0:T(8,128)S(1)} %get-tuple-element.44), channel_id=1, source_target_pairs={{0,4},{4,8},{8,12},{12,16},{16,20},{20,24},{24,28},{28,32},{32,36}... | collective-permute-start | bytes 24584 | tf_op jit(solution)/shard_map/ppermute | solution.py:27
  41.8 0.1 within.1.local_ref
  41.9 0.6 %collective-permute-done.5.tail_ref = f32[8,256]{1,0:T(8,128)S(1)} collective-permute-done((f32[8,256]{1,0:T(8,128)S(1)}, f32[8,256]{1,0:T(8,128)S(1)}, u32[]{:S(2)}, u32[]{:S(2)}) %collective-permute-start.5) | collective-permute-done | bytes 8224 | tf_op jit(solution)/shard_map/ppermute | solution.py:27
  42.5 3.5 %all-to-all-done.1.ends_ref = bf16[16,16,128]{2,1,0:T(8,128)(2,1)S(1)} async-done(((bf16[16,16,128]{2,1,0:T(8,128)(2,1)}), bf16[16,16,128]{2,1,0:T(8,128)(2,1)S(1)}, u32[]{:S(2)}, u32[]{:S(2)}) %all-to-all-start.1) | async-done | bytes 65568 | tf_op jit(solution)/shard_map/all_to_all | solution.py:380
  46.0 1.0 %third.1 = bf16[128,256]{1,0:T(8,128)(2,1)} custom-call(f32[128,256]{1,0:T(8,128)S(1)} %within.1.local_ref, f32[16,8,256]{2,1,0:T(8,128)S(1)} %get-tuple-element.41.steps_ref, bf16[128,256]{1,0:T(8,128)(2,1)S(1)} %get-tuple-element.42.stream_ref, bf16[16,16,128]{2,1,0:T(8,128)(2,1)S(1)} %all-to-all-done.1.ends_ref, ...), custom_call_target="tpu_custom_call" | custom-call | flops 1000000 | bytes 1000000 | tf_op jit(solution)/shard_map/third/pallas_call | solution.py:292
  (1 shorter events, 0.0 us)
Async XLA Ops:
  0.0 12.9 %copy-start.6 = (f32[2,7,1024]{2,0,1:T(2,128)S(1)}, f32[2,7,1024]{2,0,1:T(2,128)}, u32[]{:S(2)}) copy-start(f32[2,7,1024]{2,0,1:T(2,128)} %param.13) | copy-start | bytes 172036
  1.6 14.8 %collective-permute-start = (bf16[2,128,256]{2,1,0:T(8,128)(2,1)S(1)}, bf16[2,128,256]{2,1,0:T(8,128)(2,1)S(1)}, u32[]{:S(2)}, u32[]{:S(2)}) collective-permute-start(bf16[2,128,256]{2,1,0:T(8,128)(2,1)S(1)} %get-tuple-element.26), channel_id=1, source_target_pairs={{0,128},{64,192},{128,0},{192,64},{1,129},{65,193},{129,1},{193,65... | collective-permute-start | bytes 393224 | tf_op jit(solution)/shard_map/ppermute | solution.py:27
  5.5 11.0 %all-to-all-start = ((f32[16,1,128]{2,1,0:T(1,128)}), f32[16,1,128]{2,1,0:T(1,128)S(1)}, u32[]{:S(2)}, u32[]{:S(2)}) async-start(f32[16,1,128]{2,1,0:T(1,128)} %bitcast.1), calls=%async_computation | async-start | bytes 16384 | tf_op jit(solution)/shard_map/all_to_all | solution.py:329
  10.1 6.3 %copy-start.2 = (bf16[128,256]{1,0:T(8,128)(2,1)S(1)}, bf16[128,256]{1,0:T(8,128)(2,1)}, u32[]{:S(2)}) copy-start(bf16[128,256]{1,0:T(8,128)(2,1)} %x_ref.1) | copy-start | bytes 196612
  10.1 6.5 %collective-permute-start.1 = (bf16[2,128,256]{2,1,0:T(8,128)(2,1)S(1)}, bf16[2,128,256]{2,1,0:T(8,128)(2,1)S(1)}, u32[]{:S(2)}, u32[]{:S(2)}) collective-permute-start(bf16[2,128,256]{2,1,0:T(8,128)(2,1)S(1)} %get-tuple-element.28), channel_id=1, source_target_pairs={{0,64},{64,128},{128,192},{192,0},{1,65},{65,129},{129,193},{193,1... | collective-permute-start | bytes 393224 | tf_op jit(solution)/shard_map/ppermute | solution.py:27
  11.6 5.1 %collective-permute-start.2 = (bf16[2,128,256]{2,1,0:T(8,128)(2,1)S(1)}, bf16[2,128,256]{2,1,0:T(8,128)(2,1)S(1)}, u32[]{:S(2)}, u32[]{:S(2)}) collective-permute-start(bf16[2,128,256]{2,1,0:T(8,128)(2,1)S(1)} %get-tuple-element.29), channel_id=1, source_target_pairs={{0,192},{64,0},{128,64},{192,128},{1,193},{65,1},{129,65},{193,129... | collective-permute-start | bytes 393224 | tf_op jit(solution)/shard_map/ppermute | solution.py:27
  12.9 3.5 %copy-start.5 = (f32[1024]{0:T(1024)S(1)}, f32[1024]{0:T(1024)}, u32[]{:S(2)}) copy-start(f32[1024]{0:T(1024)} %param.12) | copy-start | bytes 12292
  16.6 9.7 %copy-start = (f32[128,1024]{1,0:T(8,128)S(1)}, f32[128,1024]{1,0:T(8,128)}, u32[]{:S(2)}) copy-start(f32[128,1024]{1,0:T(8,128)} %medium_ref.1) | copy-start | bytes 1572868
  16.6 9.7 %copy-start.1 = (f32[8,1024]{1,0:T(8,128)S(1)}, f32[8,1024]{1,0:T(8,128)}, u32[]{:S(2)}) copy-start(f32[8,1024]{1,0:T(8,128)} %rates_ref.3) | copy-start | bytes 98308
  16.6 9.7 %copy-start.3 = (f32[8,1024]{1,0:T(8,128)S(1)}, f32[8,1024]{1,0:T(8,128)}, u32[]{:S(2)}) copy-start(f32[8,1024]{1,0:T(8,128)} %residues_ref.1) | copy-start | bytes 98308
  16.9 9.4 %copy-start.4 = (f32[1024]{0:T(1024)S(1)}, f32[1024]{0:T(1024)}, u32[]{:S(2)}) copy-start(f32[1024]{0:T(1024)} %param.17) | copy-start | bytes 12292
  16.9 10.2 %collective-permute-start.3 = (bf16[160,256]{1,0:T(8,128)(2,1)S(1)}, bf16[160,256]{1,0:T(8,128)(2,1)S(1)}, u32[]{:S(2)}, u32[]{:S(2)}) collective-permute-start(bf16[160,256]{1,0:T(8,128)(2,1)S(1)} %get-tuple-element.30), channel_id=1, source_target_pairs={{0,4},{4,8},{8,12},{12,16},{16,20},{20,24},{24,28},{28,32},{32,36}... | collective-permute-start | bytes 245768 | tf_op jit(solution)/shard_map/ppermute | solution.py:27
  22.8 4.3 %collective-permute-start.4 = (bf16[16,256]{1,0:T(8,128)(2,1)S(1)}, bf16[16,256]{1,0:T(8,128)(2,1)S(1)}, u32[]{:S(2)}, u32[]{:S(2)}) collective-permute-start(bf16[16,256]{1,0:T(8,128)(2,1)S(1)} %get-tuple-element.31), channel_id=1, source_target_pairs={{0,8},{4,12},{8,16},{12,20},{16,24},{20,28},{24,32},{28,36},{32,40... | collective-permute-start | bytes 24584 | tf_op jit(solution)/shard_map/ppermute | solution.py:27
  28.9 17.2 %all-to-all-start.1 = ((bf16[16,16,128]{2,1,0:T(8,128)(2,1)}), bf16[16,16,128]{2,1,0:T(8,128)(2,1)S(1)}, u32[]{:S(2)}, u32[]{:S(2)}) async-start(bf16[16,16,128]{2,1,0:T(8,128)(2,1)} %get-tuple-element.43), calls=%async_computation.1 | async-start | bytes 131072 | tf_op jit(solution)/shard_map/all_to_all | solution.py:380
  38.2 4.3 %collective-permute-start.5 = (f32[8,256]{1,0:T(8,128)S(1)}, f32[8,256]{1,0:T(8,128)S(1)}, u32[]{:S(2)}, u32[]{:S(2)}) collective-permute-start(f32[8,256]{1,0:T(8,128)S(1)} %get-tuple-element.44), channel_id=1, source_target_pairs={{0,4},{4,8},{8,12},{12,16},{16,20},{20,24},{24,28},{28,32},{32,36}... | collective-permute-start | bytes 24584 | tf_op jit(solution)/shard_map/ppermute | solution.py:27

commit v8 on v6

--- a/solution.py
+++ b/solution.py
@@ -139,7 +139,7 @@
             partial_ref[shift, start : start + 8, here] = total
         return carry
 
-    lax.fori_loop(0, 16, step, 0, unroll=2)
+    lax.fori_loop(0, 16, step, 0, unroll=4)
 
 
 def own_kernel(

time: 47.4 us -> 47.5 us (level)
  no operation moved by 1% of the time
where the time goes in v8:
time: 47.5 us; the launch traced here: 47.1 us
  starting transfers between devices  33.5 us (71%)
  waiting for transfers between devices  7.68 us (16%)
  Pallas kernels  5.74 us (12%)
    ppermute x6, starting transfers between devices, shifted(): return lax.ppermute(value, axis, pairs)  19.5 us
    all_to_all x1, starting transfers between devices, shards(): ends = lax.all_to_all(ends, 'ctx', 0, 0, tiled=True)  9.4 us
    pallas_call x7, Pallas kernels, call(): pl.pallas_call(kernel, out_shape=outs, in_specs=[pl.BlockSpec(memory_spac...  5.74 us
    all_to_all x1, starting transfers between devices, shards(): squares = lax.all_to_all(squares, ('sec', 'ch'), 0, 0, tiled=True)  4.62 us
    all_to_all x1, waiting for transfers between devices, shards(): squares = lax.all_to_all(squares, ('sec', 'ch'), 0, 0, tiled=True)  3.53 us
    all_to_all x1, waiting for transfers between devices, shards(): ends = lax.all_to_all(ends, 'ctx', 0, 0, tiled=True)  3.5 us
  transfers between devices with their start and end apart: 8, of which 3 were waited for; matrix products, arithmetic and copies ran while one was open for 0% of the time, Pallas kernels for 2%

profile of v8, /device:TPU:1, one launch (start us, length us, event | category | flops | bytes accessed | tf_op | source)
XLA Modules:
  0.0 47.1 jit_solution(13828732927503745177)
XLA Ops:
  0.0 0.0 copy-start.6
  0.0 1.6 %pack.1 = (f32[16,128]{1,0:T(8,128)}, bf16[2,128,256]{2,1,0:T(8,128)(2,1)S(1)}, bf16[2,128,256]{2,1,0:T(8,128)(2,1)S(1)}, bf16[2,128,256]{2,1,0:T(8,128)(2,1)S(1)}, bf16[2,128,256]{2,1,0:T(8,128)(2,1)S(1)}) custom-call(bf16[128,256]{1,0:T(8,128)(2,1)} %x_ref.1, bf16[1,128,1024]{2,1,0:T(8,128)(2,1)} %q_hbm.1, bf16[1,128,1024]{2,1,0:T(8,128)(2,1)} %k_hbm.1), custom_call_target="tpu_custom_call" | custom-call | flops 1000000 | bytes 1000000 | tf_op jit(solution)/shard_map/pack/pallas_call | solution.py:290
  1.6 3.8 %collective-permute-start = (bf16[2,128,256]{2,1,0:T(8,128)(2,1)S(1)}, bf16[2,128,256]{2,1,0:T(8,128)(2,1)S(1)}, u32[]{:S(2)}, u32[]{:S(2)}) collective-permute-start(bf16[2,128,256]{2,1,0:T(8,128)(2,1)S(1)} %get-tuple-element.26), channel_id=1, source_target_pairs={{0,128},{64,192},{128,0},{192,64},{1,129},{65,193},{129,1},{193,65... | collective-permute-start | bytes 393224 | tf_op jit(solution)/shard_map/ppermute | solution.py:27
  5.5 4.6 %all-to-all-start = ((f32[16,1,128]{2,1,0:T(1,128)}), f32[16,1,128]{2,1,0:T(1,128)S(1)}, u32[]{:S(2)}, u32[]{:S(2)}) async-start(f32[16,1,128]{2,1,0:T(1,128)} %bitcast.1), calls=%async_computation | async-start | bytes 16384 | tf_op jit(solution)/shard_map/all_to_all | solution.py:327
  10.1 0.0 copy-start.2
  10.1 1.4 %collective-permute-start.1 = (bf16[2,128,256]{2,1,0:T(8,128)(2,1)S(1)}, bf16[2,128,256]{2,1,0:T(8,128)(2,1)S(1)}, u32[]{:S(2)}, u32[]{:S(2)}) collective-permute-start(bf16[2,128,256]{2,1,0:T(8,128)(2,1)S(1)} %get-tuple-element.28), channel_id=1, source_target_pairs={{0,64},{64,128},{128,192},{192,0},{1,65},{65,129},{129,193},{193,1... | collective-permute-start | bytes 393224 | tf_op jit(solution)/shard_map/ppermute | solution.py:27
  11.6 1.3 %collective-permute-start.2 = (bf16[2,128,256]{2,1,0:T(8,128)(2,1)S(1)}, bf16[2,128,256]{2,1,0:T(8,128)(2,1)S(1)}, u32[]{:S(2)}, u32[]{:S(2)}) collective-permute-start(bf16[2,128,256]{2,1,0:T(8,128)(2,1)S(1)} %get-tuple-element.29), channel_id=1, source_target_pairs={{0,192},{64,0},{128,64},{192,128},{1,193},{65,1},{129,65},{193,129... | collective-permute-start | bytes 393224 | tf_op jit(solution)/shard_map/ppermute | solution.py:27
  12.9 0.0 copy-done.6
  12.9 0.0 copy-start.5
  12.9 3.5 %all-to-all-done = f32[16,1,128]{2,1,0:T(1,128)S(1)} async-done(((f32[16,1,128]{2,1,0:T(1,128)}), f32[16,1,128]{2,1,0:T(1,128)S(1)}, u32[]{:S(2)}, u32[]{:S(2)}) %all-to-all-start) | async-done | bytes 8224 | tf_op jit(solution)/shard_map/all_to_all | solution.py:327
  16.4 0.0 collective-permute-done.across_ref.f1
  16.4 0.0 copy-done.2
  16.4 0.0 copy-done.5
  16.4 0.1 entry.1.entry_ref
  16.6 0.0 copy-start
  16.6 0.0 copy-start.1
  16.6 0.0 copy-start.3
  16.6 0.0 collective-permute-done.1.f2
  16.6 0.0 collective-permute-done.2.f3
  16.6 0.3 first.1
  16.9 0.0 copy-start.4
  16.9 5.8 %collective-permute-start.3 = (bf16[160,256]{1,0:T(8,128)(2,1)S(1)}, bf16[160,256]{1,0:T(8,128)(2,1)S(1)}, u32[]{:S(2)}, u32[]{:S(2)}) collective-permute-start(bf16[160,256]{1,0:T(8,128)(2,1)S(1)} %get-tuple-element.30), channel_id=1, source_target_pairs={{0,4},{4,8},{8,12},{12,16},{16,20},{20,24},{24,28},{28,32},{32,36}... | collective-permute-start | bytes 245768 | tf_op jit(solution)/shard_map/ppermute | solution.py:27
  22.8 3.5 %collective-permute-start.4 = (bf16[16,256]{1,0:T(8,128)(2,1)S(1)}, bf16[16,256]{1,0:T(8,128)(2,1)S(1)}, u32[]{:S(2)}, u32[]{:S(2)}) collective-permute-start(bf16[16,256]{1,0:T(8,128)(2,1)S(1)} %get-tuple-element.31), channel_id=1, source_target_pairs={{0,8},{4,12},{8,16},{12,20},{16,24},{20,28},{24,32},{28,36},{32,40... | collective-permute-start | bytes 24584 | tf_op jit(solution)/shard_map/ppermute | solution.py:27
  26.3 0.0 copy-done
  26.3 0.0 copy-done.1
  26.3 0.0 copy-done.3
  26.3 0.0 copy-done.4
  26.3 0.7 %own.1 = (f32[8,120,256]{2,1,0:T(8,128)S(1)}, f32[8,16,256]{2,1,0:T(8,128)S(1)}, f32[9,8,256]{2,1,0:T(8,128)S(1)}, f32[8,8,256]{2,1,0:T(8,128)S(1)}, f32[8,8,256]{2,1,0:T(8,128)S(1)}) custom-call(f32[128,256]{1,0:T(8,128)S(1)} %get-tuple-element.34.gated_ref, f32[128,1024]{1,0:T(8,128)S(1)} %copy-done, f32[8,1024]{1,0:T(8,128)S(1)} %copy-done.1, ...), custom_call_target="tpu_custom_call" | custom-call | flops 1000000 | bytes 1000000 | tf_op jit(solution)/shard_map/own/pallas_call | solution.py:290
  27.1 0.0 collective-permute-done.4.far_ref
  27.1 0.0 collective-permute-done.3.near_ref
  27.1 1.8 %second.1 = (bf16[128,256]{1,0:T(8,128)(2,1)S(1)}, f32[128,256]{1,0:T(8,128)S(1)}, f32[16,8,256]{2,1,0:T(8,128)S(1)}, bf16[16,16,128]{2,1,0:T(8,128)(2,1)}, f32[8,256]{1,0:T(8,128)S(1)}) custom-call(bf16[160,256]{1,0:T(8,128)(2,1)S(1)} %collective-permute-done.3.near_ref, bf16[16,256]{1,0:T(8,128)(2,1)S(1)} %collective-permute-done.4.far_ref, ...), custom_call_target="tpu_custom_call" | custom-call | flops 1000000 | bytes 1000000 | tf_op jit(solution)/shard_map/second/pallas_call | solution.py:290
  28.9 9.4 %all-to-all-start.1 = ((bf16[16,16,128]{2,1,0:T(8,128)(2,1)}), bf16[16,16,128]{2,1,0:T(8,128)(2,1)S(1)}, u32[]{:S(2)}, u32[]{:S(2)}) async-start(bf16[16,16,128]{2,1,0:T(8,128)(2,1)} %get-tuple-element.43), calls=%async_computation.1 | async-start | bytes 131072 | tf_op jit(solution)/shard_map/all_to_all | solution.py:378
  38.3 3.5 %collective-permute-start.5 = (f32[8,256]{1,0:T(8,128)S(1)}, f32[8,256]{1,0:T(8,128)S(1)}, u32[]{:S(2)}, u32[]{:S(2)}) collective-permute-start(f32[8,256]{1,0:T(8,128)S(1)} %get-tuple-element.44), channel_id=1, source_target_pairs={{0,4},{4,8},{8,12},{12,16},{16,20},{20,24},{24,28},{28,32},{32,36}... | collective-permute-start | bytes 24584 | tf_op jit(solution)/shard_map/ppermute | solution.py:27
  41.8 0.1 within.1.local_ref
  42.0 0.6 %collective-permute-done.5.tail_ref = f32[8,256]{1,0:T(8,128)S(1)} collective-permute-done((f32[8,256]{1,0:T(8,128)S(1)}, f32[8,256]{1,0:T(8,128)S(1)}, u32[]{:S(2)}, u32[]{:S(2)}) %collective-permute-start.5) | collective-permute-done | bytes 8224 | tf_op jit(solution)/shard_map/ppermute | solution.py:27
  42.6 3.5 %all-to-all-done.1.ends_ref = bf16[16,16,128]{2,1,0:T(8,128)(2,1)S(1)} async-done(((bf16[16,16,128]{2,1,0:T(8,128)(2,1)}), bf16[16,16,128]{2,1,0:T(8,128)(2,1)S(1)}, u32[]{:S(2)}, u32[]{:S(2)}) %all-to-all-start.1) | async-done | bytes 65568 | tf_op jit(solution)/shard_map/all_to_all | solution.py:378
  46.1 1.1 %third.1 = bf16[128,256]{1,0:T(8,128)(2,1)} custom-call(f32[128,256]{1,0:T(8,128)S(1)} %within.1.local_ref, f32[16,8,256]{2,1,0:T(8,128)S(1)} %get-tuple-element.41.steps_ref, bf16[128,256]{1,0:T(8,128)(2,1)S(1)} %get-tuple-element.42.stream_ref, bf16[16,16,128]{2,1,0:T(8,128)(2,1)S(1)} %all-to-all-done.1.ends_ref, ...), custom_call_target="tpu_custom_call" | custom-call | flops 1000000 | bytes 1000000 | tf_op jit(solution)/shard_map/third/pallas_call | solution.py:290
  (1 shorter events, 0.0 us)
Async XLA Ops:
  0.0 12.9 %copy-start.6 = (f32[2,7,1024]{2,0,1:T(2,128)S(1)}, f32[2,7,1024]{2,0,1:T(2,128)}, u32[]{:S(2)}) copy-start(f32[2,7,1024]{2,0,1:T(2,128)} %param.13) | copy-start | bytes 172036
  1.6 14.8 %collective-permute-start = (bf16[2,128,256]{2,1,0:T(8,128)(2,1)S(1)}, bf16[2,128,256]{2,1,0:T(8,128)(2,1)S(1)}, u32[]{:S(2)}, u32[]{:S(2)}) collective-permute-start(bf16[2,128,256]{2,1,0:T(8,128)(2,1)S(1)} %get-tuple-element.26), channel_id=1, source_target_pairs={{0,128},{64,192},{128,0},{192,64},{1,129},{65,193},{129,1},{193,65... | collective-permute-start | bytes 393224 | tf_op jit(solution)/shard_map/ppermute | solution.py:27
  5.5 11.0 %all-to-all-start = ((f32[16,1,128]{2,1,0:T(1,128)}), f32[16,1,128]{2,1,0:T(1,128)S(1)}, u32[]{:S(2)}, u32[]{:S(2)}) async-start(f32[16,1,128]{2,1,0:T(1,128)} %bitcast.1), calls=%async_computation | async-start | bytes 16384 | tf_op jit(solution)/shard_map/all_to_all | solution.py:327
  10.1 6.3 %copy-start.2 = (bf16[128,256]{1,0:T(8,128)(2,1)S(1)}, bf16[128,256]{1,0:T(8,128)(2,1)}, u32[]{:S(2)}) copy-start(bf16[128,256]{1,0:T(8,128)(2,1)} %x_ref.1) | copy-start | bytes 196612
  10.1 6.5 %collective-permute-start.1 = (bf16[2,128,256]{2,1,0:T(8,128)(2,1)S(1)}, bf16[2,128,256]{2,1,0:T(8,128)(2,1)S(1)}, u32[]{:S(2)}, u32[]{:S(2)}) collective-permute-start(bf16[2,128,256]{2,1,0:T(8,128)(2,1)S(1)} %get-tuple-element.28), channel_id=1, source_target_pairs={{0,64},{64,128},{128,192},{192,0},{1,65},{65,129},{129,193},{193,1... | collective-permute-start | bytes 393224 | tf_op jit(solution)/shard_map/ppermute | solution.py:27
  11.6 5.1 %collective-permute-start.2 = (bf16[2,128,256]{2,1,0:T(8,128)(2,1)S(1)}, bf16[2,128,256]{2,1,0:T(8,128)(2,1)S(1)}, u32[]{:S(2)}, u32[]{:S(2)}) collective-permute-start(bf16[2,128,256]{2,1,0:T(8,128)(2,1)S(1)} %get-tuple-element.29), channel_id=1, source_target_pairs={{0,192},{64,0},{128,64},{192,128},{1,193},{65,1},{129,65},{193,129... | collective-permute-start | bytes 393224 | tf_op jit(solution)/shard_map/ppermute | solution.py:27
  12.9 3.5 %copy-start.5 = (f32[1024]{0:T(1024)S(1)}, f32[1024]{0:T(1024)}, u32[]{:S(2)}) copy-start(f32[1024]{0:T(1024)} %param.12) | copy-start | bytes 12292
  16.6 9.7 %copy-start = (f32[128,1024]{1,0:T(8,128)S(1)}, f32[128,1024]{1,0:T(8,128)}, u32[]{:S(2)}) copy-start(f32[128,1024]{1,0:T(8,128)} %medium_ref.1) | copy-start | bytes 1572868
  16.6 9.7 %copy-start.1 = (f32[8,1024]{1,0:T(8,128)S(1)}, f32[8,1024]{1,0:T(8,128)}, u32[]{:S(2)}) copy-start(f32[8,1024]{1,0:T(8,128)} %rates_ref.3) | copy-start | bytes 98308
  16.6 9.7 %copy-start.3 = (f32[8,1024]{1,0:T(8,128)S(1)}, f32[8,1024]{1,0:T(8,128)}, u32[]{:S(2)}) copy-start(f32[8,1024]{1,0:T(8,128)} %residues_ref.1) | copy-start | bytes 98308
  16.9 9.4 %copy-start.4 = (f32[1024]{0:T(1024)S(1)}, f32[1024]{0:T(1024)}, u32[]{:S(2)}) copy-start(f32[1024]{0:T(1024)} %param.17) | copy-start | bytes 12292
  16.9 10.1 %collective-permute-start.3 = (bf16[160,256]{1,0:T(8,128)(2,1)S(1)}, bf16[160,256]{1,0:T(8,128)(2,1)S(1)}, u32[]{:S(2)}, u32[]{:S(2)}) collective-permute-start(bf16[160,256]{1,0:T(8,128)(2,1)S(1)} %get-tuple-element.30), channel_id=1, source_target_pairs={{0,4},{4,8},{8,12},{12,16},{16,20},{20,24},{24,28},{28,32},{32,36}... | collective-permute-start | bytes 245768 | tf_op jit(solution)/shard_map/ppermute | solution.py:27
  22.8 4.3 %collective-permute-start.4 = (bf16[16,256]{1,0:T(8,128)(2,1)S(1)}, bf16[16,256]{1,0:T(8,128)(2,1)S(1)}, u32[]{:S(2)}, u32[]{:S(2)}) collective-permute-start(bf16[16,256]{1,0:T(8,128)(2,1)S(1)} %get-tuple-element.31), channel_id=1, source_target_pairs={{0,8},{4,12},{8,16},{12,20},{16,24},{20,28},{24,32},{28,36},{32,40... | collective-permute-start | bytes 24584 | tf_op jit(solution)/shard_map/ppermute | solution.py:27
  28.9 17.2 %all-to-all-start.1 = ((bf16[16,16,128]{2,1,0:T(8,128)(2,1)}), bf16[16,16,128]{2,1,0:T(8,128)(2,1)S(1)}, u32[]{:S(2)}, u32[]{:S(2)}) async-start(bf16[16,16,128]{2,1,0:T(8,128)(2,1)} %get-tuple-element.43), calls=%async_computation.1 | async-start | bytes 131072 | tf_op jit(solution)/shard_map/all_to_all | solution.py:378
  38.3 4.3 %collective-permute-start.5 = (f32[8,256]{1,0:T(8,128)S(1)}, f32[8,256]{1,0:T(8,128)S(1)}, u32[]{:S(2)}, u32[]{:S(2)}) collective-permute-start(f32[8,256]{1,0:T(8,128)S(1)} %get-tuple-element.44), channel_id=1, source_target_pairs={{0,4},{4,8},{8,12},{12,16},{16,20},{20,24},{24,28},{28,32},{32,36}... | collective-permute-start | bytes 24584 | tf_op jit(solution)/shard_map/ppermute | solution.py:27
